TPU v7x, 32 devices: a whole 2x2x4 slice. The times are simulated.
32 devices in a mesh: dom: 16 (over z, y, x), tp: 2 (over core).
Axes of the slice: x: 2, y: 2, z: 4, core: 2. Of those that a mesh axis runs over, the one named last changes fastest.
Arguments:
- queries: bfloat16 [2, 256, 8192], P(None, 'dom', 'tp'), may hold values from -400 to 400
- new_kv: bfloat16 [2, 256, 2048], P(None, 'dom', 'tp'), may hold values from -5 to 5
- gen_cache: bfloat16 [256, 128, 2048], P('dom', None, 'tp'), may hold values from -5 to 5
- prompt_kv: bfloat16 [4096, 2048], P(None, 'tp'), may hold values from -5 to 5
- lengths: int32 [256], replicated, may hold values from 1 to 126
- ancestors: int32 [256], replicated, may hold values from 0 to 255, as said below
- tokens: int32 [2, 256], P(None, 'dom'), may hold values from 0 to 128255
- twist_vector: float32 [8192], P('tp'), may hold values from -31 to 31
- twist_bias: float32 [128256], replicated, may hold values from -5 to 5
- prior_weights: float32 [256], P('dom'), may hold values from -252 to 4
Outputs:
- twist: float32 [2, 256], P(None, 'dom')
- normalized: float32 [256], P('dom')
- resampled_cache: bfloat16 [256, 128, 2048], P('dom', None, 'tp')
- new_lengths: int32 [256], P('dom')
Inputs may be any that keep to these rules, and one draw needn't show every extreme that they name: Particle p's ancestor lies on the index of dom that holds p or at most 2 indices from it; the particles of one index of dom name at most 2 distinct ancestors on any other index, and exactly 2 for some pair of indices.
All inputs are finite; a program needn't handle non-finite values.
Results may differ from a plain program's by a relative error of at most 0.0018.
Values may be sent and summed in bfloat16 or wider, within the bound.
No kernel may reach another device: no remote copies, remote signals or barrier semaphores. Data moves between devices by JAX's collectives and lax.ppermute only.
A program may use at most 128 MiB of HBM per device.

v0:
```python
import functools
import math

import jax
import jax.numpy as jnp
from jax import lax
from jax.experimental import pallas as pl
from jax.experimental.pallas import tpu as pltpu
from jax.sharding import PartitionSpec as P

HEAD_DIM = 128
SPAN = 2
PICKS = 2
NEG_FILL = -1e30
KEY_CHUNK = 512
VMEM_BYTES = 44 * 1024 * 1024
ROW_TILE = 16
WINDOW = 2 * ROW_TILE

ORDERS = ((-2, 2, 1, -1), (1, -1, -2, 2))


def in_hbm(x):
    return pltpu.with_memory_space_constraint(x, pltpu.HBM)


def place_new_rows(cache, new_rows, length, slot, per_dev):
    rows, width = cache.shape
    first = pl.multiple_of(
        jnp.minimum(length // ROW_TILE * ROW_TILE, rows - WINDOW), ROW_TILE
    )
    row_ids = first + lax.broadcasted_iota(jnp.int32, (WINDOW, width), 0)
    old = cache[pl.ds(first, WINDOW), :].astype(jnp.float32)
    later = jnp.where(row_ids == length + 1, new_rows[pl.ds(per_dev + slot, 1), :], 0.0)
    later = jnp.where(row_ids == length, new_rows[pl.ds(slot, 1), :], later)
    cache[pl.ds(first, WINDOW), :] = jnp.where(row_ids < length, old, later).astype(
        jnp.bfloat16
    )

    def clear(tile, carry):
        start = pl.multiple_of(tile * ROW_TILE, ROW_TILE)
        cache[pl.ds(start, ROW_TILE), :] = jnp.zeros((ROW_TILE, width), jnp.bfloat16)
        return carry

    lax.fori_loop(first // ROW_TILE + WINDOW // ROW_TILE, rows // ROW_TILE, clear, 0)


def named_range(anc_ref, first, owner, per_dev):
    low, high = jnp.int32(per_dev), jnp.int32(-1)
    for j in range(per_dev):
        local = anc_ref[first + j] - owner * per_dev
        named = jnp.logical_and(local >= 0, local < per_dev)
        low = jnp.minimum(low, jnp.where(named, local, per_dev))
        high = jnp.maximum(high, jnp.where(named, local, -1))
    return low, high


def pack_kernel(per_dev, doms, step_pairs, len_hbm, anc_hbm, new_hbm, gen_hbm, *refs):
    sends = refs[: len(step_pairs)]
    new_len_ref, own_len_ref, own_anc_ref, slot_ref = refs[len(step_pairs) : len(step_pairs) + 4]
    len_ref, anc_ref, new_bf16, new_rows, list_sem, load_sem = refs[len(step_pairs) + 4 :]
    lists = [
        pltpu.make_async_copy(anc_hbm, anc_ref, list_sem.at[0]),
        pltpu.make_async_copy(len_hbm, len_ref, list_sem.at[1]),
        pltpu.make_async_copy(new_hbm, new_bf16, list_sem.at[2]),
    ]
    for copy in lists:
        copy.start()
    me, odd = lax.axis_index("dom"), lax.axis_index("tp") % 2
    lists[0].wait()
    picks = []
    loads = []
    for k, (even_step, odd_step) in enumerate(step_pairs):
        reader = jnp.clip(me + jnp.where(odd == 1, odd_step, even_step), 0, doms - 1)
        low, high = named_range(anc_ref, reader * per_dev, me, per_dev)
        for i, pick in enumerate((jnp.minimum(low, per_dev - 1), jnp.maximum(high, 0))):
            target = sends[k].at[i]
            load = pltpu.make_async_copy(gen_hbm.at[pick], target, load_sem.at[len(loads)])
            load.start()
            picks.append((pick, target))
            loads.append(load)
    lists[1].wait()
    for j in range(per_dev):
        own_anc_ref[j] = anc_ref[me * per_dev + j]
        new_len_ref[j] = len_ref[anc_ref[me * per_dev + j]] + 2
        own_len_ref[j] = len_ref[me * per_dev + j]
        slot_ref[j] = -1
    for k, (even_step, odd_step) in enumerate(step_pairs):
        source = me - jnp.where(odd == 1, odd_step, even_step)
        low, _ = named_range(anc_ref, me * per_dev, source, per_dev)
        for j in range(per_dev):
            local = anc_ref[me * per_dev + j] - source * per_dev
            named = jnp.logical_and(local >= 0, local < per_dev)
            slot = k * PICKS + jnp.where(local == low, 0, PICKS - 1)
            slot_ref[j] = jnp.where(named, slot, slot_ref[j])
    lists[2].wait()
    new_rows[...] = new_bf16[...].astype(jnp.float32).reshape(new_rows.shape)
    for load, (pick, target) in zip(loads, picks):
        load.wait()
        place_new_rows(target, new_rows, len_ref[me * per_dev + pick], pick, per_dev)


def pack(lengths, ancestors, new_kv, gen_cache, doms, step_pairs):
    per_dev, rows, width = gen_cache.shape
    count = len(step_pairs)
    smem = pl.BlockSpec(memory_space=pltpu.SMEM)
    vmem = pl.BlockSpec(memory_space=pltpu.VMEM)
    hbm = pl.BlockSpec(memory_space=pltpu.HBM)
    block_bytes = PICKS * rows * width * 2
    return pl.pallas_call(
        functools.partial(pack_kernel, per_dev, doms, step_pairs),
        out_shape=[jax.ShapeDtypeStruct((PICKS, rows, width), jnp.bfloat16)] * count
        + [jax.ShapeDtypeStruct((per_dev,), jnp.int32)] * 4,
        in_specs=[hbm] * 4,
        out_specs=[vmem] * count + [smem] * 4,
        scratch_shapes=[
            pltpu.SMEM(lengths.shape, jnp.int32),
            pltpu.SMEM(ancestors.shape, jnp.int32),
            pltpu.VMEM(new_kv.shape, jnp.bfloat16),
            pltpu.VMEM((2 * per_dev, width), jnp.float32),
            pltpu.SemaphoreType.DMA((3,)),
            pltpu.SemaphoreType.DMA((count * PICKS,)),
        ],
        compiler_params=pltpu.CompilerParams(vmem_limit_bytes=VMEM_BYTES),
        cost_estimate=pl.CostEstimate(
            flops=0, bytes_accessed=2 * count * block_bytes, transcendentals=0
        ),
        name="pack_sends",
    )(*(in_hbm(x) for x in (lengths, ancestors, new_kv, gen_cache)))


def fold_rows(block, combine):
    return combine(block.reshape(block.shape[0] // 8, 8, block.shape[1]), axis=0)


def attend_kernel(
    per_dev,
    group,
    kv_local,
    chunk,
    len_ref,
    anc_ref,
    q_ref,
    prompt_hbm,
    gen_hbm,
    new_ref,
    head_ref,
    extra_ref,
    share_ref,
    out_hbm,
    prompt,
    grown,
    scores,
    mixed_ref,
    prompt_sem,
    gen_sem,
    out_sem,
):
    me = lax.axis_index("dom")
    steps = q_ref.shape[0]
    rows, width = grown.shape[1:]
    chunks = prompt.shape[0] // chunk
    pair = 2 * HEAD_DIM
    scale = 1.0 / math.sqrt(HEAD_DIM)
    base = steps * per_dev
    lanes = group * base

    loads = [
        pltpu.make_async_copy(gen_hbm.at[p], grown.at[p], gen_sem.at[p]) for p in range(per_dev)
    ]
    for load in loads:
        load.start()

    def prompt_load(j):
        part = pl.ds(pl.multiple_of(j * chunk, chunk), chunk)
        return pltpu.make_async_copy(prompt_hbm.at[part], prompt.at[part], prompt_sem.at[j])

    for j in range(chunks):
        prompt_load(j).start()

    new_rows = new_ref[...].astype(jnp.float32).reshape(base, width)
    row_ids = lax.broadcasted_iota(jnp.int32, (rows, width), 0)
    for p in range(per_dev):
        loads[p].wait()
        behind = row_ids - len_ref[p]
        tail = jnp.where(behind == 1, new_rows[per_dev + p : per_dev + p + 1], 0.0)
        tail = jnp.where(behind == 0, new_rows[p : p + 1], tail)
        grown[p] = jnp.where(behind < 0, grown[p].astype(jnp.float32), tail).astype(
            jnp.bfloat16
        )
    homes = []
    for p in range(per_dev):
        local = anc_ref[p] - me * per_dev
        home = jnp.logical_and(local >= 0, local < per_dev)
        source = grown.at[jnp.clip(local, 0, per_dev - 1)]
        copy = pltpu.make_async_copy(source, out_hbm.at[p], out_sem.at[p])
        homes.append((home, copy))
        pl.when(home)(copy.start)

    q2 = q_ref[...].reshape(base, q_ref.shape[-1])
    queries = [
        jnp.concatenate(
            [q2[:, h * HEAD_DIM : (h + 1) * HEAD_DIM] for h in range(c * group, (c + 1) * group)],
            axis=0,
        )
        for c in range(kv_local)
    ]

    def score(keys, c):
        return lax.dot_general(
            keys, queries[c], (((1,), (1,)), ((), ())), preferred_element_type=jnp.float32
        )

    def mix(values, probs):
        return lax.dot_general(
            values, probs, (((0,), (0,)), ((), ())), preferred_element_type=jnp.float32
        )

    lane_ids = lax.broadcasted_iota(jnp.int32, (rows, lanes), 1)
    owner = lane_ids % per_dev
    last = lane_ids // per_dev % steps
    for p in range(per_dev):
        last = last + jnp.where(owner == p, len_ref[p], 0)
    visible = lax.broadcasted_iota(jnp.int32, (rows, lanes), 0) <= last

    own_scores = []
    tops = []
    for c in range(kv_local):
        keys = grown[:, :, c * pair : c * pair + HEAD_DIM].reshape(per_dev * rows, HEAD_DIM)
        every = score(keys, c)
        own = every[:rows]
        for p in range(1, per_dev):
            own = jnp.where(owner == p, every[p * rows : (p + 1) * rows], own)
        own = jnp.where(visible, own * scale, NEG_FILL)
        own_scores.append(own)
        tops.append(fold_rows(own, jnp.max))

    def score_chunk(j, tops):
        prompt_load(j).wait()
        part = pl.ds(pl.multiple_of(j * chunk, chunk), chunk)
        raised = []
        for c in range(kv_local):
            block = score(prompt[part, c * pair : c * pair + HEAD_DIM], c) * scale
            scores[c, part] = block
            raised.append(jnp.maximum(tops[c], fold_rows(block, jnp.max)))
        return tuple(raised)

    tops = lax.fori_loop(0, chunks, score_chunk, tuple(tops))
    maxima = [jnp.max(top, axis=0, keepdims=True) for top in tops]

    totals = []
    for c in range(kv_local):
        exps = jnp.where(visible, jnp.exp(own_scores[c] - maxima[c]), 0.0)
        totals.append(fold_rows(exps, jnp.sum))
        probs = jnp.concatenate(
            [jnp.where(owner == p, exps, 0.0).astype(jnp.bfloat16) for p in range(per_dev)],
            axis=0,
        )
        values = grown[:, :, c * pair + HEAD_DIM : (c + 1) * pair]
        mixed_ref[c] = mix(values.reshape(per_dev * rows, HEAD_DIM), probs)

    def mix_chunk(j, totals):
        part = pl.ds(pl.multiple_of(j * chunk, chunk), chunk)
        grew = []
        for c in range(kv_local):
            exps = jnp.exp(scores[c, part] - maxima[c])
            grew.append(totals[c] + fold_rows(exps, jnp.sum))
            mixed_ref[c] += mix(
                prompt[part, c * pair + HEAD_DIM : (c + 1) * pair], exps.astype(jnp.bfloat16)
            )
        return tuple(grew)

    totals = lax.fori_loop(0, chunks, mix_chunk, tuple(totals))
    weighted = jnp.zeros((base, HEAD_DIM), jnp.float32)
    for c in range(kv_local):
        mixed = (mixed_ref[c] / jnp.sum(totals[c], axis=0, keepdims=True)).T
        for h in range(group):
            weighted = (
                weighted + mixed[h * base : (h + 1) * base] * head_ref[c * group + h][None, :]
            )
    padding = jnp.zeros((HEAD_DIM - base, HEAD_DIM), jnp.float32)
    square = jnp.concatenate([weighted, padding], axis=0)
    row = jnp.sum(square.T, axis=0, keepdims=True) + extra_ref[...]
    share_ref[...] = jnp.broadcast_to(row[None], share_ref.shape)
    for home, copy in homes:
        pl.when(home)(copy.wait)


def attend(
    own_lengths, own_ancestors, queries, prompt_kv, gen_cache, new_kv, twist_vector, extra, devices
):
    steps, per_dev, width = queries.shape
    keys, kv_width = prompt_kv.shape
    rows = gen_cache.shape[1]
    kv_local = kv_width // (2 * HEAD_DIM)
    group = width // (kv_local * HEAD_DIM)
    lanes = steps * per_dev * group
    chunk = min(KEY_CHUNK, keys)
    head_weights = twist_vector.reshape(kv_local * group, HEAD_DIM)
    smem = pl.BlockSpec(memory_space=pltpu.SMEM)
    vmem = pl.BlockSpec(memory_space=pltpu.VMEM)
    hbm = pl.BlockSpec(memory_space=pltpu.HBM)
    score_count = lanes * kv_local * (keys + rows)
    return pl.pallas_call(
        functools.partial(attend_kernel, per_dev, group, kv_local, chunk),
        out_shape=[
            jax.ShapeDtypeStruct((devices, 1, HEAD_DIM), jnp.float32),
            jax.ShapeDtypeStruct(gen_cache.shape, jnp.bfloat16),
        ],
        in_specs=[smem, smem, vmem, hbm, hbm, vmem, vmem, vmem],
        out_specs=[vmem, hbm],
        scratch_shapes=[
            pltpu.VMEM(prompt_kv.shape, jnp.bfloat16),
            pltpu.VMEM(gen_cache.shape, jnp.bfloat16),
            pltpu.VMEM((kv_local, keys, lanes), jnp.float32),
            pltpu.VMEM((kv_local, HEAD_DIM, lanes), jnp.float32),
            pltpu.SemaphoreType.DMA((keys // chunk,)),
            pltpu.SemaphoreType.DMA((per_dev,)),
            pltpu.SemaphoreType.DMA((per_dev,)),
        ],
        compiler_params=pltpu.CompilerParams(vmem_limit_bytes=VMEM_BYTES),
        cost_estimate=pl.CostEstimate(
            flops=4 * score_count * HEAD_DIM,
            bytes_accessed=2 * (prompt_kv.size + 2 * gen_cache.size),
            transcendentals=score_count,
        ),
        name="attend",
    )(
        own_lengths,
        own_ancestors,
        queries,
        in_hbm(prompt_kv),
        in_hbm(gen_cache),
        new_kv,
        head_weights,
        extra,
    )


def finish_kernel(doms, tps, slot_ref, *refs):
    gots = refs[: len(ORDERS[0])]
    _, all_ref, out_ref, twist_ref, normal_ref, sums, sem = refs[len(gots) :]
    per_dev = out_ref.shape[0]
    for p in range(per_dev):
        slot = slot_ref[p]
        for k, got in enumerate(gots):
            for i in range(PICKS):
                copy = pltpu.make_async_copy(got.at[i], out_ref.at[p], sem.at[p])
                pl.when(slot == k * PICKS + i)(copy.start)
    for d in range(doms):
        row = all_ref[d * tps]
        for t in range(1, tps):
            row = row + all_ref[d * tps + t]
        sums[d : d + 1, :] = row
    step_0, step_1, prior = (
        slice(k * per_dev, (k + 1) * per_dev) for k in range(3)
    )
    totals = sums[...]
    log_weights = totals[:, prior] + totals[:, step_1] - totals[:, step_0]
    largest = jnp.max(log_weights, keepdims=True)
    log_total = largest + jnp.log(jnp.sum(jnp.exp(log_weights - largest), keepdims=True))
    mine = sums[pl.ds(lax.axis_index("dom"), 1), :]
    own = mine[:, prior] + mine[:, step_1] - mine[:, step_0]
    twist_ref[...] = jnp.concatenate([mine[:, step_0], mine[:, step_1]], axis=0)
    normal_ref[...] = own - log_total
    for p in range(per_dev):
        copy = pltpu.make_async_copy(gots[0].at[0], out_ref.at[p], sem.at[p])
        pl.when(slot_ref[p] >= 0)(copy.wait)


def finish(slots, gots, held, shares, doms, tps):
    per_dev = held.shape[0]
    count = len(gots)
    smem = pl.BlockSpec(memory_space=pltpu.SMEM)
    vmem = pl.BlockSpec(memory_space=pltpu.VMEM)
    hbm = pl.BlockSpec(memory_space=pl.ANY)
    return pl.pallas_call(
        functools.partial(finish_kernel, doms, tps),
        out_shape=[
            jax.ShapeDtypeStruct(held.shape, held.dtype),
            jax.ShapeDtypeStruct((2, per_dev), jnp.float32),
            jax.ShapeDtypeStruct((1, per_dev), jnp.float32),
        ],
        in_specs=[smem] + [vmem] * count + [hbm, vmem],
        out_specs=[hbm, vmem, vmem],
        input_output_aliases={1 + count: 0},
        scratch_shapes=[
            pltpu.VMEM((doms, HEAD_DIM), jnp.float32),
            pltpu.SemaphoreType.DMA((per_dev,)),
        ],
        compiler_params=pltpu.CompilerParams(vmem_limit_bytes=VMEM_BYTES),
        cost_estimate=pl.CostEstimate(
            flops=0, bytes_accessed=held.size, transcendentals=0
        ),
        name="finish",
    )(slots, *gots, held, shares)


def routes(doms, tps, steps):
    pairs = []
    for d in range(doms):
        for t in range(tps):
            target = d + steps[t % 2]
            if 0 <= target < doms:
                pairs.append((d * tps + t, target * tps + t))
    return pairs


def local(
    queries,
    new_kv,
    gen_cache,
    prompt_kv,
    lengths,
    ancestors,
    tokens,
    twist_vector,
    twist_bias,
    prior_weights,
):
    doms, tps = lax.axis_size("dom"), lax.axis_size("tp")
    per_dev = gen_cache.shape[0]
    step_pairs = list(zip(*ORDERS))
    everyone = ("dom", "tp")

    *sends, new_lengths, own_lengths, own_ancestors, slots = pack(
        lengths, ancestors, new_kv, gen_cache, doms, step_pairs
    )
    arrivals = [
        lax.ppermute(send, everyone, routes(doms, tps, steps))
        for send, steps in zip(sends, step_pairs)
    ]

    bias = jnp.take(twist_bias, tokens, axis=0).reshape(-1)
    extra = jnp.concatenate([bias, prior_weights])
    extra = jnp.where(lax.axis_index("tp") == 0, extra, 0.0)
    extra = jnp.pad(extra, (0, HEAD_DIM - extra.size))[None]
    shares, resampled = attend(
        own_lengths,
        own_ancestors,
        queries,
        prompt_kv,
        gen_cache,
        new_kv,
        twist_vector,
        extra,
        doms * tps,
    )
    shares = lax.all_to_all(shares, everyone, 0, 0, tiled=True)
    resampled, twist, normalized = finish(slots, arrivals, resampled, shares, doms, tps)
    return (twist, normalized.reshape(per_dev), resampled, new_lengths)


def solution(mesh):
    in_specs = (
        P(None, "dom", "tp"),
        P(None, "dom", "tp"),
        P("dom", None, "tp"),
        P(None, "tp"),
        P(),
        P(),
        P(None, "dom"),
        P("tp"),
        P(),
        P("dom"),
    )
    out_specs = (P(None, "dom"), P("dom"), P("dom", None, "tp"), P("dom"))
    return jax.shard_map(local, mesh=mesh, in_specs=in_specs, out_specs=out_specs, check_vma=False)
```

profile of v0, /device:TPU:0, one launch (start us, length us, event | category | flops | bytes accessed | tf_op | source)
XLA Modules:
  0.0 49.7 jit_solution(11579431920255640344)
XLA Ops:
  0.6 0.0 copy-start
  0.6 0.0 copy-start.1
  0.7 0.0 copy-start.4
  0.7 0.0 copy-start.5
  0.7 0.0 copy-start.3
  0.7 0.0 copy-start.2
  0.7 3.9 %pack_sends.1 = (bf16[2,128,1024]{2,1,0:T(8,128)(2,1)}, bf16[2,128,1024]{2,1,0:T(8,128)(2,1)}, bf16[2,128,1024]{2,1,0:T(8,128)(2,1)}, bf16[2,128,1024]{2,1,0:T(8...) custom-call(s32[256]{0:T(256)} %len_hbm.1, s32[256]{0:T(256)} %anc_hbm.1, ...), custom_call_target="tpu_custom_call" | custom-call | bytes 4194304 | tf_op jit(solution)/shard_map/pack_sends/pallas_call | solution.py:110
  4.6 1.3 %collective-permute-start = (bf16[2,128,1024]{2,1,0:T(8,128)(2,1)}, bf16[2,128,1024]{2,1,0:T(8,128)(2,1)S(1)}, u32[]{:S(2)}, u32[]{:S(2)}) collective-permute-start(bf16[2,128,1024]{2,1,0:T(8,128)(2,1)} %get-tuple-element.18), channel_id=1, source_target_pairs={{1,3},{3,5},{4,0},{5,7},{6,2},{7,9},{8,4},{9,11},{10,6},{11,13},{1... | collective-permute-start | bytes 1572872 | tf_op jit(solution)/shard_map/ppermute | solution.py:430
  5.9 5.7 %collective-permute-start.1 = (bf16[2,128,1024]{2,1,0:T(8,128)(2,1)}, bf16[2,128,1024]{2,1,0:T(8,128)(2,1)S(1)}, u32[]{:S(2)}, u32[]{:S(2)}) collective-permute-start(bf16[2,128,1024]{2,1,0:T(8,128)(2,1)} %get-tuple-element.19), channel_id=1, source_target_pairs={{0,4},{2,6},{3,1},{4,8},{5,3},{6,10},{7,5},{8,12},{9,7},{10,14},{1... | collective-permute-start | bytes 1572872 | tf_op jit(solution)/shard_map/ppermute | solution.py:430
  11.6 3.8 %collective-permute-start.2 = (bf16[2,128,1024]{2,1,0:T(8,128)(2,1)}, bf16[2,128,1024]{2,1,0:T(8,128)(2,1)S(1)}, u32[]{:S(2)}, u32[]{:S(2)}) collective-permute-start(bf16[2,128,1024]{2,1,0:T(8,128)(2,1)} %get-tuple-element.20), channel_id=1, source_target_pairs={{0,2},{2,4},{4,6},{5,1},{6,8},{7,3},{8,10},{9,5},{10,12},{11,7},{1... | collective-permute-start | bytes 1572872 | tf_op jit(solution)/shard_map/ppermute | solution.py:430
  15.4 1.3 %collective-permute-start.3 = (bf16[2,128,1024]{2,1,0:T(8,128)(2,1)S(1)}, bf16[2,128,1024]{2,1,0:T(8,128)(2,1)S(1)}, u32[]{:S(2)}, u32[]{:S(2)}) collective-permute-start(bf16[2,128,1024]{2,1,0:T(8,128)(2,1)S(1)} %get-tuple-element.21), channel_id=1, source_target_pairs={{1,5},{2,0},{3,7},{4,2},{5,9},{6,4},{7,11},{8,6},{9,13},{10,8},{11... | collective-permute-start | bytes 1572872 | tf_op jit(solution)/shard_map/ppermute | solution.py:430
  16.7 0.0 copy-done.4
  16.7 0.1 reshape.28
  16.8 0.0 copy-done
  16.8 0.7 %gather_fusion = f32[32]{0:T(128)S(1)} fusion(f32[128256]{0:T(1024)S(1)} %copy-done, s32[1024]{0:T(1024)S(1)} %pad_clamp_fusion), kind=kCustom, calls=%fused_computation | custom fusion | bytes 384 | tf_op jit(solution)/shard_map/jit(_take)/gather | solution.py:434
  17.5 0.1 reshape.27
  17.6 0.1 select_n.24
  17.7 0.0 copy-done.5
  17.7 0.1 broadcast_select_fusion
  17.8 0.0 copy-done.1
  17.8 0.0 copy-done.3
  17.8 0.0 copy-done.2
  17.8 15.6 %attend.1 = (f32[32,1,128]{2,1,0:T(1,128)S(1)}, bf16[16,128,1024]{2,1,0:T(8,128)(2,1)}) custom-call(s32[16]{0:T(128)S(1)} %get-tuple-element.22.len_ref, s32[16]{0:T(128)S(1)} %get-tuple-element.23.anc_ref, bf16[2,16,4096]{2,1,0:T(8,128)(2,1)S(1)} %copy-done.2, bf16[4096,1024]{1,0:T(8,128)(2,1)} %prompt_hbm.1, bf16[16,128,1024]{2,1,0:T(8,128)(2,1)} %gen_hbm.3, ...), custom_call_target="tpu_custom_call" | custom-call | flops 2214592512 | bytes 16777216 | tf_op jit(solution)/shard_map/attend/pallas_call | solution.py:304
  33.4 13.8 %all_to_all.5.refs_5_ = f32[32,1,128]{2,1,0:T(1,128)S(1)} all-to-all(f32[32,1,128]{2,1,0:T(1,128)S(1)} %get-tuple-element.25), channel_id=1, replica_groups=mesh['dom'=16,'tp'=2] {'dom','tp'}, dimensions={0} | all-to-all | bytes 32768 | tf_op jit(solution)/shard_map/all_to_all | solution.py:449
  47.3 0.0 collective-permute-done.refs_0_
  47.3 0.0 collective-permute-done.1.refs_1_
  47.3 0.0 collective-permute-done.2.refs_2_
  47.3 0.0 collective-permute-done.3.refs_3_
  47.3 2.4 %finish.1 = (bf16[16,128,1024]{2,1,0:T(8,128)(2,1)}, f32[2,16]{1,0:T(2,128)}, f32[1,16]{1,0:T(1,128)}) custom-call(s32[16]{0:T(128)S(1)} %get-tuple-element.17.slot_ref, bf16[2,128,1024]{2,1,0:T(8,128)(2,1)S(1)} %collective-permute-done.refs_0_, bf16[2,128,1024]{2,1,0:T(8,128)(2,1)S(1)} %collective-permute-done.1.refs_1_, ...), custom_call_target="tpu_custom_call", output_to_operand_aliasing={{0}: (5, {})} | custom-call | bytes 2097152 | tf_op jit(solution)/shard_map/finish/pallas_call | solution.py:377
  (4 shorter events, 0.0 us)
Async XLA Ops:
  0.6 16.2 %copy-start = (f32[128256]{0:T(1024)S(1)}, f32[128256]{0:T(1024)}, u32[]{:S(2)}) copy-start(f32[128256]{0:T(1024)} %param.18) | copy-start | bytes 1539076
  0.6 17.1 %copy-start.1 = (bf16[2,16,1024]{2,1,0:T(8,128)(2,1)S(1)}, bf16[2,16,1024]{2,1,0:T(8,128)(2,1)}, u32[]{:S(2)}) copy-start(bf16[2,16,1024]{2,1,0:T(8,128)(2,1)} %new_ref.1) | copy-start | bytes 196612
  0.7 16.1 %copy-start.4 = (s32[2,16]{1,0:T(2,128)S(1)}, s32[2,16]{1,0:T(2,128)}, u32[]{:S(2)}) copy-start(s32[2,16]{1,0:T(2,128)} %param.16) | copy-start | bytes 388
  0.7 17.0 %copy-start.5 = (f32[16]{0:T(128)S(1)}, f32[16]{0:T(128)}, u32[]{:S(2)}) copy-start(f32[16]{0:T(128)} %param.19) | copy-start | bytes 196
  0.7 17.1 %copy-start.3 = (f32[4096]{0:T(1024)S(1)}, f32[4096]{0:T(1024)}, u32[]{:S(2)}) copy-start(f32[4096]{0:T(1024)} %param.17) | copy-start | bytes 49156
  0.7 17.1 %copy-start.2 = (bf16[2,16,4096]{2,1,0:T(8,128)(2,1)S(1)}, bf16[2,16,4096]{2,1,0:T(8,128)(2,1)}, u32[]{:S(2)}) copy-start(bf16[2,16,4096]{2,1,0:T(8,128)(2,1)} %q_ref.1) | copy-start | bytes 786436
  4.6 42.7 %collective-permute-start = (bf16[2,128,1024]{2,1,0:T(8,128)(2,1)}, bf16[2,128,1024]{2,1,0:T(8,128)(2,1)S(1)}, u32[]{:S(2)}, u32[]{:S(2)}) collective-permute-start(bf16[2,128,1024]{2,1,0:T(8,128)(2,1)} %get-tuple-element.18), channel_id=1, source_target_pairs={{1,3},{3,5},{4,0},{5,7},{6,2},{7,9},{8,4},{9,11},{10,6},{11,13},{1... | collective-permute-start | bytes 1572872 | tf_op jit(solution)/shard_map/ppermute | solution.py:430
  5.9 41.4 %collective-permute-start.1 = (bf16[2,128,1024]{2,1,0:T(8,128)(2,1)}, bf16[2,128,1024]{2,1,0:T(8,128)(2,1)S(1)}, u32[]{:S(2)}, u32[]{:S(2)}) collective-permute-start(bf16[2,128,1024]{2,1,0:T(8,128)(2,1)} %get-tuple-element.19), channel_id=1, source_target_pairs={{0,4},{2,6},{3,1},{4,8},{5,3},{6,10},{7,5},{8,12},{9,7},{10,14},{1... | collective-permute-start | bytes 1572872 | tf_op jit(solution)/shard_map/ppermute | solution.py:430
  11.6 35.6 %collective-permute-start.2 = (bf16[2,128,1024]{2,1,0:T(8,128)(2,1)}, bf16[2,128,1024]{2,1,0:T(8,128)(2,1)S(1)}, u32[]{:S(2)}, u32[]{:S(2)}) collective-permute-start(bf16[2,128,1024]{2,1,0:T(8,128)(2,1)} %get-tuple-element.20), channel_id=1, source_target_pairs={{0,2},{2,4},{4,6},{5,1},{6,8},{7,3},{8,10},{9,5},{10,12},{11,7},{1... | collective-permute-start | bytes 1572872 | tf_op jit(solution)/shard_map/ppermute | solution.py:430
  15.4 31.9 %collective-permute-start.3 = (bf16[2,128,1024]{2,1,0:T(8,128)(2,1)S(1)}, bf16[2,128,1024]{2,1,0:T(8,128)(2,1)S(1)}, u32[]{:S(2)}, u32[]{:S(2)}) collective-permute-start(bf16[2,128,1024]{2,1,0:T(8,128)(2,1)S(1)} %get-tuple-element.21), channel_id=1, source_target_pairs={{1,5},{2,0},{3,7},{4,2},{5,9},{6,4},{7,11},{8,6},{9,13},{10,8},{11... | collective-permute-start | bytes 1572872 | tf_op jit(solution)/shard_map/ppermute | solution.py:430
where the time goes:
time: 50.1 us; the launch traced here: 49.7 us
  Pallas kernels  21.9 us (44%)
  blocking collectives  13.8 us (28%)
  starting transfers between devices  12.1 us (24%)
  local copies, waits for them, and re-layouts  0.99 us (2%)
  between operations  0.77 us (2%)
    pallas_call x1, Pallas kernels, attend(): pl.pallas_call(functools.partial(attend_kernel, per_dev, group, kv_local,...  15.6 us
    all_to_all x1, blocking collectives, local(): shares = lax.all_to_all(shares, everyone, 0, 0, tiled=True)  13.8 us
    ppermute x4, starting transfers between devices, local(): lax.ppermute(send, everyone, routes(doms, tps, steps))  12.1 us
    pallas_call x1, Pallas kernels, pack(): pl.pallas_call(functools.partial(pack_kernel, per_dev, doms, step_pairs),...  3.87 us
    pallas_call x1, Pallas kernels, finish(): pl.pallas_call(functools.partial(finish_kernel, doms, tps), out_shape=[ja...  2.42 us
  transfers between devices with their start and end apart: 4, of which 0 were waited for; matrix products, arithmetic and copies ran while one was open for 2% of the time, Pallas kernels for 31%

commit v1 on v0

--- a/solution.py
+++ b/solution.py
@@ -281,13 +281,13 @@
     padding = jnp.zeros((HEAD_DIM - base, HEAD_DIM), jnp.float32)
     square = jnp.concatenate([weighted, padding], axis=0)
     row = jnp.sum(square.T, axis=0, keepdims=True) + extra_ref[...]
-    share_ref[...] = jnp.broadcast_to(row[None], share_ref.shape)
+    share_ref[...] = jnp.broadcast_to(row, share_ref.shape)
     for home, copy in homes:
         pl.when(home)(copy.wait)
 
 
 def attend(
-    own_lengths, own_ancestors, queries, prompt_kv, gen_cache, new_kv, twist_vector, extra, devices
+    own_lengths, own_ancestors, queries, prompt_kv, gen_cache, new_kv, twist_vector, extra
 ):
     steps, per_dev, width = queries.shape
     keys, kv_width = prompt_kv.shape
@@ -304,7 +304,7 @@
     return pl.pallas_call(
         functools.partial(attend_kernel, per_dev, group, kv_local, chunk),
         out_shape=[
-            jax.ShapeDtypeStruct((devices, 1, HEAD_DIM), jnp.float32),
+            jax.ShapeDtypeStruct((8, HEAD_DIM), jnp.float32),
             jax.ShapeDtypeStruct(gen_cache.shape, jnp.bfloat16),
         ],
         in_specs=[smem, smem, vmem, hbm, hbm, vmem, vmem, vmem],
@@ -337,9 +337,9 @@
     )
 
 
-def finish_kernel(doms, tps, slot_ref, *refs):
+def deliver_kernel(slot_ref, *refs):
     gots = refs[: len(ORDERS[0])]
-    _, all_ref, out_ref, twist_ref, normal_ref, sums, sem = refs[len(gots) :]
+    _, out_ref, sem = refs[len(gots) :]
     per_dev = out_ref.shape[0]
     for p in range(per_dev):
         slot = slot_ref[p]
@@ -347,10 +347,36 @@
             for i in range(PICKS):
                 copy = pltpu.make_async_copy(got.at[i], out_ref.at[p], sem.at[p])
                 pl.when(slot == k * PICKS + i)(copy.start)
+    for p in range(per_dev):
+        copy = pltpu.make_async_copy(gots[0].at[0], out_ref.at[p], sem.at[p])
+        pl.when(slot_ref[p] >= 0)(copy.wait)
+
+
+def deliver(slots, gots, held):
+    smem = pl.BlockSpec(memory_space=pltpu.SMEM)
+    vmem = pl.BlockSpec(memory_space=pltpu.VMEM)
+    hbm = pl.BlockSpec(memory_space=pl.ANY)
+    return pl.pallas_call(
+        deliver_kernel,
+        out_shape=jax.ShapeDtypeStruct(held.shape, held.dtype),
+        in_specs=[smem] + [vmem] * len(gots) + [hbm],
+        out_specs=hbm,
+        input_output_aliases={1 + len(gots): 0},
+        scratch_shapes=[pltpu.SemaphoreType.DMA((held.shape[0],))],
+        compiler_params=pltpu.CompilerParams(vmem_limit_bytes=VMEM_BYTES),
+        cost_estimate=pl.CostEstimate(
+            flops=0, bytes_accessed=held.size, transcendentals=0
+        ),
+        name="deliver",
+    )(slots, *gots, held)
+
+
+def normalize_kernel(doms, tps, all_ref, twist_ref, normal_ref, sums):
+    per_dev = normal_ref.shape[1]
     for d in range(doms):
-        row = all_ref[d * tps]
+        row = all_ref[d * tps, :1]
         for t in range(1, tps):
-            row = row + all_ref[d * tps + t]
+            row = row + all_ref[d * tps + t, :1]
         sums[d : d + 1, :] = row
     step_0, step_1, prior = (
         slice(k * per_dev, (k + 1) * per_dev) for k in range(3)
@@ -363,37 +389,18 @@
     own = mine[:, prior] + mine[:, step_1] - mine[:, step_0]
     twist_ref[...] = jnp.concatenate([mine[:, step_0], mine[:, step_1]], axis=0)
     normal_ref[...] = own - log_total
-    for p in range(per_dev):
-        copy = pltpu.make_async_copy(gots[0].at[0], out_ref.at[p], sem.at[p])
-        pl.when(slot_ref[p] >= 0)(copy.wait)
-
-
-def finish(slots, gots, held, shares, doms, tps):
-    per_dev = held.shape[0]
-    count = len(gots)
-    smem = pl.BlockSpec(memory_space=pltpu.SMEM)
-    vmem = pl.BlockSpec(memory_space=pltpu.VMEM)
-    hbm = pl.BlockSpec(memory_space=pl.ANY)
+
+
+def normalize(shares, doms, tps, per_dev):
     return pl.pallas_call(
-        functools.partial(finish_kernel, doms, tps),
+        functools.partial(normalize_kernel, doms, tps),
         out_shape=[
-            jax.ShapeDtypeStruct(held.shape, held.dtype),
             jax.ShapeDtypeStruct((2, per_dev), jnp.float32),
             jax.ShapeDtypeStruct((1, per_dev), jnp.float32),
         ],
-        in_specs=[smem] + [vmem] * count + [hbm, vmem],
-        out_specs=[hbm, vmem, vmem],
-        input_output_aliases={1 + count: 0},
-        scratch_shapes=[
-            pltpu.VMEM((doms, HEAD_DIM), jnp.float32),
-            pltpu.SemaphoreType.DMA((per_dev,)),
-        ],
-        compiler_params=pltpu.CompilerParams(vmem_limit_bytes=VMEM_BYTES),
-        cost_estimate=pl.CostEstimate(
-            flops=0, bytes_accessed=held.size, transcendentals=0
-        ),
-        name="finish",
-    )(slots, *gots, held, shares)
+        scratch_shapes=[pltpu.VMEM((doms, HEAD_DIM), jnp.float32)],
+        name="normalize",
+    )(shares)
 
 
 def routes(doms, tps, steps):
@@ -444,10 +451,10 @@
         new_kv,
         twist_vector,
         extra,
-        doms * tps,
-    )
-    shares = lax.all_to_all(shares, everyone, 0, 0, tiled=True)
-    resampled, twist, normalized = finish(slots, arrivals, resampled, shares, doms, tps)
+    )
+    shares = lax.all_gather(shares, everyone)
+    resampled = deliver(slots, arrivals, resampled)
+    twist, normalized = normalize(shares, doms, tps, per_dev)
     return (twist, normalized.reshape(per_dev), resampled, new_lengths)
 
 

time: 50.1 us -> 81.5 us (1.63)
  blocking collectives: 13.8 us -> 43.8 us
  Pallas kernels: 21.9 us -> 23.2 us
    all_gather x0 -> x1, blocking collectives: none -> 43.8 us  [local(): shares = lax.all_gather(shares, everyone)]
    all_to_all x1 -> x0, blocking collectives: 13.8 us -> none  [local(): shares = lax.all_to_all(shares, everyone, 0, 0, tiled=True)]
    pallas_call x1 -> x2, Pallas kernels: 2.42 us -> 3.8 us  [the longest x1 1.91 us: deliver(): pl.pallas_call(deliver_kernel, out_shape=jax.ShapeDtypeStruct(held.shape,...]
  transfers between devices with their start and end apart: 4 -> 4, of which waited for: 0 -> 0; matrix products, arithmetic and copies ran while one was open for 2% -> 1% of each run, Pallas kernels for 31% -> 22%
where the time goes in v1:
time: 81.5 us; the launch traced here: 81.3 us
  blocking collectives  43.8 us (54%)
  Pallas kernels  23.2 us (28%)
  starting transfers between devices  12.4 us (15%)
  local copies, waits for them, and re-layouts  0.99 us (1%)
    all_gather x1, blocking collectives, local(): shares = lax.all_gather(shares, everyone)  43.8 us
    pallas_call x1, Pallas kernels, attend(): pl.pallas_call(functools.partial(attend_kernel, per_dev, group, kv_local,...  15.6 us
    ppermute x4, starting transfers between devices, local(): lax.ppermute(send, everyone, routes(doms, tps, steps))  12.4 us
    pallas_call x1, Pallas kernels, pack(): pl.pallas_call(functools.partial(pack_kernel, per_dev, doms, step_pairs),...  3.83 us
    pallas_call x1, Pallas kernels, deliver(): pl.pallas_call(deliver_kernel, out_shape=jax.ShapeDtypeStruct(held.shape,...  1.91 us
    pallas_call x1, Pallas kernels, normalize(): pl.pallas_call(functools.partial(normalize_kernel, doms, tps), out_shape=...  1.89 us
  transfers between devices with their start and end apart: 4, of which 0 were waited for; matrix products, arithmetic and copies ran while one was open for 1% of the time, Pallas kernels for 22%

profile of v1, /device:TPU:0, one launch (start us, length us, event | category | flops | bytes accessed | tf_op | source)
XLA Modules:
  0.0 81.3 jit_solution(13845512103972738891)
XLA Ops:
  0.6 0.0 copy-start
  0.6 0.0 copy-start.1
  0.7 0.0 copy-start.4
  0.7 0.0 copy-start.5
  0.7 0.0 copy-start.3
  0.7 0.0 copy-start.2
  0.7 3.8 %pack_sends.1 = (bf16[2,128,1024]{2,1,0:T(8,128)(2,1)}, bf16[2,128,1024]{2,1,0:T(8,128)(2,1)}, bf16[2,128,1024]{2,1,0:T(8,128)(2,1)}, bf16[2,128,1024]{2,1,0:T(8...) custom-call(s32[256]{0:T(256)} %len_hbm.1, s32[256]{0:T(256)} %anc_hbm.1, ...), custom_call_target="tpu_custom_call" | custom-call | bytes 4194304 | tf_op jit(solution)/shard_map/pack_sends/pallas_call | solution.py:110
  4.5 1.3 %collective-permute-start = (bf16[2,128,1024]{2,1,0:T(8,128)(2,1)}, bf16[2,128,1024]{2,1,0:T(8,128)(2,1)S(1)}, u32[]{:S(2)}, u32[]{:S(2)}) collective-permute-start(bf16[2,128,1024]{2,1,0:T(8,128)(2,1)} %get-tuple-element.22), channel_id=1, source_target_pairs={{1,3},{3,5},{4,0},{5,7},{6,2},{7,9},{8,4},{9,11},{10,6},{11,13},{1... | collective-permute-start | bytes 1572872 | tf_op jit(solution)/shard_map/ppermute | solution.py:437
  5.8 5.8 %collective-permute-start.1 = (bf16[2,128,1024]{2,1,0:T(8,128)(2,1)}, bf16[2,128,1024]{2,1,0:T(8,128)(2,1)S(1)}, u32[]{:S(2)}, u32[]{:S(2)}) collective-permute-start(bf16[2,128,1024]{2,1,0:T(8,128)(2,1)} %get-tuple-element.23), channel_id=1, source_target_pairs={{0,4},{2,6},{3,1},{4,8},{5,3},{6,10},{7,5},{8,12},{9,7},{10,14},{1... | collective-permute-start | bytes 1572872 | tf_op jit(solution)/shard_map/ppermute | solution.py:437
  11.6 4.1 %collective-permute-start.2 = (bf16[2,128,1024]{2,1,0:T(8,128)(2,1)}, bf16[2,128,1024]{2,1,0:T(8,128)(2,1)S(1)}, u32[]{:S(2)}, u32[]{:S(2)}) collective-permute-start(bf16[2,128,1024]{2,1,0:T(8,128)(2,1)} %get-tuple-element.24), channel_id=1, source_target_pairs={{0,2},{2,4},{4,6},{5,1},{6,8},{7,3},{8,10},{9,5},{10,12},{11,7},{1... | collective-permute-start | bytes 1572872 | tf_op jit(solution)/shard_map/ppermute | solution.py:437
  15.7 1.3 %collective-permute-start.3 = (bf16[2,128,1024]{2,1,0:T(8,128)(2,1)S(1)}, bf16[2,128,1024]{2,1,0:T(8,128)(2,1)S(1)}, u32[]{:S(2)}, u32[]{:S(2)}) collective-permute-start(bf16[2,128,1024]{2,1,0:T(8,128)(2,1)S(1)} %get-tuple-element.25), channel_id=1, source_target_pairs={{1,5},{2,0},{3,7},{4,2},{5,9},{6,4},{7,11},{8,6},{9,13},{10,8},{11... | collective-permute-start | bytes 1572872 | tf_op jit(solution)/shard_map/ppermute | solution.py:437
  17.0 0.0 copy-done.4
  17.0 0.1 reshape.28
  17.1 0.0 copy-done
  17.1 0.7 gather_fusion
  17.8 0.1 reshape.27
  17.9 0.1 select_n.24
  18.0 0.0 copy-done.5
  18.0 0.1 broadcast_select_fusion
  18.0 0.0 copy-done.1
  18.0 0.0 copy-done.3
  18.0 0.0 copy-done.2
  18.1 15.6 %attend.1 = (f32[8,128]{1,0:T(8,128)S(1)}, bf16[16,128,1024]{2,1,0:T(8,128)(2,1)}) custom-call(s32[16]{0:T(128)S(1)} %get-tuple-element.16.len_ref, s32[16]{0:T(128)S(1)} %get-tuple-element.17.anc_ref, bf16[2,16,4096]{2,1,0:T(8,128)(2,1)S(1)} %copy-done.2, bf16[4096,1024]{1,0:T(8,128)(2,1)} %prompt_hbm.1, bf16[16,128,1024]{2,1,0:T(8,128)(2,1)} %gen_hbm.3, ...), custom_call_target="tpu_custom_call" | custom-call | flops 2214592512 | bytes 16777216 | tf_op jit(solution)/shard_map/attend/pallas_call | solution.py:304
  33.7 43.8 %all-gather = f32[256,128]{1,0:T(8,128)} all-gather(f32[8,128]{1,0:T(8,128)S(1)} %get-tuple-element.18), channel_id=2, replica_groups=mesh['dom'=16,'tp'=2] {'dom','tp'}, dimensions={0}, use_global_device_ids=true | all-gather | bytes 135168 | tf_op jit(solution)/shard_map/all_gather | solution.py:455
  77.4 1.9 %normalize.1 = (f32[2,16]{1,0:T(2,128)}, f32[1,16]{1,0:T(1,128)}) custom-call(f32[32,8,128]{2,1,0:T(8,128)} %bitcast.6), custom_call_target="tpu_custom_call" | custom-call | tf_op jit(solution)/shard_map/normalize/pallas_call | solution.py:395
  79.3 0.0 collective-permute-done.refs_0_
  79.3 0.0 collective-permute-done.1.refs_1_
  79.3 0.0 collective-permute-done.2.refs_2_
  79.3 0.0 collective-permute-done.3.refs_3_
  79.4 1.9 %deliver.1 = bf16[16,128,1024]{2,1,0:T(8,128)(2,1)} custom-call(s32[16]{0:T(128)S(1)} %get-tuple-element.21.slot_ref, bf16[2,128,1024]{2,1,0:T(8,128)(2,1)S(1)} %collective-permute-done.refs_0_, bf16[2,128,1024]{2,1,0:T(8,128)(2,1)S(1)} %collective-permute-done.1.refs_1_, ...), custom_call_target="tpu_custom_call", output_to_operand_aliasing={{}: (5, {})} | custom-call | bytes 2097152 | tf_op jit(solution)/shard_map/deliver/pallas_call | solution.py:359
  (4 shorter events, 0.0 us)
Async XLA Ops:
  0.6 16.4 %copy-start = (f32[128256]{0:T(1024)S(1)}, f32[128256]{0:T(1024)}, u32[]{:S(2)}) copy-start(f32[128256]{0:T(1024)} %param.18) | copy-start | bytes 1539076
  0.6 17.4 %copy-start.1 = (bf16[2,16,1024]{2,1,0:T(8,128)(2,1)S(1)}, bf16[2,16,1024]{2,1,0:T(8,128)(2,1)}, u32[]{:S(2)}) copy-start(bf16[2,16,1024]{2,1,0:T(8,128)(2,1)} %new_ref.1) | copy-start | bytes 196612
  0.7 16.3 %copy-start.4 = (s32[2,16]{1,0:T(2,128)S(1)}, s32[2,16]{1,0:T(2,128)}, u32[]{:S(2)}) copy-start(s32[2,16]{1,0:T(2,128)} %param.16) | copy-start | bytes 388
  0.7 17.3 %copy-start.5 = (f32[16]{0:T(128)S(1)}, f32[16]{0:T(128)}, u32[]{:S(2)}) copy-start(f32[16]{0:T(128)} %param.19) | copy-start | bytes 196
  0.7 17.4 %copy-start.3 = (f32[4096]{0:T(1024)S(1)}, f32[4096]{0:T(1024)}, u32[]{:S(2)}) copy-start(f32[4096]{0:T(1024)} %param.17) | copy-start | bytes 49156
  0.7 17.4 %copy-start.2 = (bf16[2,16,4096]{2,1,0:T(8,128)(2,1)S(1)}, bf16[2,16,4096]{2,1,0:T(8,128)(2,1)}, u32[]{:S(2)}) copy-start(bf16[2,16,4096]{2,1,0:T(8,128)(2,1)} %q_ref.1) | copy-start | bytes 786436
  4.5 74.8 %collective-permute-start = (bf16[2,128,1024]{2,1,0:T(8,128)(2,1)}, bf16[2,128,1024]{2,1,0:T(8,128)(2,1)S(1)}, u32[]{:S(2)}, u32[]{:S(2)}) collective-permute-start(bf16[2,128,1024]{2,1,0:T(8,128)(2,1)} %get-tuple-element.22), channel_id=1, source_target_pairs={{1,3},{3,5},{4,0},{5,7},{6,2},{7,9},{8,4},{9,11},{10,6},{11,13},{1... | collective-permute-start | bytes 1572872 | tf_op jit(solution)/shard_map/ppermute | solution.py:437
  5.8 73.5 %collective-permute-start.1 = (bf16[2,128,1024]{2,1,0:T(8,128)(2,1)}, bf16[2,128,1024]{2,1,0:T(8,128)(2,1)S(1)}, u32[]{:S(2)}, u32[]{:S(2)}) collective-permute-start(bf16[2,128,1024]{2,1,0:T(8,128)(2,1)} %get-tuple-element.23), channel_id=1, source_target_pairs={{0,4},{2,6},{3,1},{4,8},{5,3},{6,10},{7,5},{8,12},{9,7},{10,14},{1... | collective-permute-start | bytes 1572872 | tf_op jit(solution)/shard_map/ppermute | solution.py:437
  11.6 67.7 %collective-permute-start.2 = (bf16[2,128,1024]{2,1,0:T(8,128)(2,1)}, bf16[2,128,1024]{2,1,0:T(8,128)(2,1)S(1)}, u32[]{:S(2)}, u32[]{:S(2)}) collective-permute-start(bf16[2,128,1024]{2,1,0:T(8,128)(2,1)} %get-tuple-element.24), channel_id=1, source_target_pairs={{0,2},{2,4},{4,6},{5,1},{6,8},{7,3},{8,10},{9,5},{10,12},{11,7},{1... | collective-permute-start | bytes 1572872 | tf_op jit(solution)/shard_map/ppermute | solution.py:437
  15.7 63.7 %collective-permute-start.3 = (bf16[2,128,1024]{2,1,0:T(8,128)(2,1)S(1)}, bf16[2,128,1024]{2,1,0:T(8,128)(2,1)S(1)}, u32[]{:S(2)}, u32[]{:S(2)}) collective-permute-start(bf16[2,128,1024]{2,1,0:T(8,128)(2,1)S(1)} %get-tuple-element.25), channel_id=1, source_target_pairs={{1,5},{2,0},{3,7},{4,2},{5,9},{6,4},{7,11},{8,6},{9,13},{10,8},{11... | collective-permute-start | bytes 1572872 | tf_op jit(solution)/shard_map/ppermute | solution.py:437

commit v2 on v0

--- a/solution.py
+++ b/solution.py
@@ -150,6 +150,7 @@
     out_hbm,
     prompt,
     grown,
+    new_rows,
     scores,
     mixed_ref,
     prompt_sem,
@@ -165,11 +166,11 @@
     base = steps * per_dev
     lanes = group * base
 
-    loads = [
-        pltpu.make_async_copy(gen_hbm.at[p], grown.at[p], gen_sem.at[p]) for p in range(per_dev)
-    ]
-    for load in loads:
-        load.start()
+    half = per_dev // 2
+    per_chunk = per_dev // chunks
+
+    def gen_load(p):
+        return pltpu.make_async_copy(gen_hbm.at[p], grown.at[p], gen_sem.at[p])
 
     def prompt_load(j):
         part = pl.ds(pl.multiple_of(j * chunk, chunk), chunk)
@@ -177,17 +178,55 @@
 
     for j in range(chunks):
         prompt_load(j).start()
-
-    new_rows = new_ref[...].astype(jnp.float32).reshape(base, width)
+        for i in range(per_chunk):
+            gen_load(j * per_chunk + i).start()
+
+    new_rows[...] = new_ref[...].astype(jnp.float32).reshape(base, width)
     row_ids = lax.broadcasted_iota(jnp.int32, (rows, width), 0)
-    for p in range(per_dev):
-        loads[p].wait()
+
+    def patch(p):
+        gen_load(p).wait()
         behind = row_ids - len_ref[p]
-        tail = jnp.where(behind == 1, new_rows[per_dev + p : per_dev + p + 1], 0.0)
-        tail = jnp.where(behind == 0, new_rows[p : p + 1], tail)
+        tail = jnp.where(behind == 1, new_rows[pl.ds(per_dev + p, 1), :], 0.0)
+        tail = jnp.where(behind == 0, new_rows[pl.ds(p, 1), :], tail)
         grown[p] = jnp.where(behind < 0, grown[p].astype(jnp.float32), tail).astype(
             jnp.bfloat16
         )
+
+    q2 = q_ref[...].reshape(base, q_ref.shape[-1])
+    queries = [
+        jnp.concatenate(
+            [q2[:, h * HEAD_DIM : (h + 1) * HEAD_DIM] for h in range(c * group, (c + 1) * group)],
+            axis=0,
+        )
+        for c in range(kv_local)
+    ]
+
+    def score(keys, rows):
+        return lax.dot_general(
+            keys, rows, (((1,), (1,)), ((), ())), preferred_element_type=jnp.float32
+        )
+
+    def mix(values, probs):
+        return lax.dot_general(
+            values, probs, (((0,), (0,)), ((), ())), preferred_element_type=jnp.float32
+        )
+
+    def score_chunk(j, tops):
+        prompt_load(j).wait()
+        part = pl.ds(pl.multiple_of(j * chunk, chunk), chunk)
+        raised = []
+        for c in range(kv_local):
+            block = score(prompt[part, c * pair : c * pair + HEAD_DIM], queries[c]) * scale
+            scores[c, part] = block
+            raised.append(jnp.maximum(tops[c], fold_rows(block, jnp.max)))
+        for i in range(per_chunk):
+            patch(j * per_chunk + i)
+        return tuple(raised)
+
+    lowest = jnp.full((8, lanes), NEG_FILL, jnp.float32)
+    tops = lax.fori_loop(0, chunks, score_chunk, (lowest,) * kv_local)
+
     homes = []
     for p in range(per_dev):
         local = anc_ref[p] - me * per_dev
@@ -197,67 +236,53 @@
         homes.append((home, copy))
         pl.when(home)(copy.start)
 
-    q2 = q_ref[...].reshape(base, q_ref.shape[-1])
-    queries = [
-        jnp.concatenate(
-            [q2[:, h * HEAD_DIM : (h + 1) * HEAD_DIM] for h in range(c * group, (c + 1) * group)],
-            axis=0,
-        )
-        for c in range(kv_local)
-    ]
-
-    def score(keys, c):
-        return lax.dot_general(
-            keys, queries[c], (((1,), (1,)), ((), ())), preferred_element_type=jnp.float32
-        )
-
-    def mix(values, probs):
-        return lax.dot_general(
-            values, probs, (((0,), (0,)), ((), ())), preferred_element_type=jnp.float32
-        )
-
     lane_ids = lax.broadcasted_iota(jnp.int32, (rows, lanes), 1)
     owner = lane_ids % per_dev
+    lower, seat = owner < half, owner % half
     last = lane_ids // per_dev % steps
     for p in range(per_dev):
         last = last + jnp.where(owner == p, len_ref[p], 0)
     visible = lax.broadcasted_iota(jnp.int32, (rows, lanes), 0) <= last
-
-    own_scores = []
-    tops = []
+    query_lower = lax.broadcasted_iota(jnp.int32, (lanes, HEAD_DIM), 0) % per_dev < half
+
+    def halves(block, lower, axis):
+        block = block.astype(jnp.float32)
+        parts = [jnp.where(lower, block, 0.0), jnp.where(lower, 0.0, block)]
+        return jnp.concatenate(parts, axis=axis).astype(jnp.bfloat16)
+
+    def by_seat(blocks):
+        size = blocks.shape[0] // half
+        chosen = blocks[:size]
+        for i in range(1, half):
+            chosen = jnp.where(seat == i, blocks[i * size : (i + 1) * size], chosen)
+        return chosen
+
+    totals = []
+    maxima = []
     for c in range(kv_local):
-        keys = grown[:, :, c * pair : c * pair + HEAD_DIM].reshape(per_dev * rows, HEAD_DIM)
-        every = score(keys, c)
-        own = every[:rows]
-        for p in range(1, per_dev):
-            own = jnp.where(owner == p, every[p * rows : (p + 1) * rows], own)
+        columns = slice(c * pair, c * pair + HEAD_DIM)
+        keys = jnp.concatenate(
+            [
+                jnp.concatenate([grown[i, :, columns], grown[i + half, :, columns]], axis=1)
+                for i in range(half)
+            ],
+            axis=0,
+        )
+        own = by_seat(score(keys, halves(queries[c], query_lower, 1)))
         own = jnp.where(visible, own * scale, NEG_FILL)
-        own_scores.append(own)
-        tops.append(fold_rows(own, jnp.max))
-
-    def score_chunk(j, tops):
-        prompt_load(j).wait()
-        part = pl.ds(pl.multiple_of(j * chunk, chunk), chunk)
-        raised = []
-        for c in range(kv_local):
-            block = score(prompt[part, c * pair : c * pair + HEAD_DIM], c) * scale
-            scores[c, part] = block
-            raised.append(jnp.maximum(tops[c], fold_rows(block, jnp.max)))
-        return tuple(raised)
-
-    tops = lax.fori_loop(0, chunks, score_chunk, tuple(tops))
-    maxima = [jnp.max(top, axis=0, keepdims=True) for top in tops]
-
-    totals = []
-    for c in range(kv_local):
-        exps = jnp.where(visible, jnp.exp(own_scores[c] - maxima[c]), 0.0)
+        top = jnp.maximum(tops[c], fold_rows(own, jnp.max))
+        maxima.append(jnp.max(top, axis=0, keepdims=True))
+        exps = jnp.where(visible, jnp.exp(own - maxima[c]), 0.0)
         totals.append(fold_rows(exps, jnp.sum))
-        probs = jnp.concatenate(
-            [jnp.where(owner == p, exps, 0.0).astype(jnp.bfloat16) for p in range(per_dev)],
-            axis=0,
-        )
-        values = grown[:, :, c * pair + HEAD_DIM : (c + 1) * pair]
-        mixed_ref[c] = mix(values.reshape(per_dev * rows, HEAD_DIM), probs)
+        columns = slice(c * pair + HEAD_DIM, (c + 1) * pair)
+        values = jnp.concatenate(
+            [
+                jnp.concatenate([grown[i, :, columns], grown[i + half, :, columns]], axis=0)
+                for i in range(half)
+            ],
+            axis=1,
+        )
+        mixed_ref[c] = by_seat(mix(values, halves(exps, lower, 0)))
 
     def mix_chunk(j, totals):
         part = pl.ds(pl.multiple_of(j * chunk, chunk), chunk)
@@ -312,6 +337,7 @@
         scratch_shapes=[
             pltpu.VMEM(prompt_kv.shape, jnp.bfloat16),
             pltpu.VMEM(gen_cache.shape, jnp.bfloat16),
+            pltpu.VMEM((steps * per_dev, kv_width), jnp.float32),
             pltpu.VMEM((kv_local, keys, lanes), jnp.float32),
             pltpu.VMEM((kv_local, HEAD_DIM, lanes), jnp.float32),
             pltpu.SemaphoreType.DMA((keys // chunk,)),

time: 50.1 us -> 49.8 us (level)
    pallas_call x1, Pallas kernels: 15.6 us -> 14.9 us  [attend(): pl.pallas_call(functools.partial(attend_kernel, per_dev, group, kv_local,...]
  transfers between devices with their start and end apart: 4 -> 4, of which waited for: 0 -> 0; matrix products, arithmetic and copies ran while one was open for 2% -> 2% of each run, Pallas kernels for 31% -> 30%
where the time goes in v2:
time: 49.8 us; the launch traced here: 49.5 us
  Pallas kernels  21.9 us (44%)
  blocking collectives  14.1 us (28%)
  starting transfers between devices  11.6 us (23%)
  local copies, waits for them, and re-layouts  0.99 us (2%)
  between operations  0.77 us (2%)
    pallas_call x1, Pallas kernels, attend(): pl.pallas_call(functools.partial(attend_kernel, per_dev, group, kv_local,...  14.9 us
    all_to_all x1, blocking collectives, local(): shares = lax.all_to_all(shares, everyone, 0, 0, tiled=True)  14.1 us
    ppermute x4, starting transfers between devices, local(): lax.ppermute(send, everyone, routes(doms, tps, steps))  11.6 us
    pallas_call x1, Pallas kernels, pack(): pl.pallas_call(functools.partial(pack_kernel, per_dev, doms, step_pairs),...  4.31 us
    pallas_call x1, Pallas kernels, finish(): pl.pallas_call(functools.partial(finish_kernel, doms, tps), out_shape=[ja...  2.67 us
  transfers between devices with their start and end apart: 4, of which 0 were waited for; matrix products, arithmetic and copies ran while one was open for 2% of the time, Pallas kernels for 30%

profile of v2, /device:TPU:0, one launch (start us, length us, event | category | flops | bytes accessed | tf_op | source)
XLA Modules:
  0.0 49.5 jit_solution(11238151702216998297)
XLA Ops:
  0.6 0.0 copy-start
  0.6 0.0 copy-start.1
  0.7 0.0 copy-start.4
  0.7 0.0 copy-start.5
  0.7 0.0 copy-start.3
  0.7 0.0 copy-start.2
  0.7 4.3 %pack_sends.1 = (bf16[2,128,1024]{2,1,0:T(8,128)(2,1)}, bf16[2,128,1024]{2,1,0:T(8,128)(2,1)}, bf16[2,128,1024]{2,1,0:T(8,128)(2,1)}, bf16[2,128,1024]{2,1,0:T(8...) custom-call(s32[256]{0:T(256)} %len_hbm.1, s32[256]{0:T(256)} %anc_hbm.1, ...), custom_call_target="tpu_custom_call" | custom-call | bytes 4194304 | tf_op jit(solution)/shard_map/pack_sends/pallas_call | solution.py:110
  5.0 1.3 %collective-permute-start = (bf16[2,128,1024]{2,1,0:T(8,128)(2,1)}, bf16[2,128,1024]{2,1,0:T(8,128)(2,1)S(1)}, u32[]{:S(2)}, u32[]{:S(2)}) collective-permute-start(bf16[2,128,1024]{2,1,0:T(8,128)(2,1)} %get-tuple-element.18), channel_id=1, source_target_pairs={{1,3},{3,5},{4,0},{5,7},{6,2},{7,9},{8,4},{9,11},{10,6},{11,13},{1... | collective-permute-start | bytes 1572872 | tf_op jit(solution)/shard_map/ppermute | solution.py:456
  6.3 5.1 %collective-permute-start.1 = (bf16[2,128,1024]{2,1,0:T(8,128)(2,1)}, bf16[2,128,1024]{2,1,0:T(8,128)(2,1)S(1)}, u32[]{:S(2)}, u32[]{:S(2)}) collective-permute-start(bf16[2,128,1024]{2,1,0:T(8,128)(2,1)} %get-tuple-element.19), channel_id=1, source_target_pairs={{0,4},{2,6},{3,1},{4,8},{5,3},{6,10},{7,5},{8,12},{9,7},{10,14},{1... | collective-permute-start | bytes 1572872 | tf_op jit(solution)/shard_map/ppermute | solution.py:456
  11.5 3.9 %collective-permute-start.2 = (bf16[2,128,1024]{2,1,0:T(8,128)(2,1)}, bf16[2,128,1024]{2,1,0:T(8,128)(2,1)S(1)}, u32[]{:S(2)}, u32[]{:S(2)}) collective-permute-start(bf16[2,128,1024]{2,1,0:T(8,128)(2,1)} %get-tuple-element.20), channel_id=1, source_target_pairs={{0,2},{2,4},{4,6},{5,1},{6,8},{7,3},{8,10},{9,5},{10,12},{11,7},{1... | collective-permute-start | bytes 1572872 | tf_op jit(solution)/shard_map/ppermute | solution.py:456
  15.4 1.3 %collective-permute-start.3 = (bf16[2,128,1024]{2,1,0:T(8,128)(2,1)S(1)}, bf16[2,128,1024]{2,1,0:T(8,128)(2,1)S(1)}, u32[]{:S(2)}, u32[]{:S(2)}) collective-permute-start(bf16[2,128,1024]{2,1,0:T(8,128)(2,1)S(1)} %get-tuple-element.21), channel_id=1, source_target_pairs={{1,5},{2,0},{3,7},{4,2},{5,9},{6,4},{7,11},{8,6},{9,13},{10,8},{11... | collective-permute-start | bytes 1572872 | tf_op jit(solution)/shard_map/ppermute | solution.py:456
  16.7 0.0 copy-done.4
  16.7 0.1 reshape.28
  16.8 0.0 copy-done
  16.8 0.7 %gather_fusion = f32[32]{0:T(128)S(1)} fusion(f32[128256]{0:T(1024)S(1)} %copy-done, s32[1024]{0:T(1024)S(1)} %pad_clamp_fusion), kind=kCustom, calls=%fused_computation | custom fusion | bytes 384 | tf_op jit(solution)/shard_map/jit(_take)/gather | solution.py:460
  17.5 0.1 reshape.27
  17.6 0.1 select_n.24
  17.6 0.0 copy-done.5
  17.7 0.1 broadcast_select_fusion
  17.7 0.0 copy-done.1
  17.7 0.0 copy-done.3
  17.7 0.0 copy-done.2
  17.8 14.9 %attend.1 = (f32[32,1,128]{2,1,0:T(1,128)S(1)}, bf16[16,128,1024]{2,1,0:T(8,128)(2,1)}) custom-call(s32[16]{0:T(128)S(1)} %get-tuple-element.22.len_ref, s32[16]{0:T(128)S(1)} %get-tuple-element.23.anc_ref, bf16[2,16,4096]{2,1,0:T(8,128)(2,1)S(1)} %copy-done.2, bf16[4096,1024]{1,0:T(8,128)(2,1)} %prompt_hbm.1, bf16[16,128,1024]{2,1,0:T(8,128)(2,1)} %gen_hbm.3, ...), custom_call_target="tpu_custom_call" | custom-call | flops 2214592512 | bytes 16777216 | tf_op jit(solution)/shard_map/attend/pallas_call | solution.py:329
  32.7 14.1 %all_to_all.5.refs_5_ = f32[32,1,128]{2,1,0:T(1,128)S(1)} all-to-all(f32[32,1,128]{2,1,0:T(1,128)S(1)} %get-tuple-element.25), channel_id=1, replica_groups=mesh['dom'=16,'tp'=2] {'dom','tp'}, dimensions={0} | all-to-all | bytes 32768 | tf_op jit(solution)/shard_map/all_to_all | solution.py:475
  46.8 0.0 collective-permute-done.refs_0_
  46.8 0.0 collective-permute-done.1.refs_1_
  46.8 0.0 collective-permute-done.2.refs_2_
  46.9 0.0 collective-permute-done.3.refs_3_
  46.9 2.7 %finish.1 = (bf16[16,128,1024]{2,1,0:T(8,128)(2,1)}, f32[2,16]{1,0:T(2,128)}, f32[1,16]{1,0:T(1,128)}) custom-call(s32[16]{0:T(128)S(1)} %get-tuple-element.17.slot_ref, bf16[2,128,1024]{2,1,0:T(8,128)(2,1)S(1)} %collective-permute-done.refs_0_, bf16[2,128,1024]{2,1,0:T(8,128)(2,1)S(1)} %collective-permute-done.1.refs_1_, ...), custom_call_target="tpu_custom_call", output_to_operand_aliasing={{0}: (5, {})} | custom-call | bytes 2097152 | tf_op jit(solution)/shard_map/finish/pallas_call | solution.py:403
  (4 shorter events, 0.0 us)
Async XLA Ops:
  0.6 16.1 %copy-start = (f32[128256]{0:T(1024)S(1)}, f32[128256]{0:T(1024)}, u32[]{:S(2)}) copy-start(f32[128256]{0:T(1024)} %param.18) | copy-start | bytes 1539076
  0.6 17.1 %copy-start.1 = (bf16[2,16,1024]{2,1,0:T(8,128)(2,1)S(1)}, bf16[2,16,1024]{2,1,0:T(8,128)(2,1)}, u32[]{:S(2)}) copy-start(bf16[2,16,1024]{2,1,0:T(8,128)(2,1)} %new_ref.1) | copy-start | bytes 196612
  0.7 16.0 %copy-start.4 = (s32[2,16]{1,0:T(2,128)S(1)}, s32[2,16]{1,0:T(2,128)}, u32[]{:S(2)}) copy-start(s32[2,16]{1,0:T(2,128)} %param.16) | copy-start | bytes 388
  0.7 17.0 %copy-start.5 = (f32[16]{0:T(128)S(1)}, f32[16]{0:T(128)}, u32[]{:S(2)}) copy-start(f32[16]{0:T(128)} %param.19) | copy-start | bytes 196
  0.7 17.1 %copy-start.3 = (f32[4096]{0:T(1024)S(1)}, f32[4096]{0:T(1024)}, u32[]{:S(2)}) copy-start(f32[4096]{0:T(1024)} %param.17) | copy-start | bytes 49156
  0.7 17.1 %copy-start.2 = (bf16[2,16,4096]{2,1,0:T(8,128)(2,1)S(1)}, bf16[2,16,4096]{2,1,0:T(8,128)(2,1)}, u32[]{:S(2)}) copy-start(bf16[2,16,4096]{2,1,0:T(8,128)(2,1)} %q_ref.1) | copy-start | bytes 786436
  5.0 41.8 %collective-permute-start = (bf16[2,128,1024]{2,1,0:T(8,128)(2,1)}, bf16[2,128,1024]{2,1,0:T(8,128)(2,1)S(1)}, u32[]{:S(2)}, u32[]{:S(2)}) collective-permute-start(bf16[2,128,1024]{2,1,0:T(8,128)(2,1)} %get-tuple-element.18), channel_id=1, source_target_pairs={{1,3},{3,5},{4,0},{5,7},{6,2},{7,9},{8,4},{9,11},{10,6},{11,13},{1... | collective-permute-start | bytes 1572872 | tf_op jit(solution)/shard_map/ppermute | solution.py:456
  6.3 40.5 %collective-permute-start.1 = (bf16[2,128,1024]{2,1,0:T(8,128)(2,1)}, bf16[2,128,1024]{2,1,0:T(8,128)(2,1)S(1)}, u32[]{:S(2)}, u32[]{:S(2)}) collective-permute-start(bf16[2,128,1024]{2,1,0:T(8,128)(2,1)} %get-tuple-element.19), channel_id=1, source_target_pairs={{0,4},{2,6},{3,1},{4,8},{5,3},{6,10},{7,5},{8,12},{9,7},{10,14},{1... | collective-permute-start | bytes 1572872 | tf_op jit(solution)/shard_map/ppermute | solution.py:456
  11.5 35.4 %collective-permute-start.2 = (bf16[2,128,1024]{2,1,0:T(8,128)(2,1)}, bf16[2,128,1024]{2,1,0:T(8,128)(2,1)S(1)}, u32[]{:S(2)}, u32[]{:S(2)}) collective-permute-start(bf16[2,128,1024]{2,1,0:T(8,128)(2,1)} %get-tuple-element.20), channel_id=1, source_target_pairs={{0,2},{2,4},{4,6},{5,1},{6,8},{7,3},{8,10},{9,5},{10,12},{11,7},{1... | collective-permute-start | bytes 1572872 | tf_op jit(solution)/shard_map/ppermute | solution.py:456
  15.4 31.5 %collective-permute-start.3 = (bf16[2,128,1024]{2,1,0:T(8,128)(2,1)S(1)}, bf16[2,128,1024]{2,1,0:T(8,128)(2,1)S(1)}, u32[]{:S(2)}, u32[]{:S(2)}) collective-permute-start(bf16[2,128,1024]{2,1,0:T(8,128)(2,1)S(1)} %get-tuple-element.21), channel_id=1, source_target_pairs={{1,5},{2,0},{3,7},{4,2},{5,9},{6,4},{7,11},{8,6},{9,13},{10,8},{11... | collective-permute-start | bytes 1572872 | tf_op jit(solution)/shard_map/ppermute | solution.py:456

commit v3 on v2

--- a/solution.py
+++ b/solution.py
@@ -129,8 +129,10 @@
     )(*(in_hbm(x) for x in (lengths, ancestors, new_kv, gen_cache)))
 
 
-def fold_rows(block, combine):
-    return combine(block.reshape(block.shape[0] // 8, 8, block.shape[1]), axis=0)
+def fold_lanes(block, combine, start):
+    for first in range(0, block.shape[1], HEAD_DIM):
+        start = combine(start, block[:, first : first + HEAD_DIM])
+    return start
 
 
 def attend_kernel(
@@ -152,6 +154,8 @@
     grown,
     new_rows,
     scores,
+    tops,
+    totals,
     mixed_ref,
     prompt_sem,
     gen_sem,
@@ -164,7 +168,6 @@
     pair = 2 * HEAD_DIM
     scale = 1.0 / math.sqrt(HEAD_DIM)
     base = steps * per_dev
-    lanes = group * base
 
     half = per_dev // 2
     per_chunk = per_dev // chunks
@@ -202,30 +205,28 @@
         for c in range(kv_local)
     ]
 
-    def score(keys, rows):
+    def score(query_rows, keys):
         return lax.dot_general(
-            keys, rows, (((1,), (1,)), ((), ())), preferred_element_type=jnp.float32
+            query_rows, keys, (((1,), (1,)), ((), ())), preferred_element_type=jnp.float32
         )
 
-    def mix(values, probs):
-        return lax.dot_general(
-            values, probs, (((0,), (0,)), ((), ())), preferred_element_type=jnp.float32
-        )
-
-    def score_chunk(j, tops):
+    def mix(probs, values):
+        return jnp.dot(probs, values, preferred_element_type=jnp.float32)
+
+    tops[...] = jnp.full(tops.shape, NEG_FILL, jnp.float32)
+
+    def score_chunk(j, carry):
         prompt_load(j).wait()
         part = pl.ds(pl.multiple_of(j * chunk, chunk), chunk)
-        raised = []
         for c in range(kv_local):
-            block = score(prompt[part, c * pair : c * pair + HEAD_DIM], queries[c]) * scale
-            scores[c, part] = block
-            raised.append(jnp.maximum(tops[c], fold_rows(block, jnp.max)))
+            block = score(queries[c], prompt[part, c * pair : c * pair + HEAD_DIM]) * scale
+            scores[c, j] = block
+            tops[c] = fold_lanes(block, jnp.maximum, tops[c])
         for i in range(per_chunk):
             patch(j * per_chunk + i)
-        return tuple(raised)
-
-    lowest = jnp.full((8, lanes), NEG_FILL, jnp.float32)
-    tops = lax.fori_loop(0, chunks, score_chunk, (lowest,) * kv_local)
+        return carry
+
+    lax.fori_loop(0, chunks, score_chunk, 0)
 
     homes = []
     for p in range(per_dev):
@@ -236,29 +237,29 @@
         homes.append((home, copy))
         pl.when(home)(copy.start)
 
-    lane_ids = lax.broadcasted_iota(jnp.int32, (rows, lanes), 1)
-    owner = lane_ids % per_dev
-    lower, seat = owner < half, owner % half
-    last = lane_ids // per_dev % steps
+    row_ids = lax.broadcasted_iota(jnp.int32, (base, rows), 0)
+    owner = row_ids % per_dev
+    last = row_ids // per_dev
     for p in range(per_dev):
         last = last + jnp.where(owner == p, len_ref[p], 0)
-    visible = lax.broadcasted_iota(jnp.int32, (rows, lanes), 0) <= last
-    query_lower = lax.broadcasted_iota(jnp.int32, (lanes, HEAD_DIM), 0) % per_dev < half
-
-    def halves(block, lower, axis):
+    visible = lax.broadcasted_iota(jnp.int32, (base, rows), 1) <= last
+    visible, lower, seat = (
+        jnp.concatenate([part.astype(jnp.int32)] * group, axis=0)
+        for part in (visible, owner < half, owner % half)
+    )
+    visible, lower = visible == 1, lower == 1
+
+    def halves(block):
         block = block.astype(jnp.float32)
         parts = [jnp.where(lower, block, 0.0), jnp.where(lower, 0.0, block)]
-        return jnp.concatenate(parts, axis=axis).astype(jnp.bfloat16)
+        return jnp.concatenate(parts, axis=1).astype(jnp.bfloat16)
 
     def by_seat(blocks):
-        size = blocks.shape[0] // half
-        chosen = blocks[:size]
+        chosen = blocks[:, :HEAD_DIM]
         for i in range(1, half):
-            chosen = jnp.where(seat == i, blocks[i * size : (i + 1) * size], chosen)
+            chosen = jnp.where(seat == i, blocks[:, i * HEAD_DIM : (i + 1) * HEAD_DIM], chosen)
         return chosen
 
-    totals = []
-    maxima = []
     for c in range(kv_local):
         columns = slice(c * pair, c * pair + HEAD_DIM)
         keys = jnp.concatenate(
@@ -268,12 +269,12 @@
             ],
             axis=0,
         )
-        own = by_seat(score(keys, halves(queries[c], query_lower, 1)))
-        own = jnp.where(visible, own * scale, NEG_FILL)
-        top = jnp.maximum(tops[c], fold_rows(own, jnp.max))
-        maxima.append(jnp.max(top, axis=0, keepdims=True))
-        exps = jnp.where(visible, jnp.exp(own - maxima[c]), 0.0)
-        totals.append(fold_rows(exps, jnp.sum))
+        own = jnp.where(visible, by_seat(score(halves(queries[c]), keys)) * scale, NEG_FILL)
+        top = jnp.max(jnp.maximum(tops[c], own), axis=1, keepdims=True)
+        top = jnp.broadcast_to(top, own.shape)
+        tops[c] = top
+        exps = jnp.where(visible, jnp.exp(own - top), 0.0)
+        totals[c] = exps
         columns = slice(c * pair + HEAD_DIM, (c + 1) * pair)
         values = jnp.concatenate(
             [
@@ -282,23 +283,23 @@
             ],
             axis=1,
         )
-        mixed_ref[c] = by_seat(mix(values, halves(exps, lower, 0)))
-
-    def mix_chunk(j, totals):
+        mixed_ref[c] = by_seat(mix(halves(exps), values))
+
+    def mix_chunk(j, carry):
         part = pl.ds(pl.multiple_of(j * chunk, chunk), chunk)
-        grew = []
         for c in range(kv_local):
-            exps = jnp.exp(scores[c, part] - maxima[c])
-            grew.append(totals[c] + fold_rows(exps, jnp.sum))
+            top = jnp.concatenate([tops[c]] * (chunk // HEAD_DIM), axis=1)
+            exps = jnp.exp(scores[c, j] - top)
+            totals[c] = fold_lanes(exps, jnp.add, totals[c])
             mixed_ref[c] += mix(
-                prompt[part, c * pair + HEAD_DIM : (c + 1) * pair], exps.astype(jnp.bfloat16)
+                exps.astype(jnp.bfloat16), prompt[part, c * pair + HEAD_DIM : (c + 1) * pair]
             )
-        return tuple(grew)
-
-    totals = lax.fori_loop(0, chunks, mix_chunk, tuple(totals))
+        return carry
+
+    lax.fori_loop(0, chunks, mix_chunk, 0)
     weighted = jnp.zeros((base, HEAD_DIM), jnp.float32)
     for c in range(kv_local):
-        mixed = (mixed_ref[c] / jnp.sum(totals[c], axis=0, keepdims=True)).T
+        mixed = mixed_ref[c] / jnp.sum(totals[c], axis=1, keepdims=True)
         for h in range(group):
             weighted = (
                 weighted + mixed[h * base : (h + 1) * base] * head_ref[c * group + h][None, :]
@@ -319,13 +320,13 @@
     rows = gen_cache.shape[1]
     kv_local = kv_width // (2 * HEAD_DIM)
     group = width // (kv_local * HEAD_DIM)
-    lanes = steps * per_dev * group
+    score_rows = steps * per_dev * group
     chunk = min(KEY_CHUNK, keys)
     head_weights = twist_vector.reshape(kv_local * group, HEAD_DIM)
     smem = pl.BlockSpec(memory_space=pltpu.SMEM)
     vmem = pl.BlockSpec(memory_space=pltpu.VMEM)
     hbm = pl.BlockSpec(memory_space=pltpu.HBM)
-    score_count = lanes * kv_local * (keys + rows)
+    score_count = score_rows * kv_local * (keys + rows)
     return pl.pallas_call(
         functools.partial(attend_kernel, per_dev, group, kv_local, chunk),
         out_shape=[
@@ -338,8 +339,10 @@
             pltpu.VMEM(prompt_kv.shape, jnp.bfloat16),
             pltpu.VMEM(gen_cache.shape, jnp.bfloat16),
             pltpu.VMEM((steps * per_dev, kv_width), jnp.float32),
-            pltpu.VMEM((kv_local, keys, lanes), jnp.float32),
-            pltpu.VMEM((kv_local, HEAD_DIM, lanes), jnp.float32),
+            pltpu.VMEM((kv_local, keys // chunk, score_rows, chunk), jnp.float32),
+            pltpu.VMEM((kv_local, score_rows, HEAD_DIM), jnp.float32),
+            pltpu.VMEM((kv_local, score_rows, HEAD_DIM), jnp.float32),
+            pltpu.VMEM((kv_local, score_rows, HEAD_DIM), jnp.float32),
             pltpu.SemaphoreType.DMA((keys // chunk,)),
             pltpu.SemaphoreType.DMA((per_dev,)),
             pltpu.SemaphoreType.DMA((per_dev,)),

time: 49.8 us -> 49.4 us (level)
  starting transfers between devices: 11.6 us -> 12.4 us
  Pallas kernels: 21.9 us -> 21.1 us
    ppermute x4, starting transfers between devices: 11.6 us -> 12.4 us  [local(): lax.ppermute(send, everyone, routes(doms, tps, steps))]
    pallas_call x1, Pallas kernels: 4.31 us -> 3.77 us  [pack(): pl.pallas_call(functools.partial(pack_kernel, per_dev, doms, step_pairs),...]
where the time goes in v3:
time: 49.4 us; the launch traced here: 49.2 us
  Pallas kernels  21.1 us (43%)
  blocking collectives  13.8 us (28%)
  starting transfers between devices  12.4 us (25%)
  local copies, waits for them, and re-layouts  0.99 us (2%)
  between operations  0.77 us (2%)
    pallas_call x1, Pallas kernels, attend(): pl.pallas_call(functools.partial(attend_kernel, per_dev, group, kv_local,...  14.6 us
    all_to_all x1, blocking collectives, local(): shares = lax.all_to_all(shares, everyone, 0, 0, tiled=True)  13.8 us
    ppermute x4, starting transfers between devices, local(): lax.ppermute(send, everyone, routes(doms, tps, steps))  12.4 us
    pallas_call x1, Pallas kernels, pack(): pl.pallas_call(functools.partial(pack_kernel, per_dev, doms, step_pairs),...  3.77 us
    pallas_call x1, Pallas kernels, finish(): pl.pallas_call(functools.partial(finish_kernel, doms, tps), out_shape=[ja...  2.76 us
  transfers between devices with their start and end apart: 4, of which 0 were waited for; matrix products, arithmetic and copies ran while one was open for 2% of the time, Pallas kernels for 30%

profile of v3, /device:TPU:0, one launch (start us, length us, event | category | flops | bytes accessed | tf_op | source)
XLA Modules:
  0.0 49.2 jit_solution(1769633688454315051)
XLA Ops:
  0.6 0.0 copy-start
  0.6 0.0 copy-start.1
  0.7 0.0 copy-start.4
  0.7 0.0 copy-start.5
  0.7 0.0 copy-start.3
  0.7 0.0 copy-start.2
  0.7 3.8 %pack_sends.1 = (bf16[2,128,1024]{2,1,0:T(8,128)(2,1)}, bf16[2,128,1024]{2,1,0:T(8,128)(2,1)}, bf16[2,128,1024]{2,1,0:T(8,128)(2,1)}, bf16[2,128,1024]{2,1,0:T(8...) custom-call(s32[256]{0:T(256)} %len_hbm.1, s32[256]{0:T(256)} %anc_hbm.1, ...), custom_call_target="tpu_custom_call" | custom-call | bytes 4194304 | tf_op jit(solution)/shard_map/pack_sends/pallas_call | solution.py:110
  4.5 1.3 %collective-permute-start = (bf16[2,128,1024]{2,1,0:T(8,128)(2,1)}, bf16[2,128,1024]{2,1,0:T(8,128)(2,1)S(1)}, u32[]{:S(2)}, u32[]{:S(2)}) collective-permute-start(bf16[2,128,1024]{2,1,0:T(8,128)(2,1)} %get-tuple-element.18), channel_id=1, source_target_pairs={{1,3},{3,5},{4,0},{5,7},{6,2},{7,9},{8,4},{9,11},{10,6},{11,13},{1... | collective-permute-start | bytes 1572872 | tf_op jit(solution)/shard_map/ppermute | solution.py:459
  5.8 5.7 %collective-permute-start.1 = (bf16[2,128,1024]{2,1,0:T(8,128)(2,1)}, bf16[2,128,1024]{2,1,0:T(8,128)(2,1)S(1)}, u32[]{:S(2)}, u32[]{:S(2)}) collective-permute-start(bf16[2,128,1024]{2,1,0:T(8,128)(2,1)} %get-tuple-element.19), channel_id=1, source_target_pairs={{0,4},{2,6},{3,1},{4,8},{5,3},{6,10},{7,5},{8,12},{9,7},{10,14},{1... | collective-permute-start | bytes 1572872 | tf_op jit(solution)/shard_map/ppermute | solution.py:459
  11.5 4.1 %collective-permute-start.2 = (bf16[2,128,1024]{2,1,0:T(8,128)(2,1)}, bf16[2,128,1024]{2,1,0:T(8,128)(2,1)S(1)}, u32[]{:S(2)}, u32[]{:S(2)}) collective-permute-start(bf16[2,128,1024]{2,1,0:T(8,128)(2,1)} %get-tuple-element.20), channel_id=1, source_target_pairs={{0,2},{2,4},{4,6},{5,1},{6,8},{7,3},{8,10},{9,5},{10,12},{11,7},{1... | collective-permute-start | bytes 1572872 | tf_op jit(solution)/shard_map/ppermute | solution.py:459
  15.6 1.3 %collective-permute-start.3 = (bf16[2,128,1024]{2,1,0:T(8,128)(2,1)S(1)}, bf16[2,128,1024]{2,1,0:T(8,128)(2,1)S(1)}, u32[]{:S(2)}, u32[]{:S(2)}) collective-permute-start(bf16[2,128,1024]{2,1,0:T(8,128)(2,1)S(1)} %get-tuple-element.21), channel_id=1, source_target_pairs={{1,5},{2,0},{3,7},{4,2},{5,9},{6,4},{7,11},{8,6},{9,13},{10,8},{11... | collective-permute-start | bytes 1572872 | tf_op jit(solution)/shard_map/ppermute | solution.py:459
  16.9 0.0 copy-done.4
  16.9 0.1 reshape.28
  17.0 0.0 copy-done
  17.0 0.7 %gather_fusion = f32[32]{0:T(128)S(1)} fusion(f32[128256]{0:T(1024)S(1)} %copy-done, s32[1024]{0:T(1024)S(1)} %pad_clamp_fusion), kind=kCustom, calls=%fused_computation | custom fusion | bytes 384 | tf_op jit(solution)/shard_map/jit(_take)/gather | solution.py:463
  17.7 0.1 reshape.27
  17.8 0.1 select_n.24
  17.9 0.0 copy-done.5
  17.9 0.1 broadcast_select_fusion
  18.0 0.0 copy-done.1
  18.0 0.0 copy-done.3
  18.0 0.0 copy-done.2
  18.0 14.6 %attend.1 = (f32[32,1,128]{2,1,0:T(1,128)S(1)}, bf16[16,128,1024]{2,1,0:T(8,128)(2,1)}) custom-call(s32[16]{0:T(128)S(1)} %get-tuple-element.22.len_ref, s32[16]{0:T(128)S(1)} %get-tuple-element.23.anc_ref, bf16[2,16,4096]{2,1,0:T(8,128)(2,1)S(1)} %copy-done.2, bf16[4096,1024]{1,0:T(8,128)(2,1)} %prompt_hbm.1, bf16[16,128,1024]{2,1,0:T(8,128)(2,1)} %gen_hbm.3, ...), custom_call_target="tpu_custom_call" | custom-call | flops 2214592512 | bytes 16777216 | tf_op jit(solution)/shard_map/attend/pallas_call | solution.py:330
  32.6 13.8 %all_to_all.5.refs_5_ = f32[32,1,128]{2,1,0:T(1,128)S(1)} all-to-all(f32[32,1,128]{2,1,0:T(1,128)S(1)} %get-tuple-element.25), channel_id=1, replica_groups=mesh['dom'=16,'tp'=2] {'dom','tp'}, dimensions={0} | all-to-all | bytes 32768 | tf_op jit(solution)/shard_map/all_to_all | solution.py:478
  46.4 0.0 collective-permute-done.refs_0_
  46.4 0.0 collective-permute-done.1.refs_1_
  46.4 0.0 collective-permute-done.2.refs_2_
  46.4 0.0 collective-permute-done.3.refs_3_
  46.4 2.8 %finish.1 = (bf16[16,128,1024]{2,1,0:T(8,128)(2,1)}, f32[2,16]{1,0:T(2,128)}, f32[1,16]{1,0:T(1,128)}) custom-call(s32[16]{0:T(128)S(1)} %get-tuple-element.17.slot_ref, bf16[2,128,1024]{2,1,0:T(8,128)(2,1)S(1)} %collective-permute-done.refs_0_, bf16[2,128,1024]{2,1,0:T(8,128)(2,1)S(1)} %collective-permute-done.1.refs_1_, ...), custom_call_target="tpu_custom_call", output_to_operand_aliasing={{0}: (5, {})} | custom-call | bytes 2097152 | tf_op jit(solution)/shard_map/finish/pallas_call | solution.py:406
  (4 shorter events, 0.0 us)
Async XLA Ops:
  0.6 16.4 %copy-start = (f32[128256]{0:T(1024)S(1)}, f32[128256]{0:T(1024)}, u32[]{:S(2)}) copy-start(f32[128256]{0:T(1024)} %param.18) | copy-start | bytes 1539076
  0.6 17.3 %copy-start.1 = (bf16[2,16,1024]{2,1,0:T(8,128)(2,1)S(1)}, bf16[2,16,1024]{2,1,0:T(8,128)(2,1)}, u32[]{:S(2)}) copy-start(bf16[2,16,1024]{2,1,0:T(8,128)(2,1)} %new_ref.1) | copy-start | bytes 196612
  0.7 16.2 %copy-start.4 = (s32[2,16]{1,0:T(2,128)S(1)}, s32[2,16]{1,0:T(2,128)}, u32[]{:S(2)}) copy-start(s32[2,16]{1,0:T(2,128)} %param.16) | copy-start | bytes 388
  0.7 17.2 %copy-start.5 = (f32[16]{0:T(128)S(1)}, f32[16]{0:T(128)}, u32[]{:S(2)}) copy-start(f32[16]{0:T(128)} %param.19) | copy-start | bytes 196
  0.7 17.3 %copy-start.3 = (f32[4096]{0:T(1024)S(1)}, f32[4096]{0:T(1024)}, u32[]{:S(2)}) copy-start(f32[4096]{0:T(1024)} %param.17) | copy-start | bytes 49156
  0.7 17.3 %copy-start.2 = (bf16[2,16,4096]{2,1,0:T(8,128)(2,1)S(1)}, bf16[2,16,4096]{2,1,0:T(8,128)(2,1)}, u32[]{:S(2)}) copy-start(bf16[2,16,4096]{2,1,0:T(8,128)(2,1)} %q_ref.1) | copy-start | bytes 786436
  4.5 41.9 %collective-permute-start = (bf16[2,128,1024]{2,1,0:T(8,128)(2,1)}, bf16[2,128,1024]{2,1,0:T(8,128)(2,1)S(1)}, u32[]{:S(2)}, u32[]{:S(2)}) collective-permute-start(bf16[2,128,1024]{2,1,0:T(8,128)(2,1)} %get-tuple-element.18), channel_id=1, source_target_pairs={{1,3},{3,5},{4,0},{5,7},{6,2},{7,9},{8,4},{9,11},{10,6},{11,13},{1... | collective-permute-start | bytes 1572872 | tf_op jit(solution)/shard_map/ppermute | solution.py:459
  5.8 40.6 %collective-permute-start.1 = (bf16[2,128,1024]{2,1,0:T(8,128)(2,1)}, bf16[2,128,1024]{2,1,0:T(8,128)(2,1)S(1)}, u32[]{:S(2)}, u32[]{:S(2)}) collective-permute-start(bf16[2,128,1024]{2,1,0:T(8,128)(2,1)} %get-tuple-element.19), channel_id=1, source_target_pairs={{0,4},{2,6},{3,1},{4,8},{5,3},{6,10},{7,5},{8,12},{9,7},{10,14},{1... | collective-permute-start | bytes 1572872 | tf_op jit(solution)/shard_map/ppermute | solution.py:459
  11.5 35.0 %collective-permute-start.2 = (bf16[2,128,1024]{2,1,0:T(8,128)(2,1)}, bf16[2,128,1024]{2,1,0:T(8,128)(2,1)S(1)}, u32[]{:S(2)}, u32[]{:S(2)}) collective-permute-start(bf16[2,128,1024]{2,1,0:T(8,128)(2,1)} %get-tuple-element.20), channel_id=1, source_target_pairs={{0,2},{2,4},{4,6},{5,1},{6,8},{7,3},{8,10},{9,5},{10,12},{11,7},{1... | collective-permute-start | bytes 1572872 | tf_op jit(solution)/shard_map/ppermute | solution.py:459
  15.6 30.8 %collective-permute-start.3 = (bf16[2,128,1024]{2,1,0:T(8,128)(2,1)S(1)}, bf16[2,128,1024]{2,1,0:T(8,128)(2,1)S(1)}, u32[]{:S(2)}, u32[]{:S(2)}) collective-permute-start(bf16[2,128,1024]{2,1,0:T(8,128)(2,1)S(1)} %get-tuple-element.21), channel_id=1, source_target_pairs={{1,5},{2,0},{3,7},{4,2},{5,9},{6,4},{7,11},{8,6},{9,13},{10,8},{11... | collective-permute-start | bytes 1572872 | tf_op jit(solution)/shard_map/ppermute | solution.py:459

commit v4 on v3

--- a/solution.py
+++ b/solution.py
@@ -12,7 +12,8 @@
 SPAN = 2
 PICKS = 2
 NEG_FILL = -1e30
-KEY_CHUNK = 512
+LOG2_E = math.log2(math.e)
+KEY_CHUNK = 1024
 VMEM_BYTES = 44 * 1024 * 1024
 ROW_TILE = 16
 WINDOW = 2 * ROW_TILE
@@ -84,7 +85,7 @@
         own_anc_ref[j] = anc_ref[me * per_dev + j]
         new_len_ref[j] = len_ref[anc_ref[me * per_dev + j]] + 2
         own_len_ref[j] = len_ref[me * per_dev + j]
-        slot_ref[j] = -1
+        slot_ref[j] = -PICKS
     for k, (even_step, odd_step) in enumerate(step_pairs):
         source = me - jnp.where(odd == 1, odd_step, even_step)
         low, _ = named_range(anc_ref, me * per_dev, source, per_dev)
@@ -145,9 +146,11 @@
     q_ref,
     prompt_hbm,
     gen_hbm,
+    token_ref,
+    bias_hbm,
     new_ref,
     head_ref,
-    extra_ref,
+    prior_ref,
     share_ref,
     out_hbm,
     prompt,
@@ -157,16 +160,19 @@
     tops,
     totals,
     mixed_ref,
+    bias_rows,
+    extra,
     prompt_sem,
     gen_sem,
     out_sem,
+    bias_sem,
 ):
     me = lax.axis_index("dom")
     steps = q_ref.shape[0]
     rows, width = grown.shape[1:]
     chunks = prompt.shape[0] // chunk
     pair = 2 * HEAD_DIM
-    scale = 1.0 / math.sqrt(HEAD_DIM)
+    scale = LOG2_E / math.sqrt(HEAD_DIM)
     base = steps * per_dev
 
     half = per_dev // 2
@@ -183,6 +189,10 @@
         prompt_load(j).start()
         for i in range(per_chunk):
             gen_load(j * per_chunk + i).start()
+
+    for i in range(base):
+        row = token_ref[i // per_dev, i % per_dev] // HEAD_DIM
+        pltpu.make_async_copy(bias_hbm.at[pl.ds(pl.multiple_of(row * HEAD_DIM, HEAD_DIM), HEAD_DIM)], bias_rows.at[i, 0], bias_sem.at[i]).start()
 
     new_rows[...] = new_ref[...].astype(jnp.float32).reshape(base, width)
     row_ids = lax.broadcasted_iota(jnp.int32, (rows, width), 0)
@@ -219,7 +229,7 @@
         prompt_load(j).wait()
         part = pl.ds(pl.multiple_of(j * chunk, chunk), chunk)
         for c in range(kv_local):
-            block = score(queries[c], prompt[part, c * pair : c * pair + HEAD_DIM]) * scale
+            block = score(queries[c], prompt[part, c * pair : c * pair + HEAD_DIM])
             scores[c, j] = block
             tops[c] = fold_lanes(block, jnp.maximum, tops[c])
         for i in range(per_chunk):
@@ -269,11 +279,11 @@
             ],
             axis=0,
         )
-        own = jnp.where(visible, by_seat(score(halves(queries[c]), keys)) * scale, NEG_FILL)
+        own = jnp.where(visible, by_seat(score(halves(queries[c]), keys)), NEG_FILL)
         top = jnp.max(jnp.maximum(tops[c], own), axis=1, keepdims=True)
         top = jnp.broadcast_to(top, own.shape)
         tops[c] = top
-        exps = jnp.where(visible, jnp.exp(own - top), 0.0)
+        exps = jnp.where(visible, jnp.exp2((own - top) * scale), 0.0)
         totals[c] = exps
         columns = slice(c * pair + HEAD_DIM, (c + 1) * pair)
         values = jnp.concatenate(
@@ -289,7 +299,7 @@
         part = pl.ds(pl.multiple_of(j * chunk, chunk), chunk)
         for c in range(kv_local):
             top = jnp.concatenate([tops[c]] * (chunk // HEAD_DIM), axis=1)
-            exps = jnp.exp(scores[c, j] - top)
+            exps = jnp.exp2((scores[c, j] - top) * scale)
             totals[c] = fold_lanes(exps, jnp.add, totals[c])
             mixed_ref[c] += mix(
                 exps.astype(jnp.bfloat16), prompt[part, c * pair + HEAD_DIM : (c + 1) * pair]
@@ -304,16 +314,37 @@
             weighted = (
                 weighted + mixed[h * base : (h + 1) * base] * head_ref[c * group + h][None, :]
             )
+    row_ids = lax.broadcasted_iota(jnp.int32, (base, HEAD_DIM), 0)
+    column = jnp.full((base, HEAD_DIM), -1, jnp.int32)
+    for i in range(base):
+        pltpu.make_async_copy(bias_hbm.at[pl.ds(0, HEAD_DIM)], bias_rows.at[i, 0], bias_sem.at[i]).wait()
+        column = jnp.where(row_ids == i, token_ref[i // per_dev, i % per_dev] % HEAD_DIM, column)
+    adds = lax.axis_index("tp") == 0
+    lane_ids = lax.broadcasted_iota(jnp.int32, (base, HEAD_DIM), 1)
+    bias = jnp.where(lane_ids == column, bias_rows[...].reshape(base, HEAD_DIM), 0.0)
+    weighted = weighted + jnp.where(adds, bias, 0.0)
+    extra[...] = jnp.zeros(extra.shape, jnp.float32)
+    extra[:, base : base + per_dev] = jnp.where(adds, prior_ref[...], 0.0)
     padding = jnp.zeros((HEAD_DIM - base, HEAD_DIM), jnp.float32)
     square = jnp.concatenate([weighted, padding], axis=0)
-    row = jnp.sum(square.T, axis=0, keepdims=True) + extra_ref[...]
+    row = jnp.sum(square.T, axis=0, keepdims=True) + extra[...]
     share_ref[...] = jnp.broadcast_to(row[None], share_ref.shape)
     for home, copy in homes:
         pl.when(home)(copy.wait)
 
 
 def attend(
-    own_lengths, own_ancestors, queries, prompt_kv, gen_cache, new_kv, twist_vector, extra, devices
+    own_lengths,
+    own_ancestors,
+    queries,
+    prompt_kv,
+    gen_cache,
+    tokens,
+    twist_bias,
+    new_kv,
+    twist_vector,
+    prior_weights,
+    devices,
 ):
     steps, per_dev, width = queries.shape
     keys, kv_width = prompt_kv.shape
@@ -333,7 +364,7 @@
             jax.ShapeDtypeStruct((devices, 1, HEAD_DIM), jnp.float32),
             jax.ShapeDtypeStruct(gen_cache.shape, jnp.bfloat16),
         ],
-        in_specs=[smem, smem, vmem, hbm, hbm, vmem, vmem, vmem],
+        in_specs=[smem, smem, vmem, hbm, hbm, smem, hbm, vmem, vmem, vmem],
         out_specs=[vmem, hbm],
         scratch_shapes=[
             pltpu.VMEM(prompt_kv.shape, jnp.bfloat16),
@@ -343,9 +374,12 @@
             pltpu.VMEM((kv_local, score_rows, HEAD_DIM), jnp.float32),
             pltpu.VMEM((kv_local, score_rows, HEAD_DIM), jnp.float32),
             pltpu.VMEM((kv_local, score_rows, HEAD_DIM), jnp.float32),
+            pltpu.VMEM((steps * per_dev, 1, HEAD_DIM), jnp.float32),
+            pltpu.VMEM((1, HEAD_DIM), jnp.float32),
             pltpu.SemaphoreType.DMA((keys // chunk,)),
             pltpu.SemaphoreType.DMA((per_dev,)),
             pltpu.SemaphoreType.DMA((per_dev,)),
+            pltpu.SemaphoreType.DMA((steps * per_dev,)),
         ],
         compiler_params=pltpu.CompilerParams(vmem_limit_bytes=VMEM_BYTES),
         cost_estimate=pl.CostEstimate(
@@ -360,9 +394,11 @@
         queries,
         in_hbm(prompt_kv),
         in_hbm(gen_cache),
+        tokens,
+        in_hbm(twist_bias),
         new_kv,
         head_weights,
-        extra,
+        prior_weights[None],
     )
 
 
@@ -373,9 +409,8 @@
     for p in range(per_dev):
         slot = slot_ref[p]
         for k, got in enumerate(gots):
-            for i in range(PICKS):
-                copy = pltpu.make_async_copy(got.at[i], out_ref.at[p], sem.at[p])
-                pl.when(slot == k * PICKS + i)(copy.start)
+            copy = pltpu.make_async_copy(got.at[slot % PICKS], out_ref.at[p], sem.at[p])
+            pl.when(slot // PICKS == k)(copy.start)
     for d in range(doms):
         row = all_ref[d * tps]
         for t in range(1, tps):
@@ -460,19 +495,17 @@
         for send, steps in zip(sends, step_pairs)
     ]
 
-    bias = jnp.take(twist_bias, tokens, axis=0).reshape(-1)
-    extra = jnp.concatenate([bias, prior_weights])
-    extra = jnp.where(lax.axis_index("tp") == 0, extra, 0.0)
-    extra = jnp.pad(extra, (0, HEAD_DIM - extra.size))[None]
     shares, resampled = attend(
         own_lengths,
         own_ancestors,
         queries,
         prompt_kv,
         gen_cache,
+        tokens,
+        twist_bias,
         new_kv,
         twist_vector,
-        extra,
+        prior_weights,
         doms * tps,
     )
     shares = lax.all_to_all(shares, everyone, 0, 0, tiled=True)

time: 49.4 us -> 48 us (0.972)
  local copies, waits for them, and re-layouts: 0.99 us -> 0.02 us
    gather x2 -> x0, local copies, waits for them, and re-layouts: 0.78 us -> none  [local(): bias = jnp.take(twist_bias, tokens, axis=0).reshape(-1)]
  transfers between devices with their start and end apart: 4 -> 4, of which waited for: 0 -> 0; matrix products, arithmetic and copies ran while one was open for 2% -> 0% of each run, Pallas kernels for 30% -> 31%
where the time goes in v4:
time: 48 us; the launch traced here: 47.8 us
  Pallas kernels  20.8 us (43%)
  blocking collectives  14.1 us (29%)
  starting transfers between devices  12 us (25%)
  between operations  0.77 us (2%)
    pallas_call x1, Pallas kernels, attend(): pl.pallas_call(functools.partial(attend_kernel, per_dev, group, kv_local,...  14.8 us
    all_to_all x1, blocking collectives, local(): shares = lax.all_to_all(shares, everyone, 0, 0, tiled=True)  14.1 us
    ppermute x4, starting transfers between devices, local(): lax.ppermute(send, everyone, routes(doms, tps, steps))  12 us
    pallas_call x1, Pallas kernels, pack(): pl.pallas_call(functools.partial(pack_kernel, per_dev, doms, step_pairs),...  3.32 us
    pallas_call x1, Pallas kernels, finish(): pl.pallas_call(functools.partial(finish_kernel, doms, tps), out_shape=[ja...  2.67 us
  transfers between devices with their start and end apart: 4, of which 0 were waited for; matrix products, arithmetic and copies ran while one was open for 0% of the time, Pallas kernels for 31%

profile of v4, /device:TPU:0, one launch (start us, length us, event | category | flops | bytes accessed | tf_op | source)
XLA Modules:
  0.0 47.8 jit_solution(13016072688123916614)
XLA Ops:
  0.6 0.0 copy-start
  0.6 0.0 copy-start.4
  0.7 0.0 copy-start.2
  0.7 0.0 copy-start.3
  0.7 0.0 copy-start.1
  0.7 3.3 %pack_sends.1 = (bf16[2,128,1024]{2,1,0:T(8,128)(2,1)S(1)}, bf16[2,128,1024]{2,1,0:T(8,128)(2,1)S(1)}, bf16[2,128,1024]{2,1,0:T(8,128)(2,1)S(1)}, bf16[2,128,102...) custom-call(s32[256]{0:T(256)} %len_hbm.1, s32[256]{0:T(256)} %anc_hbm.1, ...), custom_call_target="tpu_custom_call" | custom-call | bytes 4194304 | tf_op jit(solution)/shard_map/pack_sends/pallas_call | solution.py:111
  4.0 1.3 %collective-permute-start = (bf16[2,128,1024]{2,1,0:T(8,128)(2,1)S(1)}, bf16[2,128,1024]{2,1,0:T(8,128)(2,1)S(1)}, u32[]{:S(2)}, u32[]{:S(2)}) collective-permute-start(bf16[2,128,1024]{2,1,0:T(8,128)(2,1)S(1)} %get-tuple-element.18), channel_id=1, source_target_pairs={{1,3},{3,5},{4,0},{5,7},{6,2},{7,9},{8,4},{9,11},{10,6},{11,13},{1... | collective-permute-start | bytes 1572872 | tf_op jit(solution)/shard_map/ppermute | solution.py:494
  5.3 5.8 %collective-permute-start.1 = (bf16[2,128,1024]{2,1,0:T(8,128)(2,1)S(1)}, bf16[2,128,1024]{2,1,0:T(8,128)(2,1)S(1)}, u32[]{:S(2)}, u32[]{:S(2)}) collective-permute-start(bf16[2,128,1024]{2,1,0:T(8,128)(2,1)S(1)} %get-tuple-element.19), channel_id=1, source_target_pairs={{0,4},{2,6},{3,1},{4,8},{5,3},{6,10},{7,5},{8,12},{9,7},{10,14},{1... | collective-permute-start | bytes 1572872 | tf_op jit(solution)/shard_map/ppermute | solution.py:494
  11.2 3.6 %collective-permute-start.2 = (bf16[2,128,1024]{2,1,0:T(8,128)(2,1)S(1)}, bf16[2,128,1024]{2,1,0:T(8,128)(2,1)S(1)}, u32[]{:S(2)}, u32[]{:S(2)}) collective-permute-start(bf16[2,128,1024]{2,1,0:T(8,128)(2,1)S(1)} %get-tuple-element.20), channel_id=1, source_target_pairs={{0,2},{2,4},{4,6},{5,1},{6,8},{7,3},{8,10},{9,5},{10,12},{11,7},{1... | collective-permute-start | bytes 1572872 | tf_op jit(solution)/shard_map/ppermute | solution.py:494
  14.8 1.3 %collective-permute-start.3 = (bf16[2,128,1024]{2,1,0:T(8,128)(2,1)S(1)}, bf16[2,128,1024]{2,1,0:T(8,128)(2,1)S(1)}, u32[]{:S(2)}, u32[]{:S(2)}) collective-permute-start(bf16[2,128,1024]{2,1,0:T(8,128)(2,1)S(1)} %get-tuple-element.21), channel_id=1, source_target_pairs={{1,5},{2,0},{3,7},{4,2},{5,9},{6,4},{7,11},{8,6},{9,13},{10,8},{11... | collective-permute-start | bytes 1572872 | tf_op jit(solution)/shard_map/ppermute | solution.py:494
  16.1 0.0 copy-done
  16.1 0.0 copy-done.4
  16.1 0.0 copy-done.2
  16.1 0.0 copy-done.3
  16.1 0.0 copy-done.1
  16.1 14.8 %attend.1 = (f32[32,1,128]{2,1,0:T(1,128)S(1)}, bf16[16,128,1024]{2,1,0:T(8,128)(2,1)}) custom-call(s32[16]{0:T(128)S(1)} %get-tuple-element.22.len_ref, s32[16]{0:T(128)S(1)} %get-tuple-element.23.anc_ref, bf16[2,16,4096]{2,1,0:T(8,128)(2,1)S(1)} %copy-done.1, bf16[4096,1024]{1,0:T(8,128)(2,1)} %prompt_hbm.1, bf16[16,128,1024]{2,1,0:T(8,128)(2,1)} %gen_hbm.3, ...), custom_call_target="tpu_custom_call" | custom-call | flops 2214592512 | bytes 16777216 | tf_op jit(solution)/shard_map/attend/pallas_call | solution.py:361
  31.0 14.1 %all_to_all.5.refs_5_ = f32[32,1,128]{2,1,0:T(1,128)S(1)} all-to-all(f32[32,1,128]{2,1,0:T(1,128)S(1)} %get-tuple-element.25), channel_id=1, replica_groups=mesh['dom'=16,'tp'=2] {'dom','tp'}, dimensions={0} | all-to-all | bytes 32768 | tf_op jit(solution)/shard_map/all_to_all | solution.py:511
  45.1 0.0 collective-permute-done.refs_0_
  45.1 0.0 collective-permute-done.1.refs_1_
  45.1 0.0 collective-permute-done.2.refs_2_
  45.1 0.0 collective-permute-done.3.refs_3_
  45.1 2.7 %finish.1 = (bf16[16,128,1024]{2,1,0:T(8,128)(2,1)}, f32[2,16]{1,0:T(2,128)}, f32[1,16]{1,0:T(1,128)}) custom-call(s32[16]{0:T(128)S(1)} %get-tuple-element.17.slot_ref, bf16[2,128,1024]{2,1,0:T(8,128)(2,1)S(1)} %collective-permute-done.refs_0_, bf16[2,128,1024]{2,1,0:T(8,128)(2,1)S(1)} %collective-permute-done.1.refs_1_, ...), custom_call_target="tpu_custom_call", output_to_operand_aliasing={{0}: (5, {})} | custom-call | bytes 2097152 | tf_op jit(solution)/shard_map/finish/pallas_call | solution.py:441
Async XLA Ops:
  0.6 15.4 %copy-start = (bf16[2,16,1024]{2,1,0:T(8,128)(2,1)S(1)}, bf16[2,16,1024]{2,1,0:T(8,128)(2,1)}, u32[]{:S(2)}) copy-start(bf16[2,16,1024]{2,1,0:T(8,128)(2,1)} %new_ref.1) | copy-start | bytes 196612
  0.6 15.4 %copy-start.4 = (f32[16]{0:T(128)S(1)}, f32[16]{0:T(128)}, u32[]{:S(2)}) copy-start(f32[16]{0:T(128)} %param.19) | copy-start | bytes 196
  0.7 15.4 %copy-start.2 = (f32[4096]{0:T(1024)S(1)}, f32[4096]{0:T(1024)}, u32[]{:S(2)}) copy-start(f32[4096]{0:T(1024)} %param.17) | copy-start | bytes 49156
  0.7 15.4 %copy-start.3 = (s32[2,16]{1,0:T(2,128)S(1)}, s32[2,16]{1,0:T(2,128)}, u32[]{:S(2)}) copy-start(s32[2,16]{1,0:T(2,128)} %token_ref.1) | copy-start | bytes 388
  0.7 15.4 %copy-start.1 = (bf16[2,16,4096]{2,1,0:T(8,128)(2,1)S(1)}, bf16[2,16,4096]{2,1,0:T(8,128)(2,1)}, u32[]{:S(2)}) copy-start(bf16[2,16,4096]{2,1,0:T(8,128)(2,1)} %q_ref.1) | copy-start | bytes 786436
  4.0 41.1 %collective-permute-start = (bf16[2,128,1024]{2,1,0:T(8,128)(2,1)S(1)}, bf16[2,128,1024]{2,1,0:T(8,128)(2,1)S(1)}, u32[]{:S(2)}, u32[]{:S(2)}) collective-permute-start(bf16[2,128,1024]{2,1,0:T(8,128)(2,1)S(1)} %get-tuple-element.18), channel_id=1, source_target_pairs={{1,3},{3,5},{4,0},{5,7},{6,2},{7,9},{8,4},{9,11},{10,6},{11,13},{1... | collective-permute-start | bytes 1572872 | tf_op jit(solution)/shard_map/ppermute | solution.py:494
  5.3 39.8 %collective-permute-start.1 = (bf16[2,128,1024]{2,1,0:T(8,128)(2,1)S(1)}, bf16[2,128,1024]{2,1,0:T(8,128)(2,1)S(1)}, u32[]{:S(2)}, u32[]{:S(2)}) collective-permute-start(bf16[2,128,1024]{2,1,0:T(8,128)(2,1)S(1)} %get-tuple-element.19), channel_id=1, source_target_pairs={{0,4},{2,6},{3,1},{4,8},{5,3},{6,10},{7,5},{8,12},{9,7},{10,14},{1... | collective-permute-start | bytes 1572872 | tf_op jit(solution)/shard_map/ppermute | solution.py:494
  11.2 33.9 %collective-permute-start.2 = (bf16[2,128,1024]{2,1,0:T(8,128)(2,1)S(1)}, bf16[2,128,1024]{2,1,0:T(8,128)(2,1)S(1)}, u32[]{:S(2)}, u32[]{:S(2)}) collective-permute-start(bf16[2,128,1024]{2,1,0:T(8,128)(2,1)S(1)} %get-tuple-element.20), channel_id=1, source_target_pairs={{0,2},{2,4},{4,6},{5,1},{6,8},{7,3},{8,10},{9,5},{10,12},{11,7},{1... | collective-permute-start | bytes 1572872 | tf_op jit(solution)/shard_map/ppermute | solution.py:494
  14.8 30.3 %collective-permute-start.3 = (bf16[2,128,1024]{2,1,0:T(8,128)(2,1)S(1)}, bf16[2,128,1024]{2,1,0:T(8,128)(2,1)S(1)}, u32[]{:S(2)}, u32[]{:S(2)}) collective-permute-start(bf16[2,128,1024]{2,1,0:T(8,128)(2,1)S(1)} %get-tuple-element.21), channel_id=1, source_target_pairs={{1,5},{2,0},{3,7},{4,2},{5,9},{6,4},{7,11},{8,6},{9,13},{10,8},{11... | collective-permute-start | bytes 1572872 | tf_op jit(solution)/shard_map/ppermute | solution.py:494

commit v5 on v4

--- a/solution.py
+++ b/solution.py
@@ -11,6 +11,7 @@
 HEAD_DIM = 128
 SPAN = 2
 PICKS = 2
+TABLE_PARTS = 4
 NEG_FILL = -1e30
 LOG2_E = math.log2(math.e)
 KEY_CHUNK = 1024
@@ -58,8 +59,10 @@
 
 def pack_kernel(per_dev, doms, step_pairs, len_hbm, anc_hbm, new_hbm, gen_hbm, *refs):
     sends = refs[: len(step_pairs)]
-    new_len_ref, own_len_ref, own_anc_ref, slot_ref = refs[len(step_pairs) : len(step_pairs) + 4]
-    len_ref, anc_ref, new_bf16, new_rows, list_sem, load_sem = refs[len(step_pairs) + 4 :]
+    table_hbm, table, len_ref, anc_ref, new_bf16, new_rows, list_sem, load_sem = refs[
+        len(step_pairs) :
+    ]
+    new_at, own_at, anc_at, slot_at = (k * per_dev for k in range(TABLE_PARTS))
     lists = [
         pltpu.make_async_copy(anc_hbm, anc_ref, list_sem.at[0]),
         pltpu.make_async_copy(len_hbm, len_ref, list_sem.at[1]),
@@ -82,10 +85,10 @@
             loads.append(load)
     lists[1].wait()
     for j in range(per_dev):
-        own_anc_ref[j] = anc_ref[me * per_dev + j]
-        new_len_ref[j] = len_ref[anc_ref[me * per_dev + j]] + 2
-        own_len_ref[j] = len_ref[me * per_dev + j]
-        slot_ref[j] = -PICKS
+        table[anc_at + j] = anc_ref[me * per_dev + j]
+        table[new_at + j] = len_ref[anc_ref[me * per_dev + j]] + 2
+        table[own_at + j] = len_ref[me * per_dev + j]
+        table[slot_at + j] = -PICKS
     for k, (even_step, odd_step) in enumerate(step_pairs):
         source = me - jnp.where(odd == 1, odd_step, even_step)
         low, _ = named_range(anc_ref, me * per_dev, source, per_dev)
@@ -93,33 +96,36 @@
             local = anc_ref[me * per_dev + j] - source * per_dev
             named = jnp.logical_and(local >= 0, local < per_dev)
             slot = k * PICKS + jnp.where(local == low, 0, PICKS - 1)
-            slot_ref[j] = jnp.where(named, slot, slot_ref[j])
+            table[slot_at + j] = jnp.where(named, slot, table[slot_at + j])
+    table_copy = pltpu.make_async_copy(table, table_hbm, list_sem.at[3])
+    table_copy.start()
     lists[2].wait()
     new_rows[...] = new_bf16[...].astype(jnp.float32).reshape(new_rows.shape)
     for load, (pick, target) in zip(loads, picks):
         load.wait()
         place_new_rows(target, new_rows, len_ref[me * per_dev + pick], pick, per_dev)
+    table_copy.wait()
 
 
 def pack(lengths, ancestors, new_kv, gen_cache, doms, step_pairs):
     per_dev, rows, width = gen_cache.shape
     count = len(step_pairs)
-    smem = pl.BlockSpec(memory_space=pltpu.SMEM)
     vmem = pl.BlockSpec(memory_space=pltpu.VMEM)
     hbm = pl.BlockSpec(memory_space=pltpu.HBM)
     block_bytes = PICKS * rows * width * 2
     return pl.pallas_call(
         functools.partial(pack_kernel, per_dev, doms, step_pairs),
         out_shape=[jax.ShapeDtypeStruct((PICKS, rows, width), jnp.bfloat16)] * count
-        + [jax.ShapeDtypeStruct((per_dev,), jnp.int32)] * 4,
+        + [jax.ShapeDtypeStruct((TABLE_PARTS * per_dev,), jnp.int32)],
         in_specs=[hbm] * 4,
-        out_specs=[vmem] * count + [smem] * 4,
+        out_specs=[vmem] * count + [hbm],
         scratch_shapes=[
+            pltpu.SMEM((TABLE_PARTS * per_dev,), jnp.int32),
             pltpu.SMEM(lengths.shape, jnp.int32),
             pltpu.SMEM(ancestors.shape, jnp.int32),
             pltpu.VMEM(new_kv.shape, jnp.bfloat16),
             pltpu.VMEM((2 * per_dev, width), jnp.float32),
-            pltpu.SemaphoreType.DMA((3,)),
+            pltpu.SemaphoreType.DMA((4,)),
             pltpu.SemaphoreType.DMA((count * PICKS,)),
         ],
         compiler_params=pltpu.CompilerParams(vmem_limit_bytes=VMEM_BYTES),
@@ -141,12 +147,11 @@
     group,
     kv_local,
     chunk,
-    len_ref,
-    anc_ref,
+    table_hbm,
     q_ref,
     prompt_hbm,
     gen_hbm,
-    token_ref,
+    token_hbm,
     bias_hbm,
     new_ref,
     head_ref,
@@ -162,10 +167,13 @@
     mixed_ref,
     bias_rows,
     extra,
+    table,
+    token_ref,
     prompt_sem,
     gen_sem,
     out_sem,
     bias_sem,
+    list_sem,
 ):
     me = lax.axis_index("dom")
     steps = q_ref.shape[0]
@@ -185,11 +193,20 @@
         part = pl.ds(pl.multiple_of(j * chunk, chunk), chunk)
         return pltpu.make_async_copy(prompt_hbm.at[part], prompt.at[part], prompt_sem.at[j])
 
+    lists = [
+        pltpu.make_async_copy(table_hbm, table, list_sem.at[0]),
+        pltpu.make_async_copy(token_hbm, token_ref, list_sem.at[1]),
+    ]
+    for copy in lists:
+        copy.start()
     for j in range(chunks):
         prompt_load(j).start()
         for i in range(per_chunk):
             gen_load(j * per_chunk + i).start()
 
+    for copy in lists:
+        copy.wait()
+    len_ref, anc_ref = (table.at[pl.ds(k * per_dev, per_dev)] for k in (1, 2))
     for i in range(base):
         row = token_ref[i // per_dev, i % per_dev] // HEAD_DIM
         pltpu.make_async_copy(bias_hbm.at[pl.ds(pl.multiple_of(row * HEAD_DIM, HEAD_DIM), HEAD_DIM)], bias_rows.at[i, 0], bias_sem.at[i]).start()
@@ -334,8 +351,7 @@
 
 
 def attend(
-    own_lengths,
-    own_ancestors,
+    table,
     queries,
     prompt_kv,
     gen_cache,
@@ -354,7 +370,6 @@
     score_rows = steps * per_dev * group
     chunk = min(KEY_CHUNK, keys)
     head_weights = twist_vector.reshape(kv_local * group, HEAD_DIM)
-    smem = pl.BlockSpec(memory_space=pltpu.SMEM)
     vmem = pl.BlockSpec(memory_space=pltpu.VMEM)
     hbm = pl.BlockSpec(memory_space=pltpu.HBM)
     score_count = score_rows * kv_local * (keys + rows)
@@ -364,7 +379,7 @@
             jax.ShapeDtypeStruct((devices, 1, HEAD_DIM), jnp.float32),
             jax.ShapeDtypeStruct(gen_cache.shape, jnp.bfloat16),
         ],
-        in_specs=[smem, smem, vmem, hbm, hbm, smem, hbm, vmem, vmem, vmem],
+        in_specs=[hbm, vmem, hbm, hbm, hbm, hbm, vmem, vmem, vmem],
         out_specs=[vmem, hbm],
         scratch_shapes=[
             pltpu.VMEM(prompt_kv.shape, jnp.bfloat16),
@@ -376,10 +391,13 @@
             pltpu.VMEM((kv_local, score_rows, HEAD_DIM), jnp.float32),
             pltpu.VMEM((steps * per_dev, 1, HEAD_DIM), jnp.float32),
             pltpu.VMEM((1, HEAD_DIM), jnp.float32),
+            pltpu.SMEM(table.shape, jnp.int32),
+            pltpu.SMEM(tokens.shape, jnp.int32),
             pltpu.SemaphoreType.DMA((keys // chunk,)),
             pltpu.SemaphoreType.DMA((per_dev,)),
             pltpu.SemaphoreType.DMA((per_dev,)),
             pltpu.SemaphoreType.DMA((steps * per_dev,)),
+            pltpu.SemaphoreType.DMA((2,)),
         ],
         compiler_params=pltpu.CompilerParams(vmem_limit_bytes=VMEM_BYTES),
         cost_estimate=pl.CostEstimate(
@@ -389,12 +407,11 @@
         ),
         name="attend",
     )(
-        own_lengths,
-        own_ancestors,
+        in_hbm(table),
         queries,
         in_hbm(prompt_kv),
         in_hbm(gen_cache),
-        tokens,
+        in_hbm(tokens),
         in_hbm(twist_bias),
         new_kv,
         head_weights,
@@ -402,14 +419,18 @@
     )
 
 
-def finish_kernel(doms, tps, slot_ref, *refs):
+def finish_kernel(doms, tps, table_ref, *refs):
     gots = refs[: len(ORDERS[0])]
-    _, all_ref, out_ref, twist_ref, normal_ref, sums, sem = refs[len(gots) :]
+    _, all_ref, out_ref, twist_hbm, normal_hbm = refs[len(gots) : len(gots) + 5]
+    table, sums, twist, normal, copy_sem, small_sem = refs[len(gots) + 5 :]
     per_dev = out_ref.shape[0]
-    for p in range(per_dev):
-        slot = slot_ref[p]
+    table_copy = pltpu.make_async_copy(table_ref, table, small_sem.at[0])
+    table_copy.start()
+    table_copy.wait()
+    slots = [table[(TABLE_PARTS - 1) * per_dev + p] for p in range(per_dev)]
+    for p, slot in enumerate(slots):
         for k, got in enumerate(gots):
-            copy = pltpu.make_async_copy(got.at[slot % PICKS], out_ref.at[p], sem.at[p])
+            copy = pltpu.make_async_copy(got.at[slot % PICKS], out_ref.at[p], copy_sem.at[p])
             pl.when(slot // PICKS == k)(copy.start)
     for d in range(doms):
         row = all_ref[d * tps]
@@ -425,17 +446,24 @@
     log_total = largest + jnp.log(jnp.sum(jnp.exp(log_weights - largest), keepdims=True))
     mine = sums[pl.ds(lax.axis_index("dom"), 1), :]
     own = mine[:, prior] + mine[:, step_1] - mine[:, step_0]
-    twist_ref[...] = jnp.concatenate([mine[:, step_0], mine[:, step_1]], axis=0)
-    normal_ref[...] = own - log_total
-    for p in range(per_dev):
-        copy = pltpu.make_async_copy(gots[0].at[0], out_ref.at[p], sem.at[p])
-        pl.when(slot_ref[p] >= 0)(copy.wait)
-
-
-def finish(slots, gots, held, shares, doms, tps):
+    twist[...] = jnp.concatenate([mine[:, step_0], mine[:, step_1]], axis=0)
+    normal[...] = own - log_total
+    results = [
+        pltpu.make_async_copy(twist, twist_hbm, small_sem.at[1]),
+        pltpu.make_async_copy(normal, normal_hbm, small_sem.at[2]),
+    ]
+    for copy in results:
+        copy.start()
+    for p, slot in enumerate(slots):
+        copy = pltpu.make_async_copy(gots[0].at[0], out_ref.at[p], copy_sem.at[p])
+        pl.when(slot >= 0)(copy.wait)
+    for copy in results:
+        copy.wait()
+
+
+def finish(table, gots, held, shares, doms, tps):
     per_dev = held.shape[0]
     count = len(gots)
-    smem = pl.BlockSpec(memory_space=pltpu.SMEM)
     vmem = pl.BlockSpec(memory_space=pltpu.VMEM)
     hbm = pl.BlockSpec(memory_space=pl.ANY)
     return pl.pallas_call(
@@ -445,19 +473,23 @@
             jax.ShapeDtypeStruct((2, per_dev), jnp.float32),
             jax.ShapeDtypeStruct((1, per_dev), jnp.float32),
         ],
-        in_specs=[smem] + [vmem] * count + [hbm, vmem],
-        out_specs=[hbm, vmem, vmem],
+        in_specs=[vmem] + [vmem] * count + [hbm, vmem],
+        out_specs=[hbm, hbm, hbm],
         input_output_aliases={1 + count: 0},
         scratch_shapes=[
+            pltpu.SMEM(table.shape, jnp.int32),
             pltpu.VMEM((doms, HEAD_DIM), jnp.float32),
+            pltpu.VMEM((2, per_dev), jnp.float32),
+            pltpu.VMEM((1, per_dev), jnp.float32),
             pltpu.SemaphoreType.DMA((per_dev,)),
+            pltpu.SemaphoreType.DMA((3,)),
         ],
         compiler_params=pltpu.CompilerParams(vmem_limit_bytes=VMEM_BYTES),
         cost_estimate=pl.CostEstimate(
             flops=0, bytes_accessed=held.size, transcendentals=0
         ),
         name="finish",
-    )(slots, *gots, held, shares)
+    )(table, *gots, held, shares)
 
 
 def routes(doms, tps, steps):
@@ -487,7 +519,7 @@
     step_pairs = list(zip(*ORDERS))
     everyone = ("dom", "tp")
 
-    *sends, new_lengths, own_lengths, own_ancestors, slots = pack(
+    *sends, table = pack(
         lengths, ancestors, new_kv, gen_cache, doms, step_pairs
     )
     arrivals = [
@@ -496,8 +528,7 @@
     ]
 
     shares, resampled = attend(
-        own_lengths,
-        own_ancestors,
+        table,
         queries,
         prompt_kv,
         gen_cache,
@@ -509,8 +540,8 @@
         doms * tps,
     )
     shares = lax.all_to_all(shares, everyone, 0, 0, tiled=True)
-    resampled, twist, normalized = finish(slots, arrivals, resampled, shares, doms, tps)
-    return (twist, normalized.reshape(per_dev), resampled, new_lengths)
+    resampled, twist, normalized = finish(table, arrivals, resampled, shares, doms, tps)
+    return (twist, normalized.reshape(per_dev), resampled, table[:per_dev])
 
 
 def solution(mesh):

time: 48 us -> 46.7 us (0.973)
  the two profiles are of different devices: /device:TPU:0 before, /device:TPU:7 now
where the time goes in v5:
time: 46.7 us; the launch traced here: 46.6 us
  Pallas kernels  19.2 us (41%)
  blocking collectives  14.9 us (32%)
  starting transfers between devices  11.7 us (25%)
  between operations  0.77 us (2%)
    all_to_all x1, blocking collectives, local(): shares = lax.all_to_all(shares, everyone, 0, 0, tiled=True)  14.9 us
    pallas_call x1, Pallas kernels, attend(): pl.pallas_call(functools.partial(attend_kernel, per_dev, group, kv_local,...  14 us
    ppermute x4, starting transfers between devices, local(): lax.ppermute(send, everyone, routes(doms, tps, steps))  11.7 us
    pallas_call x1, Pallas kernels, pack(): pl.pallas_call(functools.partial(pack_kernel, per_dev, doms, step_pairs),...  2.62 us
    pallas_call x1, Pallas kernels, finish(): pl.pallas_call(functools.partial(finish_kernel, doms, tps), out_shape=[ja...  2.58 us
  transfers between devices with their start and end apart: 4, of which 0 were waited for; matrix products, arithmetic and copies ran while one was open for 0% of the time, Pallas kernels for 30%

profile of v5, /device:TPU:7, one launch (start us, length us, event | category | flops | bytes accessed | tf_op | source)
XLA Modules:
  0.0 46.6 jit_solution(11038845687115784540)
XLA Ops:
  0.6 0.0 copy-start
  0.6 0.0 copy-start.4
  0.7 0.0 copy-start.2
  0.7 0.0 copy-start.1
  0.7 2.6 %pack_sends.1 = (bf16[2,128,1024]{2,1,0:T(8,128)(2,1)S(1)}, bf16[2,128,1024]{2,1,0:T(8,128)(2,1)S(1)}, bf16[2,128,1024]{2,1,0:T(8,128)(2,1)S(1)}, bf16[2,128,1024]{2,1,0:T(8,128)(2,1)S(1)}, s32[64]{0:T(128)}) custom-call(s32[256]{0:T(256)} %len_hbm.1, s32[256]{0:T(256)} %anc_hbm.1, bf16[2,16,1024]{2,1,0:T(8,128)(2,1)} %new_ref.1, bf16[16,128,1024]{2,1,0:T(8,128)(2,1)} %gen_hbm.3), custom_call_target="tpu_custom_call" | custom-call | bytes 4194304 | tf_op jit(solution)/shard_map/pack_sends/pallas_call | solution.py:116
  3.3 3.6 %collective-permute-start = (bf16[2,128,1024]{2,1,0:T(8,128)(2,1)S(1)}, bf16[2,128,1024]{2,1,0:T(8,128)(2,1)S(1)}, u32[]{:S(2)}, u32[]{:S(2)}) collective-permute-start(bf16[2,128,1024]{2,1,0:T(8,128)(2,1)S(1)} %get-tuple-element.15), channel_id=1, source_target_pairs={{1,3},{3,5},{4,0},{5,7},{6,2},{7,9},{8,4},{9,11},{10,6},{11,13},{1... | collective-permute-start | bytes 1572872 | tf_op jit(solution)/shard_map/ppermute | solution.py:526
  6.9 1.9 %collective-permute-start.1 = (bf16[2,128,1024]{2,1,0:T(8,128)(2,1)S(1)}, bf16[2,128,1024]{2,1,0:T(8,128)(2,1)S(1)}, u32[]{:S(2)}, u32[]{:S(2)}) collective-permute-start(bf16[2,128,1024]{2,1,0:T(8,128)(2,1)S(1)} %get-tuple-element.16), channel_id=1, source_target_pairs={{0,4},{2,6},{3,1},{4,8},{5,3},{6,10},{7,5},{8,12},{9,7},{10,14},{1... | collective-permute-start | bytes 1572872 | tf_op jit(solution)/shard_map/ppermute | solution.py:526
  8.8 2.3 %collective-permute-start.2 = (bf16[2,128,1024]{2,1,0:T(8,128)(2,1)S(1)}, bf16[2,128,1024]{2,1,0:T(8,128)(2,1)S(1)}, u32[]{:S(2)}, u32[]{:S(2)}) collective-permute-start(bf16[2,128,1024]{2,1,0:T(8,128)(2,1)S(1)} %get-tuple-element.17), channel_id=1, source_target_pairs={{0,2},{2,4},{4,6},{5,1},{6,8},{7,3},{8,10},{9,5},{10,12},{11,7},{1... | collective-permute-start | bytes 1572872 | tf_op jit(solution)/shard_map/ppermute | solution.py:526
  11.1 3.9 %collective-permute-start.3 = (bf16[2,128,1024]{2,1,0:T(8,128)(2,1)S(1)}, bf16[2,128,1024]{2,1,0:T(8,128)(2,1)S(1)}, u32[]{:S(2)}, u32[]{:S(2)}) collective-permute-start(bf16[2,128,1024]{2,1,0:T(8,128)(2,1)S(1)} %get-tuple-element.18), channel_id=1, source_target_pairs={{1,5},{2,0},{3,7},{4,2},{5,9},{6,4},{7,11},{8,6},{9,13},{10,8},{11... | collective-permute-start | bytes 1572872 | tf_op jit(solution)/shard_map/ppermute | solution.py:526
  15.0 0.0 copy-done
  15.0 0.0 copy-done.4
  15.0 0.0 copy-done.2
  15.0 0.0 copy-done.1
  15.0 0.0 copy-start.3
  15.1 14.0 %attend.1 = (f32[32,1,128]{2,1,0:T(1,128)S(1)}, bf16[16,128,1024]{2,1,0:T(8,128)(2,1)}) custom-call(s32[64]{0:T(128)} %get-tuple-element.14.table_hbm.table_ref, bf16[2,16,4096]{2,1,0:T(8,128)(2,1)S(1)} %copy-done.1, bf16[4096,1024]{1,0:T(8,128)(2,1)} %prompt_hbm.1, bf16[16,128,1024]{2,1,0:T(8,128)(2,1)} %gen_hbm.3, s32[2,16]{1,0:T(2,128)} %token_hbm.1, ...), custom_call_target="tpu_custom_call" | custom-call | flops 2214592512 | bytes 16777216 | tf_op jit(solution)/shard_map/attend/pallas_call | solution.py:376
  29.1 14.9 %all_to_all.5.refs_5_ = f32[32,1,128]{2,1,0:T(1,128)S(1)} all-to-all(f32[32,1,128]{2,1,0:T(1,128)S(1)} %get-tuple-element.20), channel_id=1, replica_groups=mesh['dom'=16,'tp'=2] {'dom','tp'}, dimensions={0} | all-to-all | bytes 32768 | tf_op jit(solution)/shard_map/all_to_all | solution.py:542
  44.0 0.0 collective-permute-done.refs_0_
  44.0 0.0 collective-permute-done.1.refs_1_
  44.0 0.0 collective-permute-done.2.refs_2_
  44.0 0.0 collective-permute-done.3.refs_3_
  44.0 0.0 copy-done.3
  44.0 2.6 %finish.1 = (bf16[16,128,1024]{2,1,0:T(8,128)(2,1)}, f32[2,16]{1,0:T(2,128)}, f32[1,16]{1,0:T(1,128)}) custom-call(s32[64]{0:T(128)S(1)} %copy-done.3, bf16[2,128,1024]{2,1,0:T(8,128)(2,1)S(1)} %collective-permute-done.refs_0_, bf16[2,128,1024]{2,1,0:T(8,128)(2,1)S(1)} %collective-permute-done.1.refs_1_, ...), custom_call_target="tpu_custom_call", output_to_operand_aliasing={{0}: (5, {})} | custom-call | bytes 2097152 | tf_op jit(solution)/shard_map/finish/pallas_call | solution.py:469
Async XLA Ops:
  0.6 14.4 %copy-start = (bf16[2,16,1024]{2,1,0:T(8,128)(2,1)S(1)}, bf16[2,16,1024]{2,1,0:T(8,128)(2,1)}, u32[]{:S(2)}) copy-start(bf16[2,16,1024]{2,1,0:T(8,128)(2,1)} %new_ref.1) | copy-start | bytes 196612
  0.6 14.4 %copy-start.4 = (f32[16]{0:T(128)S(1)}, f32[16]{0:T(128)}, u32[]{:S(2)}) copy-start(f32[16]{0:T(128)} %param.19) | copy-start | bytes 196
  0.7 14.4 %copy-start.2 = (f32[4096]{0:T(1024)S(1)}, f32[4096]{0:T(1024)}, u32[]{:S(2)}) copy-start(f32[4096]{0:T(1024)} %param.17) | copy-start | bytes 49156
  0.7 14.4 %copy-start.1 = (bf16[2,16,4096]{2,1,0:T(8,128)(2,1)S(1)}, bf16[2,16,4096]{2,1,0:T(8,128)(2,1)}, u32[]{:S(2)}) copy-start(bf16[2,16,4096]{2,1,0:T(8,128)(2,1)} %q_ref.1) | copy-start | bytes 786436
  3.3 40.7 %collective-permute-start = (bf16[2,128,1024]{2,1,0:T(8,128)(2,1)S(1)}, bf16[2,128,1024]{2,1,0:T(8,128)(2,1)S(1)}, u32[]{:S(2)}, u32[]{:S(2)}) collective-permute-start(bf16[2,128,1024]{2,1,0:T(8,128)(2,1)S(1)} %get-tuple-element.15), channel_id=1, source_target_pairs={{1,3},{3,5},{4,0},{5,7},{6,2},{7,9},{8,4},{9,11},{10,6},{11,13},{1... | collective-permute-start | bytes 1572872 | tf_op jit(solution)/shard_map/ppermute | solution.py:526
  6.9 37.1 %collective-permute-start.1 = (bf16[2,128,1024]{2,1,0:T(8,128)(2,1)S(1)}, bf16[2,128,1024]{2,1,0:T(8,128)(2,1)S(1)}, u32[]{:S(2)}, u32[]{:S(2)}) collective-permute-start(bf16[2,128,1024]{2,1,0:T(8,128)(2,1)S(1)} %get-tuple-element.16), channel_id=1, source_target_pairs={{0,4},{2,6},{3,1},{4,8},{5,3},{6,10},{7,5},{8,12},{9,7},{10,14},{1... | collective-permute-start | bytes 1572872 | tf_op jit(solution)/shard_map/ppermute | solution.py:526
  8.8 35.2 %collective-permute-start.2 = (bf16[2,128,1024]{2,1,0:T(8,128)(2,1)S(1)}, bf16[2,128,1024]{2,1,0:T(8,128)(2,1)S(1)}, u32[]{:S(2)}, u32[]{:S(2)}) collective-permute-start(bf16[2,128,1024]{2,1,0:T(8,128)(2,1)S(1)} %get-tuple-element.17), channel_id=1, source_target_pairs={{0,2},{2,4},{4,6},{5,1},{6,8},{7,3},{8,10},{9,5},{10,12},{11,7},{1... | collective-permute-start | bytes 1572872 | tf_op jit(solution)/shard_map/ppermute | solution.py:526
  11.1 32.9 %collective-permute-start.3 = (bf16[2,128,1024]{2,1,0:T(8,128)(2,1)S(1)}, bf16[2,128,1024]{2,1,0:T(8,128)(2,1)S(1)}, u32[]{:S(2)}, u32[]{:S(2)}) collective-permute-start(bf16[2,128,1024]{2,1,0:T(8,128)(2,1)S(1)} %get-tuple-element.18), channel_id=1, source_target_pairs={{1,5},{2,0},{3,7},{4,2},{5,9},{6,4},{7,11},{8,6},{9,13},{10,8},{11... | collective-permute-start | bytes 1572872 | tf_op jit(solution)/shard_map/ppermute | solution.py:526
  15.0 29.0 %copy-start.3 = (s32[64]{0:T(128)S(1)}, s32[64]{0:T(128)}, u32[]{:S(2)}) copy-start(s32[64]{0:T(128)} %get-tuple-element.14.table_hbm.table_ref) | copy-start | bytes 772

commit v6 on v5

--- a/solution.py
+++ b/solution.py
@@ -19,7 +19,7 @@
 ROW_TILE = 16
 WINDOW = 2 * ROW_TILE
 
-ORDERS = ((-2, 2, 1, -1), (1, -1, -2, 2))
+ORDERS = ((-2, 2, 1, -1), (2, -2, -1, 1))
 
 
 def in_hbm(x):

time: 46.7 us -> 46 us (0.985)
  the two profiles are of different devices: /device:TPU:7 before, /device:TPU:0 now
where the time goes in v6:
time: 46 us; the launch traced here: 45.9 us
  Pallas kernels  18.8 us (41%)
  blocking collectives  14.4 us (31%)
  starting transfers between devices  11.9 us (26%)
  between operations  0.77 us (2%)
    all_to_all x1, blocking collectives, local(): shares = lax.all_to_all(shares, everyone, 0, 0, tiled=True)  14.4 us
    pallas_call x1, Pallas kernels, attend(): pl.pallas_call(functools.partial(attend_kernel, per_dev, group, kv_local,...  14 us
    ppermute x4, starting transfers between devices, local(): lax.ppermute(send, everyone, routes(doms, tps, steps))  11.9 us
    pallas_call x1, Pallas kernels, pack(): pl.pallas_call(functools.partial(pack_kernel, per_dev, doms, step_pairs),...  2.74 us
    pallas_call x1, Pallas kernels, finish(): pl.pallas_call(functools.partial(finish_kernel, doms, tps), out_shape=[ja...  2.06 us
  transfers between devices with their start and end apart: 4, of which 0 were waited for; matrix products, arithmetic and copies ran while one was open for 0% of the time, Pallas kernels for 31%

profile of v6, /device:TPU:0, one launch (start us, length us, event | category | flops | bytes accessed | tf_op | source)
XLA Modules:
  0.0 45.9 jit_solution(2633980379457539153)
XLA Ops:
  0.6 0.0 copy-start
  0.6 0.0 copy-start.4
  0.7 0.0 copy-start.2
  0.7 0.0 copy-start.1
  0.7 2.7 %pack_sends.1 = (bf16[2,128,1024]{2,1,0:T(8,128)(2,1)S(1)}, bf16[2,128,1024]{2,1,0:T(8,128)(2,1)S(1)}, bf16[2,128,1024]{2,1,0:T(8,128)(2,1)S(1)}, bf16[2,128,1024]{2,1,0:T(8,128)(2,1)S(1)}, s32[64]{0:T(128)}) custom-call(s32[256]{0:T(256)} %len_hbm.1, s32[256]{0:T(256)} %anc_hbm.1, bf16[2,16,1024]{2,1,0:T(8,128)(2,1)} %new_ref.1, bf16[16,128,1024]{2,1,0:T(8,128)(2,1)} %gen_hbm.3), custom_call_target="tpu_custom_call" | custom-call | bytes 4194304 | tf_op jit(solution)/shard_map/pack_sends/pallas_call | solution.py:116
  3.4 1.3 %collective-permute-start = (bf16[2,128,1024]{2,1,0:T(8,128)(2,1)S(1)}, bf16[2,128,1024]{2,1,0:T(8,128)(2,1)S(1)}, u32[]{:S(2)}, u32[]{:S(2)}) collective-permute-start(bf16[2,128,1024]{2,1,0:T(8,128)(2,1)S(1)} %get-tuple-element.15), channel_id=1, source_target_pairs={{1,5},{3,7},{4,0},{5,9},{6,2},{7,11},{8,4},{9,13},{10,6},{11,15},{... | collective-permute-start | bytes 1572872 | tf_op jit(solution)/shard_map/ppermute | solution.py:526
  4.7 5.7 %collective-permute-start.1 = (bf16[2,128,1024]{2,1,0:T(8,128)(2,1)S(1)}, bf16[2,128,1024]{2,1,0:T(8,128)(2,1)S(1)}, u32[]{:S(2)}, u32[]{:S(2)}) collective-permute-start(bf16[2,128,1024]{2,1,0:T(8,128)(2,1)S(1)} %get-tuple-element.16), channel_id=1, source_target_pairs={{0,4},{2,6},{4,8},{5,1},{6,10},{7,3},{8,12},{9,5},{10,14},{11,7},{... | collective-permute-start | bytes 1572872 | tf_op jit(solution)/shard_map/ppermute | solution.py:526
  10.4 3.6 %collective-permute-start.2 = (bf16[2,128,1024]{2,1,0:T(8,128)(2,1)S(1)}, bf16[2,128,1024]{2,1,0:T(8,128)(2,1)S(1)}, u32[]{:S(2)}, u32[]{:S(2)}) collective-permute-start(bf16[2,128,1024]{2,1,0:T(8,128)(2,1)S(1)} %get-tuple-element.17), channel_id=1, source_target_pairs={{0,2},{2,4},{3,1},{4,6},{5,3},{6,8},{7,5},{8,10},{9,7},{10,12},{11... | collective-permute-start | bytes 1572872 | tf_op jit(solution)/shard_map/ppermute | solution.py:526
  14.1 1.3 %collective-permute-start.3 = (bf16[2,128,1024]{2,1,0:T(8,128)(2,1)S(1)}, bf16[2,128,1024]{2,1,0:T(8,128)(2,1)S(1)}, u32[]{:S(2)}, u32[]{:S(2)}) collective-permute-start(bf16[2,128,1024]{2,1,0:T(8,128)(2,1)S(1)} %get-tuple-element.18), channel_id=1, source_target_pairs={{1,3},{2,0},{3,5},{4,2},{5,7},{6,4},{7,9},{8,6},{9,11},{10,8},{11,... | collective-permute-start | bytes 1572872 | tf_op jit(solution)/shard_map/ppermute | solution.py:526
  15.4 0.0 copy-done
  15.4 0.0 copy-done.4
  15.4 0.0 copy-done.2
  15.4 0.0 copy-done.1
  15.4 0.0 copy-start.3
  15.4 14.0 %attend.1 = (f32[32,1,128]{2,1,0:T(1,128)S(1)}, bf16[16,128,1024]{2,1,0:T(8,128)(2,1)}) custom-call(s32[64]{0:T(128)} %get-tuple-element.14.table_hbm.table_ref, bf16[2,16,4096]{2,1,0:T(8,128)(2,1)S(1)} %copy-done.1, bf16[4096,1024]{1,0:T(8,128)(2,1)} %prompt_hbm.1, bf16[16,128,1024]{2,1,0:T(8,128)(2,1)} %gen_hbm.3, s32[2,16]{1,0:T(2,128)} %token_hbm.1, ...), custom_call_target="tpu_custom_call" | custom-call | flops 2214592512 | bytes 16777216 | tf_op jit(solution)/shard_map/attend/pallas_call | solution.py:376
  29.4 14.4 %all_to_all.5.refs_5_ = f32[32,1,128]{2,1,0:T(1,128)S(1)} all-to-all(f32[32,1,128]{2,1,0:T(1,128)S(1)} %get-tuple-element.20), channel_id=1, replica_groups=mesh['dom'=16,'tp'=2] {'dom','tp'}, dimensions={0} | all-to-all | bytes 32768 | tf_op jit(solution)/shard_map/all_to_all | solution.py:542
  43.8 0.0 collective-permute-done.refs_0_
  43.8 0.0 collective-permute-done.1.refs_1_
  43.8 0.0 collective-permute-done.2.refs_2_
  43.8 0.0 collective-permute-done.3.refs_3_
  43.8 0.0 copy-done.3
  43.9 2.1 %finish.1 = (bf16[16,128,1024]{2,1,0:T(8,128)(2,1)}, f32[2,16]{1,0:T(2,128)}, f32[1,16]{1,0:T(1,128)}) custom-call(s32[64]{0:T(128)S(1)} %copy-done.3, bf16[2,128,1024]{2,1,0:T(8,128)(2,1)S(1)} %collective-permute-done.refs_0_, bf16[2,128,1024]{2,1,0:T(8,128)(2,1)S(1)} %collective-permute-done.1.refs_1_, ...), custom_call_target="tpu_custom_call", output_to_operand_aliasing={{0}: (5, {})} | custom-call | bytes 2097152 | tf_op jit(solution)/shard_map/finish/pallas_call | solution.py:469
Async XLA Ops:
  0.6 14.7 %copy-start = (bf16[2,16,1024]{2,1,0:T(8,128)(2,1)S(1)}, bf16[2,16,1024]{2,1,0:T(8,128)(2,1)}, u32[]{:S(2)}) copy-start(bf16[2,16,1024]{2,1,0:T(8,128)(2,1)} %new_ref.1) | copy-start | bytes 196612
  0.6 14.7 %copy-start.4 = (f32[16]{0:T(128)S(1)}, f32[16]{0:T(128)}, u32[]{:S(2)}) copy-start(f32[16]{0:T(128)} %param.19) | copy-start | bytes 196
  0.7 14.7 %copy-start.2 = (f32[4096]{0:T(1024)S(1)}, f32[4096]{0:T(1024)}, u32[]{:S(2)}) copy-start(f32[4096]{0:T(1024)} %param.17) | copy-start | bytes 49156
  0.7 14.7 %copy-start.1 = (bf16[2,16,4096]{2,1,0:T(8,128)(2,1)S(1)}, bf16[2,16,4096]{2,1,0:T(8,128)(2,1)}, u32[]{:S(2)}) copy-start(bf16[2,16,4096]{2,1,0:T(8,128)(2,1)} %q_ref.1) | copy-start | bytes 786436
  3.4 40.4 %collective-permute-start = (bf16[2,128,1024]{2,1,0:T(8,128)(2,1)S(1)}, bf16[2,128,1024]{2,1,0:T(8,128)(2,1)S(1)}, u32[]{:S(2)}, u32[]{:S(2)}) collective-permute-start(bf16[2,128,1024]{2,1,0:T(8,128)(2,1)S(1)} %get-tuple-element.15), channel_id=1, source_target_pairs={{1,5},{3,7},{4,0},{5,9},{6,2},{7,11},{8,4},{9,13},{10,6},{11,15},{... | collective-permute-start | bytes 1572872 | tf_op jit(solution)/shard_map/ppermute | solution.py:526
  4.7 39.1 %collective-permute-start.1 = (bf16[2,128,1024]{2,1,0:T(8,128)(2,1)S(1)}, bf16[2,128,1024]{2,1,0:T(8,128)(2,1)S(1)}, u32[]{:S(2)}, u32[]{:S(2)}) collective-permute-start(bf16[2,128,1024]{2,1,0:T(8,128)(2,1)S(1)} %get-tuple-element.16), channel_id=1, source_target_pairs={{0,4},{2,6},{4,8},{5,1},{6,10},{7,3},{8,12},{9,5},{10,14},{11,7},{... | collective-permute-start | bytes 1572872 | tf_op jit(solution)/shard_map/ppermute | solution.py:526
  10.4 33.4 %collective-permute-start.2 = (bf16[2,128,1024]{2,1,0:T(8,128)(2,1)S(1)}, bf16[2,128,1024]{2,1,0:T(8,128)(2,1)S(1)}, u32[]{:S(2)}, u32[]{:S(2)}) collective-permute-start(bf16[2,128,1024]{2,1,0:T(8,128)(2,1)S(1)} %get-tuple-element.17), channel_id=1, source_target_pairs={{0,2},{2,4},{3,1},{4,6},{5,3},{6,8},{7,5},{8,10},{9,7},{10,12},{11... | collective-permute-start | bytes 1572872 | tf_op jit(solution)/shard_map/ppermute | solution.py:526
  14.1 29.8 %collective-permute-start.3 = (bf16[2,128,1024]{2,1,0:T(8,128)(2,1)S(1)}, bf16[2,128,1024]{2,1,0:T(8,128)(2,1)S(1)}, u32[]{:S(2)}, u32[]{:S(2)}) collective-permute-start(bf16[2,128,1024]{2,1,0:T(8,128)(2,1)S(1)} %get-tuple-element.18), channel_id=1, source_target_pairs={{1,3},{2,0},{3,5},{4,2},{5,7},{6,4},{7,9},{8,6},{9,11},{10,8},{11,... | collective-permute-start | bytes 1572872 | tf_op jit(solution)/shard_map/ppermute | solution.py:526
  15.4 28.4 %copy-start.3 = (s32[64]{0:T(128)S(1)}, s32[64]{0:T(128)}, u32[]{:S(2)}) copy-start(s32[64]{0:T(128)} %get-tuple-element.14.table_hbm.table_ref) | copy-start | bytes 772

commit v7 on v6

--- a/solution.py
+++ b/solution.py
@@ -12,9 +12,10 @@
 SPAN = 2
 PICKS = 2
 TABLE_PARTS = 4
+AHEAD = 2
 NEG_FILL = -1e30
 LOG2_E = math.log2(math.e)
-KEY_CHUNK = 1024
+KEY_CHUNK = 512
 VMEM_BYTES = 44 * 1024 * 1024
 ROW_TILE = 16
 WINDOW = 2 * ROW_TILE
@@ -199,10 +200,13 @@
     ]
     for copy in lists:
         copy.start()
-    for j in range(chunks):
+    def start_loads(j):
         prompt_load(j).start()
         for i in range(per_chunk):
             gen_load(j * per_chunk + i).start()
+
+    for j in range(AHEAD):
+        start_loads(j)
 
     for copy in lists:
         copy.wait()
@@ -244,6 +248,7 @@
 
     def score_chunk(j, carry):
         prompt_load(j).wait()
+        pl.when(j + AHEAD < chunks)(functools.partial(start_loads, j + AHEAD))
         part = pl.ds(pl.multiple_of(j * chunk, chunk), chunk)
         for c in range(kv_local):
             block = score(queries[c], prompt[part, c * pair : c * pair + HEAD_DIM])
@@ -312,18 +317,23 @@
         )
         mixed_ref[c] = by_seat(mix(halves(exps), values))
 
-    def mix_chunk(j, carry):
-        part = pl.ds(pl.multiple_of(j * chunk, chunk), chunk)
+    def mix_chunks(step, carry):
         for c in range(kv_local):
             top = jnp.concatenate([tops[c]] * (chunk // HEAD_DIM), axis=1)
-            exps = jnp.exp2((scores[c, j] - top) * scale)
-            totals[c] = fold_lanes(exps, jnp.add, totals[c])
-            mixed_ref[c] += mix(
-                exps.astype(jnp.bfloat16), prompt[part, c * pair + HEAD_DIM : (c + 1) * pair]
-            )
+            total, mixed = totals[c], mixed_ref[c]
+            for i in range(AHEAD):
+                j = step * AHEAD + i
+                part = pl.ds(pl.multiple_of(j * chunk, chunk), chunk)
+                exps = jnp.exp2((scores[c, j] - top) * scale)
+                total = fold_lanes(exps, jnp.add, total)
+                mixed = mixed + mix(
+                    exps.astype(jnp.bfloat16), prompt[part, c * pair + HEAD_DIM : (c + 1) * pair]
+                )
+            totals[c] = total
+            mixed_ref[c] = mixed
         return carry
 
-    lax.fori_loop(0, chunks, mix_chunk, 0)
+    lax.fori_loop(0, chunks // AHEAD, mix_chunks, 0)
     weighted = jnp.zeros((base, HEAD_DIM), jnp.float32)
     for c in range(kv_local):
         mixed = mixed_ref[c] / jnp.sum(totals[c], axis=1, keepdims=True)

time: 46 us -> 45.8 us (level)
  blocking collectives: 14.4 us -> 13.9 us
    all_to_all x1, blocking collectives: 14.4 us -> 13.9 us  [local(): shares = lax.all_to_all(shares, everyone, 0, 0, tiled=True)]
  transfers between devices with their start and end apart: 4 -> 4, of which waited for: 0 -> 0; matrix products, arithmetic and copies ran while one was open for 0% -> 0% of each run, Pallas kernels for 31% -> 30%
where the time goes in v7:
time: 45.8 us; the launch traced here: 45.4 us
  Pallas kernels  18.6 us (41%)
  blocking collectives  13.9 us (30%)
  starting transfers between devices  12.2 us (27%)
  between operations  0.77 us (2%)
    all_to_all x1, blocking collectives, local(): shares = lax.all_to_all(shares, everyone, 0, 0, tiled=True)  13.9 us
    pallas_call x1, Pallas kernels, attend(): pl.pallas_call(functools.partial(attend_kernel, per_dev, group, kv_local,...  13.8 us
    ppermute x4, starting transfers between devices, local(): lax.ppermute(send, everyone, routes(doms, tps, steps))  12.2 us
    pallas_call x1, Pallas kernels, pack(): pl.pallas_call(functools.partial(pack_kernel, per_dev, doms, step_pairs),...  2.77 us
    pallas_call x1, Pallas kernels, finish(): pl.pallas_call(functools.partial(finish_kernel, doms, tps), out_shape=[ja...  1.98 us
  transfers between devices with their start and end apart: 4, of which 0 were waited for; matrix products, arithmetic and copies ran while one was open for 0% of the time, Pallas kernels for 30%

profile of v7, /device:TPU:0, one launch (start us, length us, event | category | flops | bytes accessed | tf_op | source)
XLA Modules:
  0.0 45.4 jit_solution(16086542121361901834)
XLA Ops:
  0.6 0.0 copy-start
  0.6 0.0 copy-start.4
  0.7 0.0 copy-start.2
  0.7 0.0 copy-start.1
  0.7 2.8 %pack_sends.1 = (bf16[2,128,1024]{2,1,0:T(8,128)(2,1)S(1)}, bf16[2,128,1024]{2,1,0:T(8,128)(2,1)S(1)}, bf16[2,128,1024]{2,1,0:T(8,128)(2,1)S(1)}, bf16[2,128,1024]{2,1,0:T(8,128)(2,1)S(1)}, s32[64]{0:T(128)}) custom-call(s32[256]{0:T(256)} %len_hbm.1, s32[256]{0:T(256)} %anc_hbm.1, bf16[2,16,1024]{2,1,0:T(8,128)(2,1)} %new_ref.1, bf16[16,128,1024]{2,1,0:T(8,128)(2,1)} %gen_hbm.3), custom_call_target="tpu_custom_call" | custom-call | bytes 4194304 | tf_op jit(solution)/shard_map/pack_sends/pallas_call | solution.py:117
  3.4 1.3 %collective-permute-start = (bf16[2,128,1024]{2,1,0:T(8,128)(2,1)S(1)}, bf16[2,128,1024]{2,1,0:T(8,128)(2,1)S(1)}, u32[]{:S(2)}, u32[]{:S(2)}) collective-permute-start(bf16[2,128,1024]{2,1,0:T(8,128)(2,1)S(1)} %get-tuple-element.15), channel_id=1, source_target_pairs={{1,5},{3,7},{4,0},{5,9},{6,2},{7,11},{8,4},{9,13},{10,6},{11,15},{... | collective-permute-start | bytes 1572872 | tf_op jit(solution)/shard_map/ppermute | solution.py:536
  4.7 5.6 %collective-permute-start.1 = (bf16[2,128,1024]{2,1,0:T(8,128)(2,1)S(1)}, bf16[2,128,1024]{2,1,0:T(8,128)(2,1)S(1)}, u32[]{:S(2)}, u32[]{:S(2)}) collective-permute-start(bf16[2,128,1024]{2,1,0:T(8,128)(2,1)S(1)} %get-tuple-element.16), channel_id=1, source_target_pairs={{0,4},{2,6},{4,8},{5,1},{6,10},{7,3},{8,12},{9,5},{10,14},{11,7},{... | collective-permute-start | bytes 1572872 | tf_op jit(solution)/shard_map/ppermute | solution.py:536
  10.4 4.0 %collective-permute-start.2 = (bf16[2,128,1024]{2,1,0:T(8,128)(2,1)S(1)}, bf16[2,128,1024]{2,1,0:T(8,128)(2,1)S(1)}, u32[]{:S(2)}, u32[]{:S(2)}) collective-permute-start(bf16[2,128,1024]{2,1,0:T(8,128)(2,1)S(1)} %get-tuple-element.17), channel_id=1, source_target_pairs={{0,2},{2,4},{3,1},{4,6},{5,3},{6,8},{7,5},{8,10},{9,7},{10,12},{11... | collective-permute-start | bytes 1572872 | tf_op jit(solution)/shard_map/ppermute | solution.py:536
  14.4 1.3 %collective-permute-start.3 = (bf16[2,128,1024]{2,1,0:T(8,128)(2,1)S(1)}, bf16[2,128,1024]{2,1,0:T(8,128)(2,1)S(1)}, u32[]{:S(2)}, u32[]{:S(2)}) collective-permute-start(bf16[2,128,1024]{2,1,0:T(8,128)(2,1)S(1)} %get-tuple-element.18), channel_id=1, source_target_pairs={{1,3},{2,0},{3,5},{4,2},{5,7},{6,4},{7,9},{8,6},{9,11},{10,8},{11,... | collective-permute-start | bytes 1572872 | tf_op jit(solution)/shard_map/ppermute | solution.py:536
  15.7 0.0 copy-done
  15.7 0.0 copy-done.4
  15.7 0.0 copy-done.2
  15.7 0.0 copy-done.1
  15.7 0.0 copy-start.3
  15.7 13.8 %attend.1 = (f32[32,1,128]{2,1,0:T(1,128)S(1)}, bf16[16,128,1024]{2,1,0:T(8,128)(2,1)}) custom-call(s32[64]{0:T(128)} %get-tuple-element.14.table_hbm.table_ref, bf16[2,16,4096]{2,1,0:T(8,128)(2,1)S(1)} %copy-done.1, bf16[4096,1024]{1,0:T(8,128)(2,1)} %prompt_hbm.1, bf16[16,128,1024]{2,1,0:T(8,128)(2,1)} %gen_hbm.3, s32[2,16]{1,0:T(2,128)} %token_hbm.1, ...), custom_call_target="tpu_custom_call" | custom-call | flops 2214592512 | bytes 16777216 | tf_op jit(solution)/shard_map/attend/pallas_call | solution.py:386
  29.6 13.9 %all_to_all.5.refs_5_ = f32[32,1,128]{2,1,0:T(1,128)S(1)} all-to-all(f32[32,1,128]{2,1,0:T(1,128)S(1)} %get-tuple-element.20), channel_id=1, replica_groups=mesh['dom'=16,'tp'=2] {'dom','tp'}, dimensions={0} | all-to-all | bytes 32768 | tf_op jit(solution)/shard_map/all_to_all | solution.py:552
  43.4 0.0 collective-permute-done.refs_0_
  43.4 0.0 collective-permute-done.1.refs_1_
  43.4 0.0 collective-permute-done.2.refs_2_
  43.4 0.0 collective-permute-done.3.refs_3_
  43.4 0.0 copy-done.3
  43.5 2.0 %finish.1 = (bf16[16,128,1024]{2,1,0:T(8,128)(2,1)}, f32[2,16]{1,0:T(2,128)}, f32[1,16]{1,0:T(1,128)}) custom-call(s32[64]{0:T(128)S(1)} %copy-done.3, bf16[2,128,1024]{2,1,0:T(8,128)(2,1)S(1)} %collective-permute-done.refs_0_, bf16[2,128,1024]{2,1,0:T(8,128)(2,1)S(1)} %collective-permute-done.1.refs_1_, ...), custom_call_target="tpu_custom_call", output_to_operand_aliasing={{0}: (5, {})} | custom-call | bytes 2097152 | tf_op jit(solution)/shard_map/finish/pallas_call | solution.py:479
Async XLA Ops:
  0.6 15.0 %copy-start = (bf16[2,16,1024]{2,1,0:T(8,128)(2,1)S(1)}, bf16[2,16,1024]{2,1,0:T(8,128)(2,1)}, u32[]{:S(2)}) copy-start(bf16[2,16,1024]{2,1,0:T(8,128)(2,1)} %new_ref.1) | copy-start | bytes 196612
  0.6 15.0 %copy-start.4 = (f32[16]{0:T(128)S(1)}, f32[16]{0:T(128)}, u32[]{:S(2)}) copy-start(f32[16]{0:T(128)} %param.19) | copy-start | bytes 196
  0.7 15.0 %copy-start.2 = (f32[4096]{0:T(1024)S(1)}, f32[4096]{0:T(1024)}, u32[]{:S(2)}) copy-start(f32[4096]{0:T(1024)} %param.17) | copy-start | bytes 49156
  0.7 15.0 %copy-start.1 = (bf16[2,16,4096]{2,1,0:T(8,128)(2,1)S(1)}, bf16[2,16,4096]{2,1,0:T(8,128)(2,1)}, u32[]{:S(2)}) copy-start(bf16[2,16,4096]{2,1,0:T(8,128)(2,1)} %q_ref.1) | copy-start | bytes 786436
  3.4 40.0 %collective-permute-start = (bf16[2,128,1024]{2,1,0:T(8,128)(2,1)S(1)}, bf16[2,128,1024]{2,1,0:T(8,128)(2,1)S(1)}, u32[]{:S(2)}, u32[]{:S(2)}) collective-permute-start(bf16[2,128,1024]{2,1,0:T(8,128)(2,1)S(1)} %get-tuple-element.15), channel_id=1, source_target_pairs={{1,5},{3,7},{4,0},{5,9},{6,2},{7,11},{8,4},{9,13},{10,6},{11,15},{... | collective-permute-start | bytes 1572872 | tf_op jit(solution)/shard_map/ppermute | solution.py:536
  4.7 38.7 %collective-permute-start.1 = (bf16[2,128,1024]{2,1,0:T(8,128)(2,1)S(1)}, bf16[2,128,1024]{2,1,0:T(8,128)(2,1)S(1)}, u32[]{:S(2)}, u32[]{:S(2)}) collective-permute-start(bf16[2,128,1024]{2,1,0:T(8,128)(2,1)S(1)} %get-tuple-element.16), channel_id=1, source_target_pairs={{0,4},{2,6},{4,8},{5,1},{6,10},{7,3},{8,12},{9,5},{10,14},{11,7},{... | collective-permute-start | bytes 1572872 | tf_op jit(solution)/shard_map/ppermute | solution.py:536
  10.4 33.1 %collective-permute-start.2 = (bf16[2,128,1024]{2,1,0:T(8,128)(2,1)S(1)}, bf16[2,128,1024]{2,1,0:T(8,128)(2,1)S(1)}, u32[]{:S(2)}, u32[]{:S(2)}) collective-permute-start(bf16[2,128,1024]{2,1,0:T(8,128)(2,1)S(1)} %get-tuple-element.17), channel_id=1, source_target_pairs={{0,2},{2,4},{3,1},{4,6},{5,3},{6,8},{7,5},{8,10},{9,7},{10,12},{11... | collective-permute-start | bytes 1572872 | tf_op jit(solution)/shard_map/ppermute | solution.py:536
  14.4 29.1 %collective-permute-start.3 = (bf16[2,128,1024]{2,1,0:T(8,128)(2,1)S(1)}, bf16[2,128,1024]{2,1,0:T(8,128)(2,1)S(1)}, u32[]{:S(2)}, u32[]{:S(2)}) collective-permute-start(bf16[2,128,1024]{2,1,0:T(8,128)(2,1)S(1)} %get-tuple-element.18), channel_id=1, source_target_pairs={{1,3},{2,0},{3,5},{4,2},{5,7},{6,4},{7,9},{8,6},{9,11},{10,8},{11,... | collective-permute-start | bytes 1572872 | tf_op jit(solution)/shard_map/ppermute | solution.py:536
  15.7 27.7 %copy-start.3 = (s32[64]{0:T(128)S(1)}, s32[64]{0:T(128)}, u32[]{:S(2)}) copy-start(s32[64]{0:T(128)} %get-tuple-element.14.table_hbm.table_ref) | copy-start | bytes 772

commit v8 on v7

--- a/solution.py
+++ b/solution.py
@@ -20,7 +20,22 @@
 ROW_TILE = 16
 WINDOW = 2 * ROW_TILE
 
-ORDERS = ((-2, 2, 1, -1), (2, -2, -1, 1))
+ROUNDS = ((2, 0), (2, 2), (1, 0), (1, 1))
+
+
+def is_first(device, distance, offset):
+    return (device + distance * 2 - offset) % (2 * distance) < distance
+
+
+def pairs(doms, distance, offset):
+    return [
+        [d, (d + distance) % doms] for d in range(doms) if is_first(d, distance, offset)
+    ]
+
+
+def partner(me, doms, distance, offset):
+    step = jnp.where(is_first(me, distance, offset), distance, doms - distance)
+    return (me + step) % doms
 
 
 def in_hbm(x):
@@ -58,10 +73,10 @@
     return low, high
 
 
-def pack_kernel(per_dev, doms, step_pairs, len_hbm, anc_hbm, new_hbm, gen_hbm, *refs):
-    sends = refs[: len(step_pairs)]
+def pack_kernel(per_dev, doms, len_hbm, anc_hbm, new_hbm, gen_hbm, *refs):
+    sends = refs[: len(ROUNDS)]
     table_hbm, table, len_ref, anc_ref, new_bf16, new_rows, list_sem, load_sem = refs[
-        len(step_pairs) :
+        len(ROUNDS) :
     ]
     new_at, own_at, anc_at, slot_at = (k * per_dev for k in range(TABLE_PARTS))
     lists = [
@@ -71,12 +86,12 @@
     ]
     for copy in lists:
         copy.start()
-    me, odd = lax.axis_index("dom"), lax.axis_index("tp") % 2
+    me = lax.axis_index("dom")
     lists[0].wait()
     picks = []
     loads = []
-    for k, (even_step, odd_step) in enumerate(step_pairs):
-        reader = jnp.clip(me + jnp.where(odd == 1, odd_step, even_step), 0, doms - 1)
+    for k, pairing in enumerate(ROUNDS):
+        reader = partner(me, doms, *pairing)
         low, high = named_range(anc_ref, reader * per_dev, me, per_dev)
         for i, pick in enumerate((jnp.minimum(low, per_dev - 1), jnp.maximum(high, 0))):
             target = sends[k].at[i]
@@ -90,8 +105,8 @@
         table[new_at + j] = len_ref[anc_ref[me * per_dev + j]] + 2
         table[own_at + j] = len_ref[me * per_dev + j]
         table[slot_at + j] = -PICKS
-    for k, (even_step, odd_step) in enumerate(step_pairs):
-        source = me - jnp.where(odd == 1, odd_step, even_step)
+    for k, pairing in enumerate(ROUNDS):
+        source = partner(me, doms, *pairing)
         low, _ = named_range(anc_ref, me * per_dev, source, per_dev)
         for j in range(per_dev):
             local = anc_ref[me * per_dev + j] - source * per_dev
@@ -108,14 +123,14 @@
     table_copy.wait()
 
 
-def pack(lengths, ancestors, new_kv, gen_cache, doms, step_pairs):
+def pack(lengths, ancestors, new_kv, gen_cache, doms):
     per_dev, rows, width = gen_cache.shape
-    count = len(step_pairs)
+    count = len(ROUNDS)
     vmem = pl.BlockSpec(memory_space=pltpu.VMEM)
     hbm = pl.BlockSpec(memory_space=pltpu.HBM)
     block_bytes = PICKS * rows * width * 2
     return pl.pallas_call(
-        functools.partial(pack_kernel, per_dev, doms, step_pairs),
+        functools.partial(pack_kernel, per_dev, doms),
         out_shape=[jax.ShapeDtypeStruct((PICKS, rows, width), jnp.bfloat16)] * count
         + [jax.ShapeDtypeStruct((TABLE_PARTS * per_dev,), jnp.int32)],
         in_specs=[hbm] * 4,
@@ -430,17 +445,26 @@
 
 
 def finish_kernel(doms, tps, table_ref, *refs):
-    gots = refs[: len(ORDERS[0])]
+    gots = refs[: len(ROUNDS)]
     _, all_ref, out_ref, twist_hbm, normal_hbm = refs[len(gots) : len(gots) + 5]
-    table, sums, twist, normal, copy_sem, small_sem = refs[len(gots) + 5 :]
+    arrived, table, sums, twist, normal, load_sem, copy_sem, small_sem = refs[len(gots) + 5 :]
     per_dev = out_ref.shape[0]
+    me = lax.axis_index("dom")
+    loads = []
+    for k, got in enumerate(gots):
+        theirs = jnp.where(is_first(me, *ROUNDS[k]), 1, 0)
+        loads.append(pltpu.make_async_copy(got.at[theirs], arrived.at[k], load_sem.at[k]))
+        loads[-1].start()
     table_copy = pltpu.make_async_copy(table_ref, table, small_sem.at[0])
     table_copy.start()
     table_copy.wait()
     slots = [table[(TABLE_PARTS - 1) * per_dev + p] for p in range(per_dev)]
-    for p, slot in enumerate(slots):
-        for k, got in enumerate(gots):
-            copy = pltpu.make_async_copy(got.at[slot % PICKS], out_ref.at[p], copy_sem.at[p])
+    for k, load in enumerate(loads):
+        load.wait()
+        for p, slot in enumerate(slots):
+            copy = pltpu.make_async_copy(
+                arrived.at[k, slot % PICKS], out_ref.at[p], copy_sem.at[p]
+            )
             pl.when(slot // PICKS == k)(copy.start)
     for d in range(doms):
         row = all_ref[d * tps]
@@ -465,7 +489,7 @@
     for copy in results:
         copy.start()
     for p, slot in enumerate(slots):
-        copy = pltpu.make_async_copy(gots[0].at[0], out_ref.at[p], copy_sem.at[p])
+        copy = pltpu.make_async_copy(arrived.at[0, 0], out_ref.at[p], copy_sem.at[p])
         pl.when(slot >= 0)(copy.wait)
     for copy in results:
         copy.wait()
@@ -483,14 +507,16 @@
             jax.ShapeDtypeStruct((2, per_dev), jnp.float32),
             jax.ShapeDtypeStruct((1, per_dev), jnp.float32),
         ],
-        in_specs=[vmem] + [vmem] * count + [hbm, vmem],
+        in_specs=[vmem] + [hbm] * count + [hbm, vmem],
         out_specs=[hbm, hbm, hbm],
         input_output_aliases={1 + count: 0},
         scratch_shapes=[
+            pltpu.VMEM((count, *gots[0].shape[1:]), jnp.bfloat16),
             pltpu.SMEM(table.shape, jnp.int32),
             pltpu.VMEM((doms, HEAD_DIM), jnp.float32),
             pltpu.VMEM((2, per_dev), jnp.float32),
             pltpu.VMEM((1, per_dev), jnp.float32),
+            pltpu.SemaphoreType.DMA((count,)),
             pltpu.SemaphoreType.DMA((per_dev,)),
             pltpu.SemaphoreType.DMA((3,)),
         ],
@@ -499,17 +525,7 @@
             flops=0, bytes_accessed=held.size, transcendentals=0
         ),
         name="finish",
-    )(table, *gots, held, shares)
-
-
-def routes(doms, tps, steps):
-    pairs = []
-    for d in range(doms):
-        for t in range(tps):
-            target = d + steps[t % 2]
-            if 0 <= target < doms:
-                pairs.append((d * tps + t, target * tps + t))
-    return pairs
+    )(table, *(in_hbm(got) for got in gots), held, shares)
 
 
 def local(
@@ -526,15 +542,12 @@
 ):
     doms, tps = lax.axis_size("dom"), lax.axis_size("tp")
     per_dev = gen_cache.shape[0]
-    step_pairs = list(zip(*ORDERS))
     everyone = ("dom", "tp")
 
-    *sends, table = pack(
-        lengths, ancestors, new_kv, gen_cache, doms, step_pairs
-    )
+    *sends, table = pack(lengths, ancestors, new_kv, gen_cache, doms)
     arrivals = [
-        lax.ppermute(send, everyone, routes(doms, tps, steps))
-        for send, steps in zip(sends, step_pairs)
+        lax.all_gather(send, "dom", axis_index_groups=pairs(doms, *pairing))
+        for send, pairing in zip(sends, ROUNDS)
     ]
 
     shares, resampled = attend(

time: 45.8 us -> 117 us (2.55)
  waiting for transfers between devices: 0.01 us -> 68 us
  between operations: 0.77 us -> 13.9 us
  starting transfers between devices: 12.2 us -> 0.16 us
  Pallas kernels: 18.6 us -> 20.6 us
    all_gather x0 -> x4, waiting for transfers between devices: none -> 66.1 us  [local(): lax.all_gather(send, 'dom', axis_index_groups=pairs(doms, *pairing))]
    ppermute x4 -> x0, starting transfers between devices: 12.2 us -> none  [local(): lax.ppermute(send, everyone, routes(doms, tps, steps))]
    unnamed x0 -> x4, waiting for transfers between devices: none -> 1.92 us
    pallas_call x1, Pallas kernels: 2.77 us -> 4.06 us  [pack(): pl.pallas_call(functools.partial(pack_kernel, per_dev, doms), out_shape=[...]
  transfers between devices with their start and end apart: 4 -> 4, of which waited for: 0 -> 3; matrix products, arithmetic and copies ran while one was open for 0% -> 0% of each run, Pallas kernels for 30% -> 12%
where the time goes in v8:
time: 117 us
  waiting for transfers between devices  68 us (58%)
  Pallas kernels  20.6 us (18%)
  blocking collectives  14.2 us (12%)
  between operations  13.9 us (12%)
    all_gather x4, waiting for transfers between devices, local(): lax.all_gather(send, 'dom', axis_index_groups=pairs(doms, *pairing))  66.1 us
    all_to_all x1, blocking collectives, local(): shares = lax.all_to_all(shares, everyone, 0, 0, tiled=True)  14.2 us
    pallas_call x1, Pallas kernels, attend(): pl.pallas_call(functools.partial(attend_kernel, per_dev, group, kv_local,...  13.8 us
    pallas_call x1, Pallas kernels, pack(): pl.pallas_call(functools.partial(pack_kernel, per_dev, doms), out_shape=[...  4.06 us
    pallas_call x1, Pallas kernels, finish(): pl.pallas_call(functools.partial(finish_kernel, doms, tps), out_shape=[ja...  2.7 us
  transfers between devices with their start and end apart: 4, of which 3 were waited for; matrix products, arithmetic and copies ran while one was open for 0% of the time, Pallas kernels for 12%

profile of v8, /device:TPU:0, one launch (start us, length us, event | category | flops | bytes accessed | tf_op | source)
XLA Modules:
  0.0 116.8 jit_solution(11735497852612582243)
XLA Ops:
  7.2 0.0 copy-start
  7.2 0.0 copy-start.4
  7.2 0.0 copy-start.2
  7.2 0.0 copy-start.1
  7.2 0.0 all-gather.9.cloned.1.call-start
  7.3 4.1 %pack_sends.1 = (bf16[2,128,1024]{2,1,0:T(8,128)(2,1)}, bf16[2,128,1024]{2,1,0:T(8,128)(2,1)}, bf16[2,128,1024]{2,1,0:T(8,128)(2,1)}, bf16[2,128,1024]{2,1,0:T(8,128)(2,1)}, s32[64]{0:T(128)}) custom-call(s32[256]{0:T(256)} %len_hbm.1, s32[256]{0:T(256)} %anc_hbm.1, bf16[2,16,1024]{2,1,0:T(8,128)(2,1)} %new_ref.1, bf16[16,128,1024]{2,1,0:T(8,128)(2,1)} %gen_hbm.3), custom_call_target="tpu_custom_call" | custom-call | bytes 4194304 | tf_op jit(solution)/shard_map/pack_sends/pallas_call | solution.py:132
  11.3 0.0 all-gather.9.cloned.1.call-update
  11.3 0.0 all-gather.11.cloned.1.call-start
  11.4 0.7 all-gather.11.cloned.1.call-update
  12.1 0.0 all-gather.13.cloned.1.call-start
  12.1 0.7 all-gather.13.cloned.1.call-update
  12.8 0.0 all-gather.15.cloned.1.call-start
  12.9 0.5 all-gather.15.cloned.1.call-update
  13.4 0.0 copy-done
  13.4 0.0 copy-done.4
  13.4 0.0 copy-done.2
  13.4 0.0 copy-done.1
  13.4 0.0 copy-start.3
  13.5 13.8 %attend.1 = (f32[32,1,128]{2,1,0:T(1,128)S(1)}, bf16[16,128,1024]{2,1,0:T(8,128)(2,1)}) custom-call(s32[64]{0:T(128)} %get-tuple-element.14.table_hbm.table_ref, bf16[2,16,4096]{2,1,0:T(8,128)(2,1)S(1)} %copy-done.1, bf16[4096,1024]{1,0:T(8,128)(2,1)} %prompt_hbm.1, bf16[16,128,1024]{2,1,0:T(8,128)(2,1)} %gen_hbm.3, s32[2,16]{1,0:T(2,128)} %token_hbm.1, ...), custom_call_target="tpu_custom_call" | custom-call | flops 2214592512 | bytes 16777216 | tf_op jit(solution)/shard_map/attend/pallas_call | solution.py:401
  27.3 14.2 %all_to_all.5.refs_5_ = f32[32,1,128]{2,1,0:T(1,128)S(1)} all-to-all(f32[32,1,128]{2,1,0:T(1,128)S(1)} %get-tuple-element.20), channel_id=1, replica_groups=mesh['dom'=16,'tp'=2] {'dom','tp'}, dimensions={0} | all-to-all | bytes 32768 | tf_op jit(solution)/shard_map/all_to_all | solution.py:565
  41.5 0.0 all-gather.9.cloned.1.call-done
  41.5 19.6 %all-gather.11.cloned.1.call-done = bf16[4,128,1024]{2,1,0:T(8,128)(2,1)} async-done(((bf16[2,128,1024]{2,1,0:T(8,128)(2,1)}), bf16[4,128,1024]{2,1,0:T(8,128)(2,1)}) %all-gather.11.cloned.1.call-update) | async-done | bytes 1048592 | tf_op jit(solution)/shard_map/all_gather | solution.py:549
  61.1 20.1 %all-gather.13.cloned.1.call-done = bf16[4,128,1024]{2,1,0:T(8,128)(2,1)} async-done(((bf16[2,128,1024]{2,1,0:T(8,128)(2,1)}), bf16[4,128,1024]{2,1,0:T(8,128)(2,1)}) %all-gather.13.cloned.1.call-update) | async-done | bytes 1048592 | tf_op jit(solution)/shard_map/all_gather | solution.py:549
  81.2 26.4 %all-gather.15.cloned.1.call-done = bf16[4,128,1024]{2,1,0:T(8,128)(2,1)} async-done(((bf16[2,128,1024]{2,1,0:T(8,128)(2,1)}), bf16[4,128,1024]{2,1,0:T(8,128)(2,1)}) %all-gather.15.cloned.1.call-update) | async-done | bytes 1048592 | tf_op jit(solution)/shard_map/all_gather | solution.py:549
  107.6 0.0 copy-done.3
  107.6 2.7 %finish.1 = (bf16[16,128,1024]{2,1,0:T(8,128)(2,1)}, f32[2,16]{1,0:T(2,128)}, f32[1,16]{1,0:T(1,128)}) custom-call(s32[64]{0:T(128)S(1)} %copy-done.3, bf16[2,2,128,1024]{3,2,1,0:T(8,128)(2,1)} %bitcast.11, bf16[2,2,128,1024]{3,2,1,0:T(8,128)(2,1)} %bitcast.12, bf16[2,2,128,1024]{3,2,1,0:T(8,128)(2,1)} %bitcast.13, ...), custom_call_target="tpu_custom_call", output_to_operand_aliasing={{0}: (5, {})} | custom-call | bytes 2097152 | tf_op jit(solution)/shard_map/finish/pallas_call | solution.py:503
Async XLA Ops:
  7.2 6.2 %copy-start = (bf16[2,16,1024]{2,1,0:T(8,128)(2,1)S(1)}, bf16[2,16,1024]{2,1,0:T(8,128)(2,1)}, u32[]{:S(2)}) copy-start(bf16[2,16,1024]{2,1,0:T(8,128)(2,1)} %new_ref.1) | copy-start | bytes 196612
  7.2 6.2 %copy-start.4 = (f32[16]{0:T(128)S(1)}, f32[16]{0:T(128)}, u32[]{:S(2)}) copy-start(f32[16]{0:T(128)} %param.19) | copy-start | bytes 196
  7.2 6.2 %copy-start.2 = (f32[4096]{0:T(1024)S(1)}, f32[4096]{0:T(1024)}, u32[]{:S(2)}) copy-start(f32[4096]{0:T(1024)} %param.17) | copy-start | bytes 49156
  7.2 6.2 %copy-start.1 = (bf16[2,16,4096]{2,1,0:T(8,128)(2,1)S(1)}, bf16[2,16,4096]{2,1,0:T(8,128)(2,1)}, u32[]{:S(2)}) copy-start(bf16[2,16,4096]{2,1,0:T(8,128)(2,1)} %q_ref.1) | copy-start | bytes 786436
  7.2 34.3 %all-gather.9.cloned.1.call-start = ((), (), s32[]{:S(2)}) async-start(), calls=%async_computation.1 | async-start | bytes 1572864 | tf_op jit(solution)/shard_map/all_gather | solution.py:549
  11.3 49.7 %all-gather.11.cloned.1.call-start = ((), (), s32[]{:S(2)}) async-start(), calls=%async_computation.2 | async-start | bytes 1572864 | tf_op jit(solution)/shard_map/all_gather | solution.py:549
  12.1 69.1 %all-gather.13.cloned.1.call-start = ((), (), s32[]{:S(2)}) async-start(), calls=%async_computation.3 | async-start | bytes 1572864 | tf_op jit(solution)/shard_map/all_gather | solution.py:549
  12.8 94.8 %all-gather.15.cloned.1.call-start = ((), (), s32[]{:S(2)}) async-start(), calls=%async_computation.4 | async-start | bytes 1572864 | tf_op jit(solution)/shard_map/all_gather | solution.py:549
  13.4 94.1 %copy-start.3 = (s32[64]{0:T(128)S(1)}, s32[64]{0:T(128)}, u32[]{:S(2)}) copy-start(s32[64]{0:T(128)} %get-tuple-element.14.table_hbm.table_ref) | copy-start | bytes 772
Sparse Core Ops, SparseCore 0:
  11.5 23.8 all-gather.8
  36.9 24.0 all-gather.10
  62.6 18.5 all-gather.12
  82.6 24.9 all-gather.14

commit v9 on v8

--- a/solution.py
+++ b/solution.py
@@ -33,6 +33,16 @@
     ]
 
 
+def swaps(doms, tps, distance, offset):
+    routes = []
+    for first, second in pairs(doms, distance, offset):
+        if second - first == distance:
+            for t in range(tps):
+                ends = (first * tps + t, second * tps + t)
+                routes += [ends, ends[::-1]]
+    return routes
+
+
 def partner(me, doms, distance, offset):
     step = jnp.where(is_first(me, distance, offset), distance, doms - distance)
     return (me + step) % doms
@@ -75,7 +85,7 @@
 
 def pack_kernel(per_dev, doms, len_hbm, anc_hbm, new_hbm, gen_hbm, *refs):
     sends = refs[: len(ROUNDS)]
-    table_hbm, table, len_ref, anc_ref, new_bf16, new_rows, list_sem, load_sem = refs[
+    table_hbm, table, len_ref, anc_ref, new_bf16, new_rows, held, list_sem, load_sem = refs[
         len(ROUNDS) :
     ]
     new_at, own_at, anc_at, slot_at = (k * per_dev for k in range(TABLE_PARTS))
@@ -94,7 +104,7 @@
         reader = partner(me, doms, *pairing)
         low, high = named_range(anc_ref, reader * per_dev, me, per_dev)
         for i, pick in enumerate((jnp.minimum(low, per_dev - 1), jnp.maximum(high, 0))):
-            target = sends[k].at[i]
+            target = held.at[i] if k == 0 else sends[k].at[i]
             load = pltpu.make_async_copy(gen_hbm.at[pick], target, load_sem.at[len(loads)])
             load.start()
             picks.append((pick, target))
@@ -117,10 +127,14 @@
     table_copy.start()
     lists[2].wait()
     new_rows[...] = new_bf16[...].astype(jnp.float32).reshape(new_rows.shape)
-    for load, (pick, target) in zip(loads, picks):
+    first_send = pltpu.make_async_copy(held, sends[0], list_sem.at[4])
+    for k, (load, (pick, target)) in enumerate(zip(loads, picks)):
         load.wait()
         place_new_rows(target, new_rows, len_ref[me * per_dev + pick], pick, per_dev)
+        if k == PICKS - 1:
+            first_send.start()
     table_copy.wait()
+    first_send.wait()
 
 
 def pack(lengths, ancestors, new_kv, gen_cache, doms):
@@ -134,14 +148,15 @@
         out_shape=[jax.ShapeDtypeStruct((PICKS, rows, width), jnp.bfloat16)] * count
         + [jax.ShapeDtypeStruct((TABLE_PARTS * per_dev,), jnp.int32)],
         in_specs=[hbm] * 4,
-        out_specs=[vmem] * count + [hbm],
+        out_specs=[hbm] + [vmem] * (count - 1) + [hbm],
         scratch_shapes=[
             pltpu.SMEM((TABLE_PARTS * per_dev,), jnp.int32),
             pltpu.SMEM(lengths.shape, jnp.int32),
             pltpu.SMEM(ancestors.shape, jnp.int32),
             pltpu.VMEM(new_kv.shape, jnp.bfloat16),
             pltpu.VMEM((2 * per_dev, width), jnp.float32),
-            pltpu.SemaphoreType.DMA((4,)),
+            pltpu.VMEM((PICKS, rows, width), jnp.bfloat16),
+            pltpu.SemaphoreType.DMA((5,)),
             pltpu.SemaphoreType.DMA((count * PICKS,)),
         ],
         compiler_params=pltpu.CompilerParams(vmem_limit_bytes=VMEM_BYTES),
@@ -449,23 +464,21 @@
     _, all_ref, out_ref, twist_hbm, normal_hbm = refs[len(gots) : len(gots) + 5]
     arrived, table, sums, twist, normal, load_sem, copy_sem, small_sem = refs[len(gots) + 5 :]
     per_dev = out_ref.shape[0]
-    me = lax.axis_index("dom")
-    loads = []
-    for k, got in enumerate(gots):
-        theirs = jnp.where(is_first(me, *ROUNDS[k]), 1, 0)
-        loads.append(pltpu.make_async_copy(got.at[theirs], arrived.at[k], load_sem.at[k]))
-        loads[-1].start()
+    theirs = jnp.where(is_first(lax.axis_index("dom"), *ROUNDS[0]), 1, 0)
+    load = pltpu.make_async_copy(gots[0].at[theirs], arrived, load_sem)
+    load.start()
     table_copy = pltpu.make_async_copy(table_ref, table, small_sem.at[0])
     table_copy.start()
     table_copy.wait()
     slots = [table[(TABLE_PARTS - 1) * per_dev + p] for p in range(per_dev)]
-    for k, load in enumerate(loads):
-        load.wait()
-        for p, slot in enumerate(slots):
-            copy = pltpu.make_async_copy(
-                arrived.at[k, slot % PICKS], out_ref.at[p], copy_sem.at[p]
-            )
+    for p, slot in enumerate(slots):
+        for k in range(1, len(gots)):
+            copy = pltpu.make_async_copy(gots[k].at[slot % PICKS], out_ref.at[p], copy_sem.at[p])
             pl.when(slot // PICKS == k)(copy.start)
+    load.wait()
+    for p, slot in enumerate(slots):
+        copy = pltpu.make_async_copy(arrived.at[slot % PICKS], out_ref.at[p], copy_sem.at[p])
+        pl.when(slot // PICKS == 0)(copy.start)
     for d in range(doms):
         row = all_ref[d * tps]
         for t in range(1, tps):
@@ -489,7 +502,7 @@
     for copy in results:
         copy.start()
     for p, slot in enumerate(slots):
-        copy = pltpu.make_async_copy(arrived.at[0, 0], out_ref.at[p], copy_sem.at[p])
+        copy = pltpu.make_async_copy(arrived.at[0], out_ref.at[p], copy_sem.at[p])
         pl.when(slot >= 0)(copy.wait)
     for copy in results:
         copy.wait()
@@ -507,16 +520,16 @@
             jax.ShapeDtypeStruct((2, per_dev), jnp.float32),
             jax.ShapeDtypeStruct((1, per_dev), jnp.float32),
         ],
-        in_specs=[vmem] + [hbm] * count + [hbm, vmem],
+        in_specs=[vmem, hbm] + [vmem] * (count - 1) + [hbm, vmem],
         out_specs=[hbm, hbm, hbm],
         input_output_aliases={1 + count: 0},
         scratch_shapes=[
-            pltpu.VMEM((count, *gots[0].shape[1:]), jnp.bfloat16),
+            pltpu.VMEM(gots[0].shape[1:], jnp.bfloat16),
             pltpu.SMEM(table.shape, jnp.int32),
             pltpu.VMEM((doms, HEAD_DIM), jnp.float32),
             pltpu.VMEM((2, per_dev), jnp.float32),
             pltpu.VMEM((1, per_dev), jnp.float32),
-            pltpu.SemaphoreType.DMA((count,)),
+            pltpu.SemaphoreType.DMA,
             pltpu.SemaphoreType.DMA((per_dev,)),
             pltpu.SemaphoreType.DMA((3,)),
         ],
@@ -525,7 +538,7 @@
             flops=0, bytes_accessed=held.size, transcendentals=0
         ),
         name="finish",
-    )(table, *(in_hbm(got) for got in gots), held, shares)
+    )(table, in_hbm(gots[0]), *gots[1:], held, shares)
 
 
 def local(
@@ -545,10 +558,9 @@
     everyone = ("dom", "tp")
 
     *sends, table = pack(lengths, ancestors, new_kv, gen_cache, doms)
-    arrivals = [
-        lax.all_gather(send, "dom", axis_index_groups=pairs(doms, *pairing))
-        for send, pairing in zip(sends, ROUNDS)
-    ]
+    arrivals = [lax.all_gather(sends[0], "dom", axis_index_groups=pairs(doms, *ROUNDS[0]))]
+    for send, pairing in zip(sends[1:], ROUNDS[1:]):
+        arrivals.append(lax.ppermute(send, everyone, swaps(doms, tps, *pairing)))
 
     shares, resampled = attend(
         table,

time: 117 us -> 59.7 us (0.51)
  waiting for transfers between devices: 68 us -> 4.07 us
  starting transfers between devices: 0.16 us -> 4.53 us
  blocking collectives: 14.2 us -> 17.1 us
  Pallas kernels: 20.6 us -> 19.3 us
    all_gather x4 -> x1, waiting for transfers between devices: 66.1 us -> 4.05 us  [local(): lax.all_gather(sends[0], 'dom', axis_index_groups=pairs(doms, *ROUNDS[0]))]
    ppermute x0 -> x3, starting transfers between devices: none -> 4.49 us  [local(): arrivals.append(lax.ppermute(send, everyone, swaps(doms, tps, *pairing)))]
    all_to_all x1, blocking collectives: 14.2 us -> 17.1 us  [local(): shares = lax.all_to_all(shares, everyone, 0, 0, tiled=True)]
    unnamed x4 -> x1, waiting for transfers between devices: 1.92 us -> 0.02 us
  transfers between devices with their start and end apart: 4 -> 4, of which waited for: 3 -> 1; matrix products, arithmetic and copies ran while one was open for 0% -> 0% of each run, Pallas kernels for 12% -> 24%
where the time goes in v9:
time: 59.7 us; the launch traced here: 59.2 us
  Pallas kernels  19.3 us (32%)
  blocking collectives  17.1 us (29%)
  between operations  14.2 us (24%)
  starting transfers between devices  4.53 us (8%)
  waiting for transfers between devices  4.07 us (7%)
    all_to_all x1, blocking collectives, local(): shares = lax.all_to_all(shares, everyone, 0, 0, tiled=True)  17.1 us
    pallas_call x1, Pallas kernels, attend(): pl.pallas_call(functools.partial(attend_kernel, per_dev, group, kv_local,...  13.9 us
    ppermute x3, starting transfers between devices, local(): arrivals.append(lax.ppermute(send, everyone, swaps(doms, tps, *pairing)))  4.49 us
    all_gather x1, waiting for transfers between devices, local(): lax.all_gather(sends[0], 'dom', axis_index_groups=pairs(doms, *ROUNDS[0]))  4.05 us
    pallas_call x1, Pallas kernels, pack(): pl.pallas_call(functools.partial(pack_kernel, per_dev, doms), out_shape=[...  3.01 us
    pallas_call x1, Pallas kernels, finish(): pl.pallas_call(functools.partial(finish_kernel, doms, tps), out_shape=[ja...  2.39 us
  transfers between devices with their start and end apart: 4, of which 1 were waited for; matrix products, arithmetic and copies ran while one was open for 0% of the time, Pallas kernels for 24%

profile of v9, /device:TPU:0, one launch (start us, length us, event | category | flops | bytes accessed | tf_op | source)
XLA Modules:
  0.0 59.2 jit_solution(12327184359699093254)
XLA Ops:
  7.2 0.0 copy-start
  7.2 0.0 copy-start.4
  7.2 0.0 copy-start.2
  7.2 0.0 copy-start.1
  7.2 0.0 all-gather.3.cloned.1.call-start
  7.3 3.0 %pack_sends.1 = (bf16[2,128,1024]{2,1,0:T(8,128)(2,1)}, bf16[2,128,1024]{2,1,0:T(8,128)(2,1)S(1)}, bf16[2,128,1024]{2,1,0:T(8,128)(2,1)S(1)}, bf16[2,128,1024]{2,1,0:T(8,128)(2,1)S(1)}, s32[64]{0:T(128)}) custom-call(s32[256]{0:T(256)} %len_hbm.1, s32[256]{0:T(256)} %anc_hbm.1, bf16[2,16,1024]{2,1,0:T(8,128)(2,1)} %new_ref.1, bf16[16,128,1024]{2,1,0:T(8,128)(2,1)} %gen_hbm.3), custom_call_target="tpu_custom_call" | custom-call | bytes 4194304 | tf_op jit(solution)/shard_map/pack_sends/pallas_call | solution.py:146
  10.3 0.0 all-gather.3.cloned.1.call-update
  10.3 0.7 %collective-permute-start = (bf16[2,128,1024]{2,1,0:T(8,128)(2,1)S(1)}, bf16[2,128,1024]{2,1,0:T(8,128)(2,1)S(1)}, u32[]{:S(2)}, u32[]{:S(2)}) collective-permute-start(bf16[2,128,1024]{2,1,0:T(8,128)(2,1)S(1)} %get-tuple-element.16), channel_id=1, source_target_pairs={{4,8},{8,4},{5,9},{9,5},{6,10},{10,6},{7,11},{11,7},{12,16},{16,12... | collective-permute-start | bytes 1572872 | tf_op jit(solution)/shard_map/ppermute | solution.py:563
  11.0 3.1 %collective-permute-start.1 = (bf16[2,128,1024]{2,1,0:T(8,128)(2,1)S(1)}, bf16[2,128,1024]{2,1,0:T(8,128)(2,1)S(1)}, u32[]{:S(2)}, u32[]{:S(2)}) collective-permute-start(bf16[2,128,1024]{2,1,0:T(8,128)(2,1)S(1)} %get-tuple-element.17), channel_id=1, source_target_pairs={{0,2},{2,0},{1,3},{3,1},{4,6},{6,4},{5,7},{7,5},{8,10},{10,8},{9,1... | collective-permute-start | bytes 1572872 | tf_op jit(solution)/shard_map/ppermute | solution.py:563
  14.1 0.7 %collective-permute-start.2 = (bf16[2,128,1024]{2,1,0:T(8,128)(2,1)S(1)}, bf16[2,128,1024]{2,1,0:T(8,128)(2,1)S(1)}, u32[]{:S(2)}, u32[]{:S(2)}) collective-permute-start(bf16[2,128,1024]{2,1,0:T(8,128)(2,1)S(1)} %get-tuple-element.18), channel_id=1, source_target_pairs={{2,4},{4,2},{3,5},{5,3},{6,8},{8,6},{7,9},{9,7},{10,12},{12,10},{1... | collective-permute-start | bytes 1572872 | tf_op jit(solution)/shard_map/ppermute | solution.py:563
  14.8 0.0 copy-done
  14.8 0.0 copy-done.4
  14.8 0.0 copy-done.2
  14.8 0.0 copy-done.1
  14.8 0.0 copy-start.3
  14.9 13.9 %attend.1 = (f32[32,1,128]{2,1,0:T(1,128)S(1)}, bf16[16,128,1024]{2,1,0:T(8,128)(2,1)}) custom-call(s32[64]{0:T(128)} %get-tuple-element.14.table_hbm.table_ref, bf16[2,16,4096]{2,1,0:T(8,128)(2,1)S(1)} %copy-done.1, bf16[4096,1024]{1,0:T(8,128)(2,1)} %prompt_hbm.1, bf16[16,128,1024]{2,1,0:T(8,128)(2,1)} %gen_hbm.3, s32[2,16]{1,0:T(2,128)} %token_hbm.1, ...), custom_call_target="tpu_custom_call" | custom-call | flops 2214592512 | bytes 16777216 | tf_op jit(solution)/shard_map/attend/pallas_call | solution.py:416
  28.8 17.1 %all_to_all.5.refs_5_ = f32[32,1,128]{2,1,0:T(1,128)S(1)} all-to-all(f32[32,1,128]{2,1,0:T(1,128)S(1)} %get-tuple-element.20), channel_id=1, replica_groups=mesh['dom'=16,'tp'=2] {'dom','tp'}, dimensions={0} | all-to-all | bytes 32768 | tf_op jit(solution)/shard_map/all_to_all | solution.py:577
  45.9 0.0 collective-permute-done.refs_1_
  45.9 0.0 collective-permute-done.1.refs_2_
  45.9 0.0 collective-permute-done.2.refs_3_
  45.9 4.0 %all-gather.3.cloned.1.call-done = bf16[4,128,1024]{2,1,0:T(8,128)(2,1)} async-done(((bf16[2,128,1024]{2,1,0:T(8,128)(2,1)}), bf16[4,128,1024]{2,1,0:T(8,128)(2,1)}) %all-gather.3.cloned.1.call-update) | async-done | bytes 1048592 | tf_op jit(solution)/shard_map/all_gather | solution.py:561
  49.9 0.0 copy-done.3
  49.9 2.4 %finish.1 = (bf16[16,128,1024]{2,1,0:T(8,128)(2,1)}, f32[2,16]{1,0:T(2,128)}, f32[1,16]{1,0:T(1,128)}) custom-call(s32[64]{0:T(128)S(1)} %copy-done.3, bf16[2,2,128,1024]{3,2,1,0:T(8,128)(2,1)} %bitcast.8, bf16[2,128,1024]{2,1,0:T(8,128)(2,1)S(1)} %collective-permute-done.refs_1_, ...), custom_call_target="tpu_custom_call", output_to_operand_aliasing={{0}: (5, {})} | custom-call | bytes 2097152 | tf_op jit(solution)/shard_map/finish/pallas_call | solution.py:516
Async XLA Ops:
  7.2 7.6 %copy-start = (bf16[2,16,1024]{2,1,0:T(8,128)(2,1)S(1)}, bf16[2,16,1024]{2,1,0:T(8,128)(2,1)}, u32[]{:S(2)}) copy-start(bf16[2,16,1024]{2,1,0:T(8,128)(2,1)} %new_ref.1) | copy-start | bytes 196612
  7.2 7.6 %copy-start.4 = (f32[16]{0:T(128)S(1)}, f32[16]{0:T(128)}, u32[]{:S(2)}) copy-start(f32[16]{0:T(128)} %param.19) | copy-start | bytes 196
  7.2 7.6 %copy-start.2 = (f32[4096]{0:T(1024)S(1)}, f32[4096]{0:T(1024)}, u32[]{:S(2)}) copy-start(f32[4096]{0:T(1024)} %param.17) | copy-start | bytes 49156
  7.2 7.6 %copy-start.1 = (bf16[2,16,4096]{2,1,0:T(8,128)(2,1)S(1)}, bf16[2,16,4096]{2,1,0:T(8,128)(2,1)}, u32[]{:S(2)}) copy-start(bf16[2,16,4096]{2,1,0:T(8,128)(2,1)} %q_ref.1) | copy-start | bytes 786436
  7.2 42.7 %all-gather.3.cloned.1.call-start = ((), (), s32[]{:S(2)}) async-start(), calls=%async_computation.1 | async-start | bytes 1572864 | tf_op jit(solution)/shard_map/all_gather | solution.py:561
  10.3 35.6 %collective-permute-start = (bf16[2,128,1024]{2,1,0:T(8,128)(2,1)S(1)}, bf16[2,128,1024]{2,1,0:T(8,128)(2,1)S(1)}, u32[]{:S(2)}, u32[]{:S(2)}) collective-permute-start(bf16[2,128,1024]{2,1,0:T(8,128)(2,1)S(1)} %get-tuple-element.16), channel_id=1, source_target_pairs={{4,8},{8,4},{5,9},{9,5},{6,10},{10,6},{7,11},{11,7},{12,16},{16,12... | collective-permute-start | bytes 1572872 | tf_op jit(solution)/shard_map/ppermute | solution.py:563
  11.0 34.9 %collective-permute-start.1 = (bf16[2,128,1024]{2,1,0:T(8,128)(2,1)S(1)}, bf16[2,128,1024]{2,1,0:T(8,128)(2,1)S(1)}, u32[]{:S(2)}, u32[]{:S(2)}) collective-permute-start(bf16[2,128,1024]{2,1,0:T(8,128)(2,1)S(1)} %get-tuple-element.17), channel_id=1, source_target_pairs={{0,2},{2,0},{1,3},{3,1},{4,6},{6,4},{5,7},{7,5},{8,10},{10,8},{9,1... | collective-permute-start | bytes 1572872 | tf_op jit(solution)/shard_map/ppermute | solution.py:563
  14.1 31.7 %collective-permute-start.2 = (bf16[2,128,1024]{2,1,0:T(8,128)(2,1)S(1)}, bf16[2,128,1024]{2,1,0:T(8,128)(2,1)S(1)}, u32[]{:S(2)}, u32[]{:S(2)}) collective-permute-start(bf16[2,128,1024]{2,1,0:T(8,128)(2,1)S(1)} %get-tuple-element.18), channel_id=1, source_target_pairs={{2,4},{4,2},{3,5},{5,3},{6,8},{8,6},{7,9},{9,7},{10,12},{12,10},{1... | collective-permute-start | bytes 1572872 | tf_op jit(solution)/shard_map/ppermute | solution.py:563
  14.8 35.1 %copy-start.3 = (s32[64]{0:T(128)S(1)}, s32[64]{0:T(128)}, u32[]{:S(2)}) copy-start(s32[64]{0:T(128)} %get-tuple-element.14.table_hbm.table_ref) | copy-start | bytes 772
Sparse Core Ops, SparseCore 0:
  10.4 39.4 all-gather.2

commit v10 on v8

--- a/solution.py
+++ b/solution.py
@@ -31,6 +31,16 @@
     return [
         [d, (d + distance) % doms] for d in range(doms) if is_first(d, distance, offset)
     ]
+
+
+def swaps(doms, tps, distance, offset):
+    routes = []
+    for first, second in pairs(doms, distance, offset):
+        if second - first == distance:
+            for t in range(tps):
+                ends = (first * tps + t, second * tps + t)
+                routes += [ends, ends[::-1]]
+    return routes
 
 
 def partner(me, doms, distance, offset):
@@ -447,24 +457,15 @@
 def finish_kernel(doms, tps, table_ref, *refs):
     gots = refs[: len(ROUNDS)]
     _, all_ref, out_ref, twist_hbm, normal_hbm = refs[len(gots) : len(gots) + 5]
-    arrived, table, sums, twist, normal, load_sem, copy_sem, small_sem = refs[len(gots) + 5 :]
+    table, sums, twist, normal, copy_sem, small_sem = refs[len(gots) + 5 :]
     per_dev = out_ref.shape[0]
-    me = lax.axis_index("dom")
-    loads = []
-    for k, got in enumerate(gots):
-        theirs = jnp.where(is_first(me, *ROUNDS[k]), 1, 0)
-        loads.append(pltpu.make_async_copy(got.at[theirs], arrived.at[k], load_sem.at[k]))
-        loads[-1].start()
     table_copy = pltpu.make_async_copy(table_ref, table, small_sem.at[0])
     table_copy.start()
     table_copy.wait()
     slots = [table[(TABLE_PARTS - 1) * per_dev + p] for p in range(per_dev)]
-    for k, load in enumerate(loads):
-        load.wait()
-        for p, slot in enumerate(slots):
-            copy = pltpu.make_async_copy(
-                arrived.at[k, slot % PICKS], out_ref.at[p], copy_sem.at[p]
-            )
+    for p, slot in enumerate(slots):
+        for k, got in enumerate(gots):
+            copy = pltpu.make_async_copy(got.at[slot % PICKS], out_ref.at[p], copy_sem.at[p])
             pl.when(slot // PICKS == k)(copy.start)
     for d in range(doms):
         row = all_ref[d * tps]
@@ -489,7 +490,7 @@
     for copy in results:
         copy.start()
     for p, slot in enumerate(slots):
-        copy = pltpu.make_async_copy(arrived.at[0, 0], out_ref.at[p], copy_sem.at[p])
+        copy = pltpu.make_async_copy(gots[0].at[0], out_ref.at[p], copy_sem.at[p])
         pl.when(slot >= 0)(copy.wait)
     for copy in results:
         copy.wait()
@@ -507,16 +508,14 @@
             jax.ShapeDtypeStruct((2, per_dev), jnp.float32),
             jax.ShapeDtypeStruct((1, per_dev), jnp.float32),
         ],
-        in_specs=[vmem] + [hbm] * count + [hbm, vmem],
+        in_specs=[vmem] + [vmem] * count + [hbm, vmem],
         out_specs=[hbm, hbm, hbm],
         input_output_aliases={1 + count: 0},
         scratch_shapes=[
-            pltpu.VMEM((count, *gots[0].shape[1:]), jnp.bfloat16),
             pltpu.SMEM(table.shape, jnp.int32),
             pltpu.VMEM((doms, HEAD_DIM), jnp.float32),
             pltpu.VMEM((2, per_dev), jnp.float32),
             pltpu.VMEM((1, per_dev), jnp.float32),
-            pltpu.SemaphoreType.DMA((count,)),
             pltpu.SemaphoreType.DMA((per_dev,)),
             pltpu.SemaphoreType.DMA((3,)),
         ],
@@ -525,7 +524,7 @@
             flops=0, bytes_accessed=held.size, transcendentals=0
         ),
         name="finish",
-    )(table, *(in_hbm(got) for got in gots), held, shares)
+    )(table, *gots, held, shares)
 
 
 def local(
@@ -546,7 +545,7 @@
 
     *sends, table = pack(lengths, ancestors, new_kv, gen_cache, doms)
     arrivals = [
-        lax.all_gather(send, "dom", axis_index_groups=pairs(doms, *pairing))
+        lax.ppermute(send, everyone, swaps(doms, tps, *pairing))
         for send, pairing in zip(sends, ROUNDS)
     ]
 

time: 117 us -> 43 us (0.37)
  waiting for transfers between devices: 68 us -> 0.01 us
  between operations: 13.9 us -> 0.76 us
  starting transfers between devices: 0.16 us -> 6 us
  blocking collectives: 14.2 us -> 17.2 us
  Pallas kernels: 20.6 us -> 18.5 us
    all_gather x4 -> x0, waiting for transfers between devices: 66.1 us -> none  [local(): lax.all_gather(send, 'dom', axis_index_groups=pairs(doms, *pairing))]
    ppermute x0 -> x4, starting transfers between devices: none -> 6 us  [local(): lax.ppermute(send, everyone, swaps(doms, tps, *pairing))]
    all_to_all x1, blocking collectives: 14.2 us -> 17.2 us  [local(): shares = lax.all_to_all(shares, everyone, 0, 0, tiled=True)]
    unnamed x4 -> x0, waiting for transfers between devices: 1.92 us -> none
    pallas_call x1, Pallas kernels: 4.06 us -> 2.71 us  [pack(): pl.pallas_call(functools.partial(pack_kernel, per_dev, doms), out_shape=[...]
  transfers between devices with their start and end apart: 4 -> 4, of which waited for: 3 -> 0; matrix products, arithmetic and copies ran while one was open for 0% -> 0% of each run, Pallas kernels for 12% -> 32%
where the time goes in v10:
time: 43 us; the launch traced here: 42.5 us
  Pallas kernels  18.5 us (43%)
  blocking collectives  17.2 us (40%)
  starting transfers between devices  6 us (14%)
  between operations  0.76 us (2%)
    all_to_all x1, blocking collectives, local(): shares = lax.all_to_all(shares, everyone, 0, 0, tiled=True)  17.2 us
    pallas_call x1, Pallas kernels, attend(): pl.pallas_call(functools.partial(attend_kernel, per_dev, group, kv_local,...  13.8 us
    ppermute x4, starting transfers between devices, local(): lax.ppermute(send, everyone, swaps(doms, tps, *pairing))  6 us
    pallas_call x1, Pallas kernels, pack(): pl.pallas_call(functools.partial(pack_kernel, per_dev, doms), out_shape=[...  2.71 us
    pallas_call x1, Pallas kernels, finish(): pl.pallas_call(functools.partial(finish_kernel, doms, tps), out_shape=[ja...  1.95 us
  transfers between devices with their start and end apart: 4, of which 0 were waited for; matrix products, arithmetic and copies ran while one was open for 0% of the time, Pallas kernels for 32%

profile of v10, /device:TPU:0, one launch (start us, length us, event | category | flops | bytes accessed | tf_op | source)
XLA Modules:
  0.0 42.5 jit_solution(4357702522594004665)
XLA Ops:
  0.6 0.0 copy-start
  0.6 0.0 copy-start.4
  0.7 0.0 copy-start.2
  0.7 0.0 copy-start.1
  0.7 2.7 %pack_sends.1 = (bf16[2,128,1024]{2,1,0:T(8,128)(2,1)S(1)}, bf16[2,128,1024]{2,1,0:T(8,128)(2,1)S(1)}, bf16[2,128,1024]{2,1,0:T(8,128)(2,1)S(1)}, bf16[2,128,1024]{2,1,0:T(8,128)(2,1)S(1)}, s32[64]{0:T(128)}) custom-call(s32[256]{0:T(256)} %len_hbm.1, s32[256]{0:T(256)} %anc_hbm.1, bf16[2,16,1024]{2,1,0:T(8,128)(2,1)} %new_ref.1, bf16[16,128,1024]{2,1,0:T(8,128)(2,1)} %gen_hbm.3), custom_call_target="tpu_custom_call" | custom-call | bytes 4194304 | tf_op jit(solution)/shard_map/pack_sends/pallas_call | solution.py:142
  3.4 3.2 %collective-permute-start = (bf16[2,128,1024]{2,1,0:T(8,128)(2,1)S(1)}, bf16[2,128,1024]{2,1,0:T(8,128)(2,1)S(1)}, u32[]{:S(2)}, u32[]{:S(2)}) collective-permute-start(bf16[2,128,1024]{2,1,0:T(8,128)(2,1)S(1)} %get-tuple-element.15), channel_id=1, source_target_pairs={{0,4},{4,0},{1,5},{5,1},{2,6},{6,2},{3,7},{7,3},{8,12},{12,8},{9,1... | collective-permute-start | bytes 1572872 | tf_op jit(solution)/shard_map/ppermute | solution.py:548
  6.6 0.7 %collective-permute-start.1 = (bf16[2,128,1024]{2,1,0:T(8,128)(2,1)S(1)}, bf16[2,128,1024]{2,1,0:T(8,128)(2,1)S(1)}, u32[]{:S(2)}, u32[]{:S(2)}) collective-permute-start(bf16[2,128,1024]{2,1,0:T(8,128)(2,1)S(1)} %get-tuple-element.16), channel_id=1, source_target_pairs={{4,8},{8,4},{5,9},{9,5},{6,10},{10,6},{7,11},{11,7},{12,16},{16,12... | collective-permute-start | bytes 1572872 | tf_op jit(solution)/shard_map/ppermute | solution.py:548
  7.3 1.4 %collective-permute-start.2 = (bf16[2,128,1024]{2,1,0:T(8,128)(2,1)S(1)}, bf16[2,128,1024]{2,1,0:T(8,128)(2,1)S(1)}, u32[]{:S(2)}, u32[]{:S(2)}) collective-permute-start(bf16[2,128,1024]{2,1,0:T(8,128)(2,1)S(1)} %get-tuple-element.17), channel_id=1, source_target_pairs={{0,2},{2,0},{1,3},{3,1},{4,6},{6,4},{5,7},{7,5},{8,10},{10,8},{9,1... | collective-permute-start | bytes 1572872 | tf_op jit(solution)/shard_map/ppermute | solution.py:548
  8.7 0.7 %collective-permute-start.3 = (bf16[2,128,1024]{2,1,0:T(8,128)(2,1)S(1)}, bf16[2,128,1024]{2,1,0:T(8,128)(2,1)S(1)}, u32[]{:S(2)}, u32[]{:S(2)}) collective-permute-start(bf16[2,128,1024]{2,1,0:T(8,128)(2,1)S(1)} %get-tuple-element.18), channel_id=1, source_target_pairs={{2,4},{4,2},{3,5},{5,3},{6,8},{8,6},{7,9},{9,7},{10,12},{12,10},{1... | collective-permute-start | bytes 1572872 | tf_op jit(solution)/shard_map/ppermute | solution.py:548
  9.4 0.0 copy-done
  9.4 0.0 copy-done.4
  9.4 0.0 copy-done.2
  9.4 0.0 copy-done.1
  9.4 0.0 copy-start.3
  9.5 13.8 %attend.1 = (f32[32,1,128]{2,1,0:T(1,128)S(1)}, bf16[16,128,1024]{2,1,0:T(8,128)(2,1)}) custom-call(s32[64]{0:T(128)} %get-tuple-element.14.table_hbm.table_ref, bf16[2,16,4096]{2,1,0:T(8,128)(2,1)S(1)} %copy-done.1, bf16[4096,1024]{1,0:T(8,128)(2,1)} %prompt_hbm.1, bf16[16,128,1024]{2,1,0:T(8,128)(2,1)} %gen_hbm.3, s32[2,16]{1,0:T(2,128)} %token_hbm.1, ...), custom_call_target="tpu_custom_call" | custom-call | flops 2214592512 | bytes 16777216 | tf_op jit(solution)/shard_map/attend/pallas_call | solution.py:411
  23.3 17.2 %all_to_all.5.refs_5_ = f32[32,1,128]{2,1,0:T(1,128)S(1)} all-to-all(f32[32,1,128]{2,1,0:T(1,128)S(1)} %get-tuple-element.20), channel_id=1, replica_groups=mesh['dom'=16,'tp'=2] {'dom','tp'}, dimensions={0} | all-to-all | bytes 32768 | tf_op jit(solution)/shard_map/all_to_all | solution.py:564
  40.5 0.0 collective-permute-done.refs_0_
  40.5 0.0 collective-permute-done.1.refs_1_
  40.5 0.0 collective-permute-done.2.refs_2_
  40.5 0.0 collective-permute-done.3.refs_3_
  40.5 0.0 copy-done.3
  40.5 1.9 %finish.1 = (bf16[16,128,1024]{2,1,0:T(8,128)(2,1)}, f32[2,16]{1,0:T(2,128)}, f32[1,16]{1,0:T(1,128)}) custom-call(s32[64]{0:T(128)S(1)} %copy-done.3, bf16[2,128,1024]{2,1,0:T(8,128)(2,1)S(1)} %collective-permute-done.refs_0_, bf16[2,128,1024]{2,1,0:T(8,128)(2,1)S(1)} %collective-permute-done.1.refs_1_, ...), custom_call_target="tpu_custom_call", output_to_operand_aliasing={{0}: (5, {})} | custom-call | bytes 2097152 | tf_op jit(solution)/shard_map/finish/pallas_call | solution.py:504
Async XLA Ops:
  0.6 8.8 %copy-start = (bf16[2,16,1024]{2,1,0:T(8,128)(2,1)S(1)}, bf16[2,16,1024]{2,1,0:T(8,128)(2,1)}, u32[]{:S(2)}) copy-start(bf16[2,16,1024]{2,1,0:T(8,128)(2,1)} %new_ref.1) | copy-start | bytes 196612
  0.6 8.8 %copy-start.4 = (f32[16]{0:T(128)S(1)}, f32[16]{0:T(128)}, u32[]{:S(2)}) copy-start(f32[16]{0:T(128)} %param.19) | copy-start | bytes 196
  0.7 8.8 %copy-start.2 = (f32[4096]{0:T(1024)S(1)}, f32[4096]{0:T(1024)}, u32[]{:S(2)}) copy-start(f32[4096]{0:T(1024)} %param.17) | copy-start | bytes 49156
  0.7 8.8 %copy-start.1 = (bf16[2,16,4096]{2,1,0:T(8,128)(2,1)S(1)}, bf16[2,16,4096]{2,1,0:T(8,128)(2,1)}, u32[]{:S(2)}) copy-start(bf16[2,16,4096]{2,1,0:T(8,128)(2,1)} %q_ref.1) | copy-start | bytes 786436
  3.4 37.1 %collective-permute-start = (bf16[2,128,1024]{2,1,0:T(8,128)(2,1)S(1)}, bf16[2,128,1024]{2,1,0:T(8,128)(2,1)S(1)}, u32[]{:S(2)}, u32[]{:S(2)}) collective-permute-start(bf16[2,128,1024]{2,1,0:T(8,128)(2,1)S(1)} %get-tuple-element.15), channel_id=1, source_target_pairs={{0,4},{4,0},{1,5},{5,1},{2,6},{6,2},{3,7},{7,3},{8,12},{12,8},{9,1... | collective-permute-start | bytes 1572872 | tf_op jit(solution)/shard_map/ppermute | solution.py:548
  6.6 33.9 %collective-permute-start.1 = (bf16[2,128,1024]{2,1,0:T(8,128)(2,1)S(1)}, bf16[2,128,1024]{2,1,0:T(8,128)(2,1)S(1)}, u32[]{:S(2)}, u32[]{:S(2)}) collective-permute-start(bf16[2,128,1024]{2,1,0:T(8,128)(2,1)S(1)} %get-tuple-element.16), channel_id=1, source_target_pairs={{4,8},{8,4},{5,9},{9,5},{6,10},{10,6},{7,11},{11,7},{12,16},{16,12... | collective-permute-start | bytes 1572872 | tf_op jit(solution)/shard_map/ppermute | solution.py:548
  7.3 33.2 %collective-permute-start.2 = (bf16[2,128,1024]{2,1,0:T(8,128)(2,1)S(1)}, bf16[2,128,1024]{2,1,0:T(8,128)(2,1)S(1)}, u32[]{:S(2)}, u32[]{:S(2)}) collective-permute-start(bf16[2,128,1024]{2,1,0:T(8,128)(2,1)S(1)} %get-tuple-element.17), channel_id=1, source_target_pairs={{0,2},{2,0},{1,3},{3,1},{4,6},{6,4},{5,7},{7,5},{8,10},{10,8},{9,1... | collective-permute-start | bytes 1572872 | tf_op jit(solution)/shard_map/ppermute | solution.py:548
  8.7 31.8 %collective-permute-start.3 = (bf16[2,128,1024]{2,1,0:T(8,128)(2,1)S(1)}, bf16[2,128,1024]{2,1,0:T(8,128)(2,1)S(1)}, u32[]{:S(2)}, u32[]{:S(2)}) collective-permute-start(bf16[2,128,1024]{2,1,0:T(8,128)(2,1)S(1)} %get-tuple-element.18), channel_id=1, source_target_pairs={{2,4},{4,2},{3,5},{5,3},{6,8},{8,6},{7,9},{9,7},{10,12},{12,10},{1... | collective-permute-start | bytes 1572872 | tf_op jit(solution)/shard_map/ppermute | solution.py:548
  9.4 31.1 %copy-start.3 = (s32[64]{0:T(128)S(1)}, s32[64]{0:T(128)}, u32[]{:S(2)}) copy-start(s32[64]{0:T(128)} %get-tuple-element.14.table_hbm.table_ref) | copy-start | bytes 772

commit v11 on v10

--- a/solution.py
+++ b/solution.py
@@ -20,7 +20,7 @@
 ROW_TILE = 16
 WINDOW = 2 * ROW_TILE
 
-ROUNDS = ((2, 0), (2, 2), (1, 0), (1, 1))
+ROUNDS = ((2, 0), (2, 2), (1, 1), (1, 0))
 
 
 def is_first(device, distance, offset):

time: 43 us -> 46.8 us (1.088)
  starting transfers between devices: 6 us -> 11.4 us
  blocking collectives: 17.2 us -> 15.7 us
    ppermute x4, starting transfers between devices: 6 us -> 11.4 us  [local(): lax.ppermute(send, everyone, swaps(doms, tps, *pairing))]
    all_to_all x1, blocking collectives: 17.2 us -> 15.7 us  [local(): shares = lax.all_to_all(shares, everyone, 0, 0, tiled=True)]
  transfers between devices with their start and end apart: 4 -> 4, of which waited for: 0 -> 0; matrix products, arithmetic and copies ran while one was open for 0% -> 0% of each run, Pallas kernels for 32% -> 30%
where the time goes in v11:
time: 46.8 us; the launch traced here: 46.5 us
  Pallas kernels  18.6 us (40%)
  blocking collectives  15.7 us (34%)
  starting transfers between devices  11.4 us (24%)
  between operations  0.73 us (2%)
    all_to_all x1, blocking collectives, local(): shares = lax.all_to_all(shares, everyone, 0, 0, tiled=True)  15.7 us
    pallas_call x1, Pallas kernels, attend(): pl.pallas_call(functools.partial(attend_kernel, per_dev, group, kv_local,...  13.8 us
    ppermute x4, starting transfers between devices, local(): lax.ppermute(send, everyone, swaps(doms, tps, *pairing))  11.4 us
    pallas_call x1, Pallas kernels, pack(): pl.pallas_call(functools.partial(pack_kernel, per_dev, doms), out_shape=[...  2.79 us
    pallas_call x1, Pallas kernels, finish(): pl.pallas_call(functools.partial(finish_kernel, doms, tps), out_shape=[ja...  1.99 us
  transfers between devices with their start and end apart: 4, of which 0 were waited for; matrix products, arithmetic and copies ran while one was open for 0% of the time, Pallas kernels for 30%

profile of v11, /device:TPU:0, one launch (start us, length us, event | category | flops | bytes accessed | tf_op | source)
XLA Modules:
  0.0 46.5 jit_solution(7762769088788516232)
XLA Ops:
  0.6 0.0 copy-start
  0.6 0.0 copy-start.4
  0.7 0.0 copy-start.2
  0.7 0.0 copy-start.1
  0.7 2.8 %pack_sends.1 = (bf16[2,128,1024]{2,1,0:T(8,128)(2,1)S(1)}, bf16[2,128,1024]{2,1,0:T(8,128)(2,1)S(1)}, bf16[2,128,1024]{2,1,0:T(8,128)(2,1)S(1)}, bf16[2,128,1024]{2,1,0:T(8,128)(2,1)S(1)}, s32[64]{0:T(128)}) custom-call(s32[256]{0:T(256)} %len_hbm.1, s32[256]{0:T(256)} %anc_hbm.1, bf16[2,16,1024]{2,1,0:T(8,128)(2,1)} %new_ref.1, bf16[16,128,1024]{2,1,0:T(8,128)(2,1)} %gen_hbm.3), custom_call_target="tpu_custom_call" | custom-call | bytes 4194304 | tf_op jit(solution)/shard_map/pack_sends/pallas_call | solution.py:142
  3.5 3.3 %collective-permute-start = (bf16[2,128,1024]{2,1,0:T(8,128)(2,1)S(1)}, bf16[2,128,1024]{2,1,0:T(8,128)(2,1)S(1)}, u32[]{:S(2)}, u32[]{:S(2)}) collective-permute-start(bf16[2,128,1024]{2,1,0:T(8,128)(2,1)S(1)} %get-tuple-element.15), channel_id=1, source_target_pairs={{0,4},{4,0},{1,5},{5,1},{2,6},{6,2},{3,7},{7,3},{8,12},{12,8},{9,1... | collective-permute-start | bytes 1572872 | tf_op jit(solution)/shard_map/ppermute | solution.py:548
  6.7 0.7 %collective-permute-start.1 = (bf16[2,128,1024]{2,1,0:T(8,128)(2,1)S(1)}, bf16[2,128,1024]{2,1,0:T(8,128)(2,1)S(1)}, u32[]{:S(2)}, u32[]{:S(2)}) collective-permute-start(bf16[2,128,1024]{2,1,0:T(8,128)(2,1)S(1)} %get-tuple-element.16), channel_id=1, source_target_pairs={{4,8},{8,4},{5,9},{9,5},{6,10},{10,6},{7,11},{11,7},{12,16},{16,12... | collective-permute-start | bytes 1572872 | tf_op jit(solution)/shard_map/ppermute | solution.py:548
  7.4 0.7 %collective-permute-start.2 = (bf16[2,128,1024]{2,1,0:T(8,128)(2,1)S(1)}, bf16[2,128,1024]{2,1,0:T(8,128)(2,1)S(1)}, u32[]{:S(2)}, u32[]{:S(2)}) collective-permute-start(bf16[2,128,1024]{2,1,0:T(8,128)(2,1)S(1)} %get-tuple-element.17), channel_id=1, source_target_pairs={{2,4},{4,2},{3,5},{5,3},{6,8},{8,6},{7,9},{9,7},{10,12},{12,10},{1... | collective-permute-start | bytes 1572872 | tf_op jit(solution)/shard_map/ppermute | solution.py:548
  8.1 6.8 %collective-permute-start.3 = (bf16[2,128,1024]{2,1,0:T(8,128)(2,1)S(1)}, bf16[2,128,1024]{2,1,0:T(8,128)(2,1)S(1)}, u32[]{:S(2)}, u32[]{:S(2)}) collective-permute-start(bf16[2,128,1024]{2,1,0:T(8,128)(2,1)S(1)} %get-tuple-element.18), channel_id=1, source_target_pairs={{0,2},{2,0},{1,3},{3,1},{4,6},{6,4},{5,7},{7,5},{8,10},{10,8},{9,1... | collective-permute-start | bytes 1572872 | tf_op jit(solution)/shard_map/ppermute | solution.py:548
  14.9 0.0 copy-done
  14.9 0.0 copy-done.4
  14.9 0.0 copy-done.2
  14.9 0.0 copy-done.1
  14.9 0.0 copy-start.3
  15.0 13.8 %attend.1 = (f32[32,1,128]{2,1,0:T(1,128)S(1)}, bf16[16,128,1024]{2,1,0:T(8,128)(2,1)}) custom-call(s32[64]{0:T(128)} %get-tuple-element.14.table_hbm.table_ref, bf16[2,16,4096]{2,1,0:T(8,128)(2,1)S(1)} %copy-done.1, bf16[4096,1024]{1,0:T(8,128)(2,1)} %prompt_hbm.1, bf16[16,128,1024]{2,1,0:T(8,128)(2,1)} %gen_hbm.3, s32[2,16]{1,0:T(2,128)} %token_hbm.1, ...), custom_call_target="tpu_custom_call" | custom-call | flops 2214592512 | bytes 16777216 | tf_op jit(solution)/shard_map/attend/pallas_call | solution.py:411
  28.8 15.7 %all_to_all.5.refs_5_ = f32[32,1,128]{2,1,0:T(1,128)S(1)} all-to-all(f32[32,1,128]{2,1,0:T(1,128)S(1)} %get-tuple-element.20), channel_id=1, replica_groups=mesh['dom'=16,'tp'=2] {'dom','tp'}, dimensions={0} | all-to-all | bytes 32768 | tf_op jit(solution)/shard_map/all_to_all | solution.py:564
  44.5 0.0 collective-permute-done.refs_0_
  44.5 0.0 collective-permute-done.1.refs_1_
  44.5 0.0 collective-permute-done.2.refs_2_
  44.5 0.0 collective-permute-done.3.refs_3_
  44.5 0.0 copy-done.3
  44.5 2.0 %finish.1 = (bf16[16,128,1024]{2,1,0:T(8,128)(2,1)}, f32[2,16]{1,0:T(2,128)}, f32[1,16]{1,0:T(1,128)}) custom-call(s32[64]{0:T(128)S(1)} %copy-done.3, bf16[2,128,1024]{2,1,0:T(8,128)(2,1)S(1)} %collective-permute-done.refs_0_, bf16[2,128,1024]{2,1,0:T(8,128)(2,1)S(1)} %collective-permute-done.1.refs_1_, ...), custom_call_target="tpu_custom_call", output_to_operand_aliasing={{0}: (5, {})} | custom-call | bytes 2097152 | tf_op jit(solution)/shard_map/finish/pallas_call | solution.py:504
Async XLA Ops:
  0.6 14.3 %copy-start = (bf16[2,16,1024]{2,1,0:T(8,128)(2,1)S(1)}, bf16[2,16,1024]{2,1,0:T(8,128)(2,1)}, u32[]{:S(2)}) copy-start(bf16[2,16,1024]{2,1,0:T(8,128)(2,1)} %new_ref.1) | copy-start | bytes 196612
  0.6 14.3 %copy-start.4 = (f32[16]{0:T(128)S(1)}, f32[16]{0:T(128)}, u32[]{:S(2)}) copy-start(f32[16]{0:T(128)} %param.19) | copy-start | bytes 196
  0.7 14.3 %copy-start.2 = (f32[4096]{0:T(1024)S(1)}, f32[4096]{0:T(1024)}, u32[]{:S(2)}) copy-start(f32[4096]{0:T(1024)} %param.17) | copy-start | bytes 49156
  0.7 14.3 %copy-start.1 = (bf16[2,16,4096]{2,1,0:T(8,128)(2,1)S(1)}, bf16[2,16,4096]{2,1,0:T(8,128)(2,1)}, u32[]{:S(2)}) copy-start(bf16[2,16,4096]{2,1,0:T(8,128)(2,1)} %q_ref.1) | copy-start | bytes 786436
  3.5 41.0 %collective-permute-start = (bf16[2,128,1024]{2,1,0:T(8,128)(2,1)S(1)}, bf16[2,128,1024]{2,1,0:T(8,128)(2,1)S(1)}, u32[]{:S(2)}, u32[]{:S(2)}) collective-permute-start(bf16[2,128,1024]{2,1,0:T(8,128)(2,1)S(1)} %get-tuple-element.15), channel_id=1, source_target_pairs={{0,4},{4,0},{1,5},{5,1},{2,6},{6,2},{3,7},{7,3},{8,12},{12,8},{9,1... | collective-permute-start | bytes 1572872 | tf_op jit(solution)/shard_map/ppermute | solution.py:548
  6.7 37.7 %collective-permute-start.1 = (bf16[2,128,1024]{2,1,0:T(8,128)(2,1)S(1)}, bf16[2,128,1024]{2,1,0:T(8,128)(2,1)S(1)}, u32[]{:S(2)}, u32[]{:S(2)}) collective-permute-start(bf16[2,128,1024]{2,1,0:T(8,128)(2,1)S(1)} %get-tuple-element.16), channel_id=1, source_target_pairs={{4,8},{8,4},{5,9},{9,5},{6,10},{10,6},{7,11},{11,7},{12,16},{16,12... | collective-permute-start | bytes 1572872 | tf_op jit(solution)/shard_map/ppermute | solution.py:548
  7.4 37.1 %collective-permute-start.2 = (bf16[2,128,1024]{2,1,0:T(8,128)(2,1)S(1)}, bf16[2,128,1024]{2,1,0:T(8,128)(2,1)S(1)}, u32[]{:S(2)}, u32[]{:S(2)}) collective-permute-start(bf16[2,128,1024]{2,1,0:T(8,128)(2,1)S(1)} %get-tuple-element.17), channel_id=1, source_target_pairs={{2,4},{4,2},{3,5},{5,3},{6,8},{8,6},{7,9},{9,7},{10,12},{12,10},{1... | collective-permute-start | bytes 1572872 | tf_op jit(solution)/shard_map/ppermute | solution.py:548
  8.1 36.4 %collective-permute-start.3 = (bf16[2,128,1024]{2,1,0:T(8,128)(2,1)S(1)}, bf16[2,128,1024]{2,1,0:T(8,128)(2,1)S(1)}, u32[]{:S(2)}, u32[]{:S(2)}) collective-permute-start(bf16[2,128,1024]{2,1,0:T(8,128)(2,1)S(1)} %get-tuple-element.18), channel_id=1, source_target_pairs={{0,2},{2,0},{1,3},{3,1},{4,6},{6,4},{5,7},{7,5},{8,10},{10,8},{9,1... | collective-permute-start | bytes 1572872 | tf_op jit(solution)/shard_map/ppermute | solution.py:548
  14.9 29.6 %copy-start.3 = (s32[64]{0:T(128)S(1)}, s32[64]{0:T(128)}, u32[]{:S(2)}) copy-start(s32[64]{0:T(128)} %get-tuple-element.14.table_hbm.table_ref) | copy-start | bytes 772

commit v12 on v11

--- a/solution.py
+++ b/solution.py
@@ -20,7 +20,7 @@
 ROW_TILE = 16
 WINDOW = 2 * ROW_TILE
 
-ROUNDS = ((2, 0), (2, 2), (1, 1), (1, 0))
+ROUNDS = ((2, 0), (1, 0), (2, 2), (1, 1))
 
 
 def is_first(device, distance, offset):

time: 46.8 us -> 43 us (0.919)
  starting transfers between devices: 11.4 us -> 6.32 us
  blocking collectives: 15.7 us -> 16.9 us
    ppermute x4, starting transfers between devices: 11.4 us -> 6.32 us  [local(): lax.ppermute(send, everyone, swaps(doms, tps, *pairing))]
    all_to_all x1, blocking collectives: 15.7 us -> 16.9 us  [local(): shares = lax.all_to_all(shares, everyone, 0, 0, tiled=True)]
  transfers between devices with their start and end apart: 4 -> 4, of which waited for: 0 -> 0; matrix products, arithmetic and copies ran while one was open for 0% -> 0% of each run, Pallas kernels for 30% -> 33%
where the time goes in v12:
time: 43 us; the launch traced here: 42.4 us
  Pallas kernels  18.4 us (43%)
  blocking collectives  16.9 us (39%)
  starting transfers between devices  6.32 us (15%)
  between operations  0.76 us (2%)
    all_to_all x1, blocking collectives, local(): shares = lax.all_to_all(shares, everyone, 0, 0, tiled=True)  16.9 us
    pallas_call x1, Pallas kernels, attend(): pl.pallas_call(functools.partial(attend_kernel, per_dev, group, kv_local,...  13.8 us
    ppermute x4, starting transfers between devices, local(): lax.ppermute(send, everyone, swaps(doms, tps, *pairing))  6.32 us
    pallas_call x1, Pallas kernels, pack(): pl.pallas_call(functools.partial(pack_kernel, per_dev, doms), out_shape=[...  2.62 us
    pallas_call x1, Pallas kernels, finish(): pl.pallas_call(functools.partial(finish_kernel, doms, tps), out_shape=[ja...  1.99 us
  transfers between devices with their start and end apart: 4, of which 0 were waited for; matrix products, arithmetic and copies ran while one was open for 0% of the time, Pallas kernels for 33%

profile of v12, /device:TPU:0, one launch (start us, length us, event | category | flops | bytes accessed | tf_op | source)
XLA Modules:
  0.0 42.4 jit_solution(13716025819250052686)
XLA Ops:
  0.6 0.0 copy-start
  0.6 0.0 copy-start.4
  0.7 0.0 copy-start.2
  0.7 0.0 copy-start.1
  0.7 2.6 %pack_sends.1 = (bf16[2,128,1024]{2,1,0:T(8,128)(2,1)S(1)}, bf16[2,128,1024]{2,1,0:T(8,128)(2,1)S(1)}, bf16[2,128,1024]{2,1,0:T(8,128)(2,1)S(1)}, bf16[2,128,1024]{2,1,0:T(8,128)(2,1)S(1)}, s32[64]{0:T(128)}) custom-call(s32[256]{0:T(256)} %len_hbm.1, s32[256]{0:T(256)} %anc_hbm.1, bf16[2,16,1024]{2,1,0:T(8,128)(2,1)} %new_ref.1, bf16[16,128,1024]{2,1,0:T(8,128)(2,1)} %gen_hbm.3), custom_call_target="tpu_custom_call" | custom-call | bytes 4194304 | tf_op jit(solution)/shard_map/pack_sends/pallas_call | solution.py:142
  3.3 3.3 %collective-permute-start = (bf16[2,128,1024]{2,1,0:T(8,128)(2,1)S(1)}, bf16[2,128,1024]{2,1,0:T(8,128)(2,1)S(1)}, u32[]{:S(2)}, u32[]{:S(2)}) collective-permute-start(bf16[2,128,1024]{2,1,0:T(8,128)(2,1)S(1)} %get-tuple-element.15), channel_id=1, source_target_pairs={{0,4},{4,0},{1,5},{5,1},{2,6},{6,2},{3,7},{7,3},{8,12},{12,8},{9,1... | collective-permute-start | bytes 1572872 | tf_op jit(solution)/shard_map/ppermute | solution.py:548
  6.6 1.7 %collective-permute-start.1 = (bf16[2,128,1024]{2,1,0:T(8,128)(2,1)S(1)}, bf16[2,128,1024]{2,1,0:T(8,128)(2,1)S(1)}, u32[]{:S(2)}, u32[]{:S(2)}) collective-permute-start(bf16[2,128,1024]{2,1,0:T(8,128)(2,1)S(1)} %get-tuple-element.16), channel_id=1, source_target_pairs={{0,2},{2,0},{1,3},{3,1},{4,6},{6,4},{5,7},{7,5},{8,10},{10,8},{9,1... | collective-permute-start | bytes 1572872 | tf_op jit(solution)/shard_map/ppermute | solution.py:548
  8.2 0.7 %collective-permute-start.2 = (bf16[2,128,1024]{2,1,0:T(8,128)(2,1)S(1)}, bf16[2,128,1024]{2,1,0:T(8,128)(2,1)S(1)}, u32[]{:S(2)}, u32[]{:S(2)}) collective-permute-start(bf16[2,128,1024]{2,1,0:T(8,128)(2,1)S(1)} %get-tuple-element.17), channel_id=1, source_target_pairs={{4,8},{8,4},{5,9},{9,5},{6,10},{10,6},{7,11},{11,7},{12,16},{16,12... | collective-permute-start | bytes 1572872 | tf_op jit(solution)/shard_map/ppermute | solution.py:548
  8.9 0.7 %collective-permute-start.3 = (bf16[2,128,1024]{2,1,0:T(8,128)(2,1)S(1)}, bf16[2,128,1024]{2,1,0:T(8,128)(2,1)S(1)}, u32[]{:S(2)}, u32[]{:S(2)}) collective-permute-start(bf16[2,128,1024]{2,1,0:T(8,128)(2,1)S(1)} %get-tuple-element.18), channel_id=1, source_target_pairs={{2,4},{4,2},{3,5},{5,3},{6,8},{8,6},{7,9},{9,7},{10,12},{12,10},{1... | collective-permute-start | bytes 1572872 | tf_op jit(solution)/shard_map/ppermute | solution.py:548
  9.6 0.0 copy-done
  9.6 0.0 copy-done.4
  9.7 0.0 copy-done.2
  9.7 0.0 copy-done.1
  9.7 0.0 copy-start.3
  9.7 13.8 %attend.1 = (f32[32,1,128]{2,1,0:T(1,128)S(1)}, bf16[16,128,1024]{2,1,0:T(8,128)(2,1)}) custom-call(s32[64]{0:T(128)} %get-tuple-element.14.table_hbm.table_ref, bf16[2,16,4096]{2,1,0:T(8,128)(2,1)S(1)} %copy-done.1, bf16[4096,1024]{1,0:T(8,128)(2,1)} %prompt_hbm.1, bf16[16,128,1024]{2,1,0:T(8,128)(2,1)} %gen_hbm.3, s32[2,16]{1,0:T(2,128)} %token_hbm.1, ...), custom_call_target="tpu_custom_call" | custom-call | flops 2214592512 | bytes 16777216 | tf_op jit(solution)/shard_map/attend/pallas_call | solution.py:411
  23.5 16.9 %all_to_all.5.refs_5_ = f32[32,1,128]{2,1,0:T(1,128)S(1)} all-to-all(f32[32,1,128]{2,1,0:T(1,128)S(1)} %get-tuple-element.20), channel_id=1, replica_groups=mesh['dom'=16,'tp'=2] {'dom','tp'}, dimensions={0} | all-to-all | bytes 32768 | tf_op jit(solution)/shard_map/all_to_all | solution.py:564
  40.4 0.0 collective-permute-done.refs_0_
  40.4 0.0 collective-permute-done.1.refs_1_
  40.4 0.0 collective-permute-done.2.refs_2_
  40.4 0.0 collective-permute-done.3.refs_3_
  40.4 0.0 copy-done.3
  40.4 2.0 %finish.1 = (bf16[16,128,1024]{2,1,0:T(8,128)(2,1)}, f32[2,16]{1,0:T(2,128)}, f32[1,16]{1,0:T(1,128)}) custom-call(s32[64]{0:T(128)S(1)} %copy-done.3, bf16[2,128,1024]{2,1,0:T(8,128)(2,1)S(1)} %collective-permute-done.refs_0_, bf16[2,128,1024]{2,1,0:T(8,128)(2,1)S(1)} %collective-permute-done.1.refs_1_, ...), custom_call_target="tpu_custom_call", output_to_operand_aliasing={{0}: (5, {})} | custom-call | bytes 2097152 | tf_op jit(solution)/shard_map/finish/pallas_call | solution.py:504
Async XLA Ops:
  0.6 9.0 %copy-start = (bf16[2,16,1024]{2,1,0:T(8,128)(2,1)S(1)}, bf16[2,16,1024]{2,1,0:T(8,128)(2,1)}, u32[]{:S(2)}) copy-start(bf16[2,16,1024]{2,1,0:T(8,128)(2,1)} %new_ref.1) | copy-start | bytes 196612
  0.6 9.0 %copy-start.4 = (f32[16]{0:T(128)S(1)}, f32[16]{0:T(128)}, u32[]{:S(2)}) copy-start(f32[16]{0:T(128)} %param.19) | copy-start | bytes 196
  0.7 9.0 %copy-start.2 = (f32[4096]{0:T(1024)S(1)}, f32[4096]{0:T(1024)}, u32[]{:S(2)}) copy-start(f32[4096]{0:T(1024)} %param.17) | copy-start | bytes 49156
  0.7 9.0 %copy-start.1 = (bf16[2,16,4096]{2,1,0:T(8,128)(2,1)S(1)}, bf16[2,16,4096]{2,1,0:T(8,128)(2,1)}, u32[]{:S(2)}) copy-start(bf16[2,16,4096]{2,1,0:T(8,128)(2,1)} %q_ref.1) | copy-start | bytes 786436
  3.3 37.1 %collective-permute-start = (bf16[2,128,1024]{2,1,0:T(8,128)(2,1)S(1)}, bf16[2,128,1024]{2,1,0:T(8,128)(2,1)S(1)}, u32[]{:S(2)}, u32[]{:S(2)}) collective-permute-start(bf16[2,128,1024]{2,1,0:T(8,128)(2,1)S(1)} %get-tuple-element.15), channel_id=1, source_target_pairs={{0,4},{4,0},{1,5},{5,1},{2,6},{6,2},{3,7},{7,3},{8,12},{12,8},{9,1... | collective-permute-start | bytes 1572872 | tf_op jit(solution)/shard_map/ppermute | solution.py:548
  6.6 33.9 %collective-permute-start.1 = (bf16[2,128,1024]{2,1,0:T(8,128)(2,1)S(1)}, bf16[2,128,1024]{2,1,0:T(8,128)(2,1)S(1)}, u32[]{:S(2)}, u32[]{:S(2)}) collective-permute-start(bf16[2,128,1024]{2,1,0:T(8,128)(2,1)S(1)} %get-tuple-element.16), channel_id=1, source_target_pairs={{0,2},{2,0},{1,3},{3,1},{4,6},{6,4},{5,7},{7,5},{8,10},{10,8},{9,1... | collective-permute-start | bytes 1572872 | tf_op jit(solution)/shard_map/ppermute | solution.py:548
  8.2 32.2 %collective-permute-start.2 = (bf16[2,128,1024]{2,1,0:T(8,128)(2,1)S(1)}, bf16[2,128,1024]{2,1,0:T(8,128)(2,1)S(1)}, u32[]{:S(2)}, u32[]{:S(2)}) collective-permute-start(bf16[2,128,1024]{2,1,0:T(8,128)(2,1)S(1)} %get-tuple-element.17), channel_id=1, source_target_pairs={{4,8},{8,4},{5,9},{9,5},{6,10},{10,6},{7,11},{11,7},{12,16},{16,12... | collective-permute-start | bytes 1572872 | tf_op jit(solution)/shard_map/ppermute | solution.py:548
  8.9 31.5 %collective-permute-start.3 = (bf16[2,128,1024]{2,1,0:T(8,128)(2,1)S(1)}, bf16[2,128,1024]{2,1,0:T(8,128)(2,1)S(1)}, u32[]{:S(2)}, u32[]{:S(2)}) collective-permute-start(bf16[2,128,1024]{2,1,0:T(8,128)(2,1)S(1)} %get-tuple-element.18), channel_id=1, source_target_pairs={{2,4},{4,2},{3,5},{5,3},{6,8},{8,6},{7,9},{9,7},{10,12},{12,10},{1... | collective-permute-start | bytes 1572872 | tf_op jit(solution)/shard_map/ppermute | solution.py:548
  9.7 30.8 %copy-start.3 = (s32[64]{0:T(128)S(1)}, s32[64]{0:T(128)}, u32[]{:S(2)}) copy-start(s32[64]{0:T(128)} %get-tuple-element.14.table_hbm.table_ref) | copy-start | bytes 772
